TPU v7x, 32 devices: a whole 2x2x4 slice. The times are simulated.
32 devices in a mesh: shot: 8 (over y, x, core), freq: 4 (over z).
Axes of the slice: x: 2, y: 2, z: 4, core: 2. Of those that a mesh axis runs over, the one named last changes fastest.
Arguments:
- traces: float32 [32, 2048, 1024], P('shot', 'freq'), may hold values from -6 to 6
- interp_weights: float32 [32, 16, 128, 128], P('shot'), may hold values from -0.09375 to 0.09375
- tile_ids: int32 [32, 16], P('shot'), may hold values from 0 to 15, as said below
Outputs:
- binned: float32 [16, 2, 384, 128], P('shot', None, 'freq')
Inputs may be any that keep to these rules, and one draw needn't show every extreme that they name: `tile_ids`: tile g is owned by index g // 2 of shot. Among the receiver blocks of the shots of one index of shot, at most 10 land on tiles of one owner, and in every draw each index of shot sends exactly 10 to one owner.
All inputs are finite; a program needn't handle non-finite values.
Results may differ from a plain program's by a relative error of at most 0.0003.
Values sent between devices are 32-bit elements; how exact they have to be, the bound alone decides.
No kernel may reach another device: no remote copies, remote signals or barrier semaphores. Data moves between devices by JAX's collectives and lax.ppermute only.
A program may use at most 128 MiB of HBM per device.

v0:
```python
import math

import jax
import jax.numpy as jnp
from jax import lax
from jax.sharding import PartitionSpec as P

NF = 384
TILES_DEV = 2


def shards(traces, interp_weights, tile_ids):
    highest = lax.Precision.HIGHEST
    shot_count = lax.axis_size("shot")
    freq_count = lax.axis_size("freq")
    shots_here = traces.shape[0]
    time_len = traces.shape[2]
    block_count = interp_weights.shape[1]
    block_len = interp_weights.shape[2]
    tile_len = interp_weights.shape[3]
    freq_here = NF // freq_count
    freq_index = jnp.arange(NF, dtype=jnp.int32)
    time_index = jnp.arange(time_len, dtype=jnp.int32)
    phase = freq_index[:, None] * time_index[None, :] % time_len
    angle = phase.astype(jnp.float32) * (2.0 * math.pi / time_len)
    tables = jnp.stack([jnp.cos(angle), -jnp.sin(angle)]) * (1.0 / math.sqrt(time_len))
    spectrum = jnp.einsum("cft,srt->scfr", tables, traces, precision=highest)
    gathered = lax.all_to_all(spectrum, "freq", split_axis=2, concat_axis=3, tiled=True)
    blocks = gathered.reshape(shots_here, 2 * freq_here, block_count, block_len)
    partial_value = jnp.einsum("scbr,sbrt->sbct", blocks, interp_weights, precision=highest)
    row_count = shots_here * block_count
    width = 2 * freq_here * tile_len
    partial_value = partial_value.reshape(row_count, width)
    tile_rows = tile_ids.reshape(row_count)
    cap_slots = (row_count + shot_count - 1) // shot_count + 2
    owner_of = tile_rows // TILES_DEV
    local_tile = tile_rows % TILES_DEV
    owner_hits = (owner_of[:, None] == jnp.arange(shot_count, dtype=jnp.int32)[None, :]).astype(
        jnp.int32
    )
    running = jnp.cumsum(owner_hits, axis=0)
    position = jnp.sum(running * owner_hits, axis=1) - 1
    slot_index = owner_of * cap_slots + position
    slot_range = jnp.arange(shot_count * cap_slots, dtype=jnp.int32)
    placing = slot_index[None, :] == slot_range[:, None]
    send_rows = jnp.dot(placing.astype(jnp.float32), partial_value, precision=highest)
    send_tiles = jnp.sum(jnp.where(placing, local_tile[None, :] + 1, 0), axis=1) - 1
    received, got_tiles = (
        lax.all_to_all(
            send_rows.reshape(shot_count, cap_slots, width),
            "shot",
            split_axis=0,
            concat_axis=0,
            tiled=True,
        ),
        lax.all_to_all(
            send_tiles.reshape(shot_count, cap_slots),
            "shot",
            split_axis=0,
            concat_axis=0,
            tiled=True,
        ),
    )
    landing = (
        got_tiles.reshape(shot_count * cap_slots)[None, :]
        == jnp.arange(TILES_DEV, dtype=jnp.int32)[:, None]
    ).astype(jnp.float32)
    binned = jnp.dot(landing, received.reshape(shot_count * cap_slots, width), precision=highest)
    return binned.reshape(TILES_DEV, 2, freq_here, tile_len)


def solution(mesh):
    in_specs = (P("shot", "freq", None), P("shot", None, None, None), P("shot", None))
    out_specs = P("shot", None, "freq", None)
    return jax.shard_map(shards, mesh=mesh, in_specs=in_specs, out_specs=out_specs, check_vma=False)
```

profile of v0, /device:TPU:0, one launch (start us, length us, event | category | flops | bytes accessed | tf_op | source)
XLA Modules:
  0.0 401.9 jit_solution(16220811649558486330)
XLA Ops:
  0.0 6.2 %sine_negate_fusion = (f32[1,384,1024]{2,1,0:T(8,128)S(1)}, f32[1,384,1024]{2,1,0:T(8,128)S(1)}) fusion(), kind=kLoop, calls=%fused_computation.19 | loop fusion | flops 5898240 | bytes 3145728 | tf_op jit(solution)/shard_map/neg | solution.py:26
  6.2 24.5 %fusion.10 = f32[4,2,384,512]{3,2,0,1:T(8,128)S(1)} fusion(f32[4,512,1024]{2,1,0:T(8,128)} %param.3, f32[1,384,1024]{2,1,0:T(8,128)S(1)} %get-tuple-element.7, f32[1,384,1024]{2,1,0:T(8,128)S(1)} %get-tuple-element.8), kind=kOutput, calls=%fused_computation.11 | convolution fusion | flops 19328925696 | bytes 17825792 | tf_op jit(solution)/shard_map/cft,srt->scfr/dot_general | solution.py:27
  30.7 6.7 %copy.16 = f32[4,2,384,512]{3,0,1,2:T(4,128)} copy(f32[4,2,384,512]{3,2,0,1:T(8,128)S(1)} %fusion.10) | data formatting | bytes 12582912 | tf_op jit(solution)/shard_map/cft,srt->scfr/transpose | solution.py:27
  37.4 0.0 copy-start
  37.4 6.5 %all-to-all-start.1 = ((f32[4,2,384,512]{3,0,1,2:T(4,128)}), f32[4,2,384,512]{3,0,1,2:T(4,128)}, u32[]{:S(2)}, u32[]{:S(2)}) async-start(f32[4,2,384,512]{3,0,1,2:T(4,128)} %copy.16), calls=%async_computation.1 | async-start | bytes 12582912 | tf_op jit(solution)/shard_map/all_to_all | solution.py:28
  43.9 0.0 copy-done
  43.9 0.1 reshape.207
  44.0 0.1 fusion.27
  44.1 0.1 reduce_window_sum.11
  44.1 0.2 select_reduce_fusion.1
  44.3 0.1 select_reduce_fusion
  44.5 0.7 sub.19
  45.1 137.5 %all-to-all-done.1 = f32[4,2,384,512]{3,0,1,2:T(4,128)} async-done(((f32[4,2,384,512]{3,0,1,2:T(4,128)}), f32[4,2,384,512]{3,0,1,2:T(4,128)}, u32[]{:S(2)}, u32[]{:S(2)}) %all-to-all-start.1) | async-done | bytes 6291488 | tf_op jit(solution)/shard_map/all_to_all | solution.py:28
  182.6 3.8 all-to-all-start
  186.4 9.5 %copy.29 = f32[4,2,4,96,512]{4,2,3,1,0:T(4,128)} copy(f32[4,2,4,96,512]{4,0,1,3,2:T(4,128)} %bitcast.7) | data formatting | bytes 12582912 | tf_op jit(solution)/shard_map/all_to_all | solution.py:28
  195.9 7.9 %reshape.208 = f32[4,192,16,128]{3,2,1,0:T(8,128)} reshape(f32[4,2,96,4,512]{4,3,2,1,0:T(4,128)} %bitcast.36) | data formatting | bytes 12582912 | tf_op jit(solution)/shard_map/reshape | solution.py:29
  203.8 12.4 %fusion.4 = f32[4,16,192,128]{3,2,1,0:T(8,128)} fusion(f32[4,16,128,128]{3,2,1,0:T(8,128)} %param.4, f32[4,192,16,128]{3,2,1,0:T(8,128)} %reshape.208), kind=kOutput, calls=%fused_computation.4 | convolution fusion | flops 2415919104 | bytes 16777216 | tf_op jit(solution)/shard_map/scbr,sbrt->sbct/dot_general | solution.py:30
  216.2 6.3 %reshape.213 = f32[64,24576,1]{1,0,2:T(8,128)} reshape(f32[4,16,192,128]{3,2,1,0:T(8,128)} %fusion.4) | data formatting | bytes 12582912 | tf_op jit(solution)/shard_map/reshape | solution.py:33
  222.4 12.1 %fusion.23 = f32[8,10,24576]{2,1,0:T(8,128)} fusion(f32[64,24576,1]{1,0,2:T(8,128)} %reshape.213, s32[8,10]{1,0:T(8,128)S(1)} %multiply_add_fusion, s32[64]{0:T(128)S(1)} %add_add_fusion), kind=kOutput, calls=%fused_computation.24 | convolution fusion | flops 1509954560 | bytes 14156352 | tf_op jit(solution)/shard_map/dot_general | solution.py:46
  234.6 0.0 all-to-all-done
  234.6 5.3 %all-to-all-start.2 = ((f32[8,10,24576]{2,1,0:T(8,128)}), f32[8,10,24576]{2,1,0:T(8,128)}, u32[]{:S(2)}, u32[]{:S(2)}) async-start(f32[8,10,24576]{2,1,0:T(8,128)} %fusion.23), calls=%async_computation.2 | async-start | bytes 25165824 | tf_op jit(solution)/shard_map/all_to_all | solution.py:49
  239.9 0.5 broadcast.239
  240.4 0.7 reduce.3
  241.1 0.1 eq.68
  241.2 137.7 %all-to-all-done.2 = f32[8,10,24576]{2,1,0:T(8,128)} async-done(((f32[8,10,24576]{2,1,0:T(8,128)}), f32[8,10,24576]{2,1,0:T(8,128)}, u32[]{:S(2)}, u32[]{:S(2)}) %all-to-all-start.2) | async-done | bytes 7864352 | tf_op jit(solution)/shard_map/all_to_all | solution.py:49
  378.9 10.5 %reshape.210 = f32[80,24576]{1,0:T(8,128)} reshape(f32[8,10,24576]{2,1,0:T(8,128)} %all-to-all-done.2) | data formatting | bytes 15728640 | tf_op jit(solution)/shard_map/reshape | solution.py:68
  389.4 4.6 %copy.23 = f32[10,8,192,128]{3,2,1,0:T(8,128)S(1)} copy(f32[10,8,192,128]{3,1,2,0:T(8,128)} %bitcast.35) | data formatting | bytes 15728640
  394.0 7.0 %fusion.2 = f32[2,2,96,128]{3,0,2,1:T(2,128)S(1)} fusion(f32[2,96,128,80]{2,1,0,3:T(8,128)S(1)} %bitcast.34, s32[80]{0:T(128)S(1)} %eq.68), kind=kOutput, calls=%fused_computation.2 | convolution fusion | flops 47186080 | bytes 8061248 | tf_op jit(solution)/shard_map/dot_general | solution.py:68
  401.0 0.7 copy.20
  (4 shorter events, 0.0 us)
Async XLA Ops:
  37.4 6.5 %copy-start = (s32[4,16]{1,0:T(4,128)S(1)}, s32[4,16]{1,0:T(4,128)}, u32[]{:S(2)}) copy-start(s32[4,16]{1,0:T(4,128)} %param.5) | copy-start | bytes 772
  37.4 145.2 %all-to-all-start.1 = ((f32[4,2,384,512]{3,0,1,2:T(4,128)}), f32[4,2,384,512]{3,0,1,2:T(4,128)}, u32[]{:S(2)}, u32[]{:S(2)}) async-start(f32[4,2,384,512]{3,0,1,2:T(4,128)} %copy.16), calls=%async_computation.1 | async-start | bytes 12582912 | tf_op jit(solution)/shard_map/all_to_all | solution.py:28
  182.6 52.0 %all-to-all-start = ((s32[8,1,10]{2,1,0:T(1,128)}), s32[8,1,10]{2,1,0:T(1,128)S(1)}, u32[]{:S(2)}, u32[]{:S(2)}) async-start(s32[8,1,10]{2,1,0:T(1,128)} %bitcast), calls=%async_computation | async-start | bytes 8192 | tf_op jit(solution)/shard_map/all_to_all | solution.py:56
  234.6 144.4 %all-to-all-start.2 = ((f32[8,10,24576]{2,1,0:T(8,128)}), f32[8,10,24576]{2,1,0:T(8,128)}, u32[]{:S(2)}, u32[]{:S(2)}) async-start(f32[8,10,24576]{2,1,0:T(8,128)} %fusion.23), calls=%async_computation.2 | async-start | bytes 25165824 | tf_op jit(solution)/shard_map/all_to_all | solution.py:49
where the time goes:
time: 408 us; the launch traced here: 402 us
  waiting for transfers between devices  275 us (67%)
  matrix products  56.1 us (14%)
  local copies, waits for them, and re-layouts  47.5 us (12%)
  starting transfers between devices  15.6 us (4%)
  other arithmetic  7.32 us (2%)
    all_to_all x1, waiting for transfers between devices, shards(): lax.all_to_all(send_rows.reshape(shot_count, cap_slots, width), 'shot', s...  138 us
    all_to_all x1, waiting for transfers between devices, shards(): lax.all_to_all(spectrum, 'freq', split_axis=2, concat_axis=3, tiled=True)  137 us
    dot_general x1, matrix products, shards(): spectrum = jnp.einsum('cft,srt->scfr', tables, traces, precision=highest)  24.5 us
    dot_general x1, matrix products, shards(): jnp.einsum('scbr,sbrt->sbct', blocks, interp_weights, precision=highest)  12.4 us
    dot_general x1, matrix products, shards(): jnp.dot(placing.astype(jnp.float32), partial_value, precision=highest)  12.1 us
    reshape x1, local copies, waits for them, and re-layouts, shards(): received.reshape(shot_count * cap_slots, width)  10.5 us
    all_to_all x1, local copies, waits for them, and re-layouts, shards(): lax.all_to_all(spectrum, 'freq', split_axis=2, concat_axis=3, tiled=True)  9.48 us
  transfers between devices with their start and end apart: 3, of which 2 were waited for; matrix products, arithmetic and copies ran while one was open for 13% of the time, Pallas kernels for 0%

commit v1 on v0

v1 whole, which is shorter than its diff:
```python
import math

import jax
import jax.numpy as jnp
import numpy as np
from jax import lax
from jax.experimental import pallas as pl
from jax.experimental.pallas import tpu as pltpu
from jax.sharding import PartitionSpec as P

NF = 384
TILES_DEV = 2
RADIX = 4
GROUPS = ((0, 2), (1, 3))
PAIR = 2


def bit_orders(shot_count):
    bits = list(range(1, shot_count.bit_length() - 1))
    turn = len(bits) // 2
    return bits, bits[turn:] + bits[:turn]


def dft_table(residues, freq_count, time_len):
    fold = time_len // RADIX
    freq_here = NF // freq_count
    rows = []
    for owner in range(freq_count):
        for residue in residues:
            freqs = owner * freq_here + np.arange(residue, freq_here, RADIX)
            angle = 2.0 * math.pi / time_len * (freqs[:, None] * np.arange(fold)[None, :] % time_len)
            cos, sin = np.cos(angle), np.sin(angle)
            if residue % 2 == 0:
                rows += [cos, -sin]
            else:
                sign = 1.0 if residue == 1 else -1.0
                rows += [np.hstack([cos, -sign * sin]), np.hstack([-sin, -sign * cos])]
    table = np.concatenate(rows) / math.sqrt(time_len)
    return table.reshape(freq_count, -1, table.shape[-1]).astype(np.float32)


def split(value):
    high = value.astype(jnp.bfloat16)
    return high, (value - high.astype(jnp.float32)).astype(jnp.bfloat16)


def dot_nt(a, b):
    return lax.dot_general(a, b, (((1,), (1,)), ((), ())), preferred_element_type=jnp.float32)


def bin_kernel(residues, freq_count, half, meta, x_ref, w_ref, t_ref, far_ref, own_ref, table):
    step = pl.program_id(0)
    slot_count = pl.num_programs(0) * PAIR
    fold = x_ref.shape[-1] // RADIX
    even = residues[0] % 2 == 0
    per_owner = t_ref.shape[1]

    @pl.when(step == 0)
    def _():
        far_ref[...] = jnp.zeros_like(far_ref)
        own_ref[...] = jnp.zeros_like(own_ref)
        me = meta[slot_count]
        parts = [t_ref[jnp.bitwise_xor(me, i)] for i in range(freq_count)]
        if even:
            sub = per_owner // len(residues)
            parts = [part[r * sub : (r + 1) * sub] for r in range(len(residues)) for part in parts]
        high, low = split(jnp.concatenate(parts, axis=0))
        table[...] = jnp.concatenate([high, low, high], axis=1)

    x = x_ref[0]
    x0, x1, x2, x3 = (x[:, i * fold : (i + 1) * fold] for i in range(RADIX))
    if even:
        plus, cross = x0 + x2, x1 + x3
        rows = freq_count * per_owner // len(residues)
        sub = per_owner // len(residues)
        spectra = []
        for r, folded in enumerate((plus + cross, plus - cross)):
            high, low = split(folded)
            spectra.append(dot_nt(table[r * rows : (r + 1) * rows, :], jnp.concatenate([high, high, low], axis=1)))
        spectrum = jnp.concatenate(
            [s[i * sub : (i + 1) * sub] for i in range(freq_count) for s in spectra], axis=0
        )
    else:
        high, low = split(jnp.concatenate([x0 - x2, x1 - x3], axis=1))
        spectrum = dot_nt(table[...], jnp.concatenate([high, high, low], axis=1))
    block = w_ref.shape[2]
    for h in range(PAIR):
        s_high, s_low = split(spectrum[:, h * block : (h + 1) * block])
        w_high, w_low = split(w_ref[0, h])
        weights = jnp.concatenate(
            [
                jnp.concatenate([w_high, w_low], axis=1),
                jnp.concatenate([w_high, jnp.zeros_like(w_low)], axis=1),
            ],
            axis=0,
        )
        both = jnp.dot(
            jnp.concatenate([s_high, s_low], axis=1), weights, preferred_element_type=jnp.float32
        )
        tile_len = both.shape[1] // 2
        value = both[:, :tile_len] + both[:, tile_len:]
        slot = meta[step * PAIR + h]

        @pl.when(slot >= half)
        def _():
            far_ref[slot - half] += value

        @pl.when(slot < half)
        def _():
            own_ref[slot] += value


def bin_group(meta, traces, interp_weights, residues, freq_count, half):
    shots_here, recs_here, time_len = traces.shape
    block_len, tile_len = interp_weights.shape[2:]
    blocks_here = recs_here // block_len
    pairs = blocks_here // PAIR
    table = dft_table(residues, freq_count, time_len)
    rows = table.shape[0] * table.shape[1]
    slot_count = shots_here * blocks_here
    out = jax.ShapeDtypeStruct((half, rows, tile_len), jnp.float32)
    out_spec = pl.BlockSpec((half, rows, tile_len), lambda i, m: (0, 0, 0))

    def body(meta, *refs):
        bin_kernel(residues, freq_count, half, meta, *refs)

    return pl.pallas_call(
        body,
        grid_spec=pltpu.PrefetchScalarGridSpec(
            num_scalar_prefetch=1,
            grid=(shots_here * pairs,),
            in_specs=[
                pl.BlockSpec((1, PAIR * block_len, time_len), lambda i, m: (i // pairs, i % pairs, 0)),
                pl.BlockSpec(
                    (1, PAIR, block_len, tile_len),
                    lambda i, m: (i // pairs, m[slot_count] * pairs + i % pairs, 0, 0),
                ),
                pl.BlockSpec(table.shape, lambda i, m: (0, 0, 0)),
            ],
            out_specs=[out_spec, out_spec],
            scratch_shapes=[pltpu.VMEM((rows, 3 * table.shape[-1]) if residues[0] % 2 else (rows, 3 * table.shape[-1]), jnp.bfloat16)],
        ),
        out_shape=[out, out],
        compiler_params=pltpu.CompilerParams(vmem_limit_bytes=56 << 20),
        cost_estimate=pl.CostEstimate(
            flops=2 * 3 * rows * table.shape[-1] * block_len * slot_count,
            bytes_accessed=traces.size * 4 + 2 * half * rows * tile_len * 4,
            transcendentals=0,
        ),
        name="bin_group",
    )(meta, traces, interp_weights, table)


def shards(traces, interp_weights, tile_ids):
    shot_count = lax.axis_size("shot")
    freq_count = lax.axis_size("freq")
    shots_here, recs_here, time_len = traces.shape
    block_len, tile_len = interp_weights.shape[2:]
    blocks_here = recs_here // block_len
    half = shot_count // 2 * TILES_DEV
    me_shot = lax.axis_index("shot")
    me_freq = lax.axis_index("freq")
    orders = bit_orders(shot_count)

    tiles = lax.dynamic_slice_in_dim(tile_ids, me_freq * blocks_here, blocks_here, axis=1).reshape(-1)
    owner = tiles // TILES_DEV
    apart = owner ^ me_shot

    def place(order):
        index = jnp.zeros_like(apart)
        for bit in order:
            index = index * 2 + ((apart >> bit) & 1)
        return index

    index = jnp.where(owner & 1 == 0, place(orders[0]), place(orders[1]))
    slots = (apart & 1) * half + index * TILES_DEV + tiles % TILES_DEV
    meta = jnp.concatenate([slots, me_freq[None]]).astype(jnp.int32)

    def shot_pairs(flip):
        return [(i, i ^ flip(i & 1)) for i in range(shot_count)]

    def freq_pairs(flip):
        return [(i, i ^ flip) for i in range(freq_count)]

    groups = []
    for residues in GROUPS:
        far, own = bin_group(meta, traces, interp_weights, residues, freq_count, half)
        groups.append((far, own))
    results = []
    for residues, (far, own) in zip(GROUPS, groups):
        value = own + lax.ppermute(far, "shot", shot_pairs(lambda core: 1))
        for level in range(len(orders[0])):
            keep = value.shape[0] // 2
            got = lax.ppermute(value[keep:], "shot", shot_pairs(lambda core: 1 << orders[core][level]))
            value = value[:keep] + got
        value = value.reshape(TILES_DEV, freq_count, -1, tile_len)
        flip = 1
        while flip < freq_count:
            value = value.reshape(TILES_DEV, -1, 2, value.shape[-2], tile_len)
            got = lax.ppermute(value[:, :, 1], "freq", freq_pairs(flip))
            value = value[:, :, 0] + got
            flip *= 2
        results.append(value.reshape(TILES_DEV, len(residues), 2, -1, tile_len))
    both = jnp.stack(results, axis=2)
    both = both.reshape(TILES_DEV, RADIX, 2, -1, tile_len)
    return both.transpose(0, 2, 3, 1, 4).reshape(TILES_DEV, 2, NF // freq_count, tile_len)


def solution(mesh):
    in_specs = (P("shot", "freq", None), P("shot", None, None, None), P("shot", None))
    out_specs = P("shot", None, "freq", None)
    return jax.shard_map(shards, mesh=mesh, in_specs=in_specs, out_specs=out_specs, check_vma=False)
```

time: 408 us -> 74.9 us (0.18); the launches traced: 402 us -> 74.5 us
  waiting for transfers between devices: 275 us -> 26.3 us
  matrix products: 56.1 us -> 0 us
  local copies, waits for them, and re-layouts: 47.5 us -> 1.88 us
  Pallas kernels: 0 us -> 25.6 us
  other arithmetic: 7.32 us -> 1.35 us
    all_to_all x3 -> x0, waiting for transfers between devices: 275 us -> none  [the longest x1 138 us: shards(): lax.all_to_all(send_rows.reshape(shot_count, cap_slots, width), 'shot', s...]
    dot_general x4 -> x0, matrix products: 56.1 us -> none  [the longest x1 24.5 us: shards(): spectrum = jnp.einsum('cft,srt->scfr', tables, traces, precision=highest)]
    ppermute x0 -> x10, waiting for transfers between devices: none -> 26.3 us  [the longest x4 21.1 us: shards(): lax.ppermute(value[keep:], 'shot', shot_pairs(lambda core: 1 << orders[co...]
    pallas_call x0 -> x2, Pallas kernels: none -> 25.6 us  [bin_group(): pl.pallas_call(body, grid_spec=pltpu.PrefetchScalarGridSpec(num_scalar_pr...]
    reshape x4 -> x1, local copies, waits for them, and re-layouts: 24.7 us -> 0.09 us  [shards(): lax.dynamic_slice_in_dim(tile_ids, me_freq * blocks_here, blocks_here, ax...]
    ppermute x0 -> x10, starting transfers between devices: none -> 19.2 us  [the longest x4 9.66 us: shards(): lax.ppermute(value[keep:], 'shot', shot_pairs(lambda core: 1 << orders[co...]
    all_to_all x3 -> x0, starting transfers between devices: 15.6 us -> none  [the longest x1 6.45 us: shards(): lax.all_to_all(spectrum, 'freq', split_axis=2, concat_axis=3, tiled=True)]
    all_to_all x2 -> x0, local copies, waits for them, and re-layouts: 10 us -> none  [the longest x1 9.48 us: shards(): lax.all_to_all(spectrum, 'freq', split_axis=2, concat_axis=3, tiled=True)]
  transfers between devices with their start and end apart: 3 -> 10, of which waited for: 2 -> 6; matrix products, arithmetic and copies ran while one was open for 13% -> 1% of each run, Pallas kernels for 0% -> 17%
where the time goes in v1:
time: 74.9 us; the launch traced here: 74.5 us
  waiting for transfers between devices  26.3 us (35%)
  Pallas kernels  25.6 us (34%)
  starting transfers between devices  19.2 us (26%)
  local copies, waits for them, and re-layouts  1.88 us (3%)
  other arithmetic  1.35 us (2%)
    pallas_call x2, Pallas kernels, bin_group(): pl.pallas_call(body, grid_spec=pltpu.PrefetchScalarGridSpec(num_scalar_pr...  25.6 us
    ppermute x4, waiting for transfers between devices, shards(): lax.ppermute(value[keep:], 'shot', shot_pairs(lambda core: 1 << orders[co...  21.1 us
    ppermute x4, starting transfers between devices, shards(): lax.ppermute(value[keep:], 'shot', shot_pairs(lambda core: 1 << orders[co...  9.66 us
    ppermute x4, starting transfers between devices, shards(): got = lax.ppermute(value[:, :, 1], 'freq', freq_pairs(flip))  9.04 us
    ppermute x4, waiting for transfers between devices, shards(): got = lax.ppermute(value[:, :, 1], 'freq', freq_pairs(flip))  4.75 us
  transfers between devices with their start and end apart: 10, of which 6 were waited for; matrix products, arithmetic and copies ran while one was open for 1% of the time, Pallas kernels for 17%

profile of v1, /device:TPU:0, one launch (start us, length us, event | category | flops | bytes accessed | tf_op | source)
XLA Modules:
  0.0 74.5 jit_solution(16343454282860167912)
XLA Ops:
  0.0 0.0 copy-start
  0.0 0.7 copy-done
  0.7 0.1 constant_dynamic-slice_fusion
  0.8 0.1 reshape.15
  0.9 0.6 pad_add_fusion.meta
  1.4 13.1 %bin_group.3 = (f32[8,384,128]{2,1,0:T(8,128)}, f32[8,384,128]{2,1,0:T(8,128)}) custom-call(s32[17]{0:T(128)} %pad_add_fusion.meta, f32[4,512,1024]{2,1,0:T(8,128)} %refs_0_.3, f32[4,16,128,128]{3,2,1,0:T(8,128)} %refs_1_.3, f32[4,96,512]{2,1,0:T(8,128)} %constant.50.clone.refs_2_), custom_call_target="tpu_custom_call" | custom-call | flops 2415919104 | bytes 11534336 | tf_op jit(solution)/shard_map/bin_group/pallas_call | solution.py:127
  14.5 0.0 copy-start.2
  14.5 0.5 collective-permute-start.5
  15.0 12.5 %bin_group.2 = (f32[8,384,128]{2,1,0:T(8,128)}, f32[8,384,128]{2,1,0:T(8,128)}) custom-call(s32[17]{0:T(128)} %pad_add_fusion.meta, f32[4,512,1024]{2,1,0:T(8,128)} %refs_0_.3, f32[4,16,128,128]{3,2,1,0:T(8,128)} %refs_1_.3, f32[4,96,256]{2,1,0:T(8,128)} %constant.49.clone.refs_2_), custom_call_target="tpu_custom_call" | custom-call | flops 1207959552 | bytes 11534336 | tf_op jit(solution)/shard_map/bin_group/pallas_call | solution.py:127
  27.5 0.1 collective-permute-start
  27.5 0.0 collective-permute-done.5
  27.6 0.0 copy-done.2
  27.6 0.2 add.63
  27.7 0.0 copy-start.1
  27.7 0.1 slice.73
  27.8 2.9 %collective-permute-start.6 = (f32[4,384,128]{2,1,0:T(8,128)S(1)}, f32[4,384,128]{2,1,0:T(8,128)S(1)}, u32[]{:S(2)}, u32[]{:S(2)}) collective-permute-start(f32[4,384,128]{2,1,0:T(8,128)S(1)} %slice.73), channel_id=1, source_target_pairs={{0,8},{4,20},{8,0},{12,28},{16,24},{20,4},{24,16},{28,12},{1,9},{5... | collective-permute-start | bytes 2359304 | tf_op jit(solution)/shard_map/ppermute | solution.py:194
  30.7 0.4 collective-permute-done
  31.1 0.0 copy-done.1
  31.1 0.2 add.58
  31.4 0.1 slice.65
  31.4 2.6 %collective-permute-start.1 = (f32[4,384,128]{2,1,0:T(8,128)S(1)}, f32[4,384,128]{2,1,0:T(8,128)S(1)}, u32[]{:S(2)}, u32[]{:S(2)}) collective-permute-start(f32[4,384,128]{2,1,0:T(8,128)S(1)} %slice.65), channel_id=1, source_target_pairs={{0,8},{4,20},{8,0},{12,28},{16,24},{20,4},{24,16},{28,12},{1,9},{5... | collective-permute-start | bytes 2359304 | tf_op jit(solution)/shard_map/ppermute | solution.py:194
  34.0 6.6 %collective-permute-done.6 = f32[4,384,128]{2,1,0:T(8,128)S(1)} collective-permute-done((f32[4,384,128]{2,1,0:T(8,128)S(1)}, f32[4,384,128]{2,1,0:T(8,128)S(1)}, u32[]{:S(2)}, u32[]{:S(2)}) %collective-permute-start.6) | collective-permute-done | bytes 786464 | tf_op jit(solution)/shard_map/ppermute | solution.py:194
  40.6 0.1 slice_add_fusion
  40.7 2.1 %collective-permute-start.7 = (f32[2,384,128]{2,1,0:T(8,128)S(1)}, f32[2,384,128]{2,1,0:T(8,128)S(1)}, u32[]{:S(2)}, u32[]{:S(2)}) collective-permute-start(f32[2,384,128]{2,1,0:T(8,128)S(1)} %slice.75), channel_id=1, source_target_pairs={{0,16},{4,12},{8,24},{12,4},{16,0},{20,28},{24,8},{28,20},{1,17},{... | collective-permute-start | bytes 1179656 | tf_op jit(solution)/shard_map/ppermute | solution.py:194
  42.9 10.4 %collective-permute-done.1 = f32[4,384,128]{2,1,0:T(8,128)S(1)} collective-permute-done((f32[4,384,128]{2,1,0:T(8,128)S(1)}, f32[4,384,128]{2,1,0:T(8,128)S(1)}, u32[]{:S(2)}, u32[]{:S(2)}) %collective-permute-start.1) | collective-permute-done | bytes 786464 | tf_op jit(solution)/shard_map/ppermute | solution.py:194
  53.3 0.1 slice_add_fusion.1
  53.4 2.1 %collective-permute-start.2 = (f32[2,384,128]{2,1,0:T(8,128)S(1)}, f32[2,384,128]{2,1,0:T(8,128)S(1)}, u32[]{:S(2)}, u32[]{:S(2)}) collective-permute-start(f32[2,384,128]{2,1,0:T(8,128)S(1)} %slice.67), channel_id=1, source_target_pairs={{0,16},{4,12},{8,24},{12,4},{16,0},{20,28},{24,8},{28,20},{1,17},{... | collective-permute-start | bytes 1179656 | tf_op jit(solution)/shard_map/ppermute | solution.py:194
  55.5 0.0 collective-permute-done.7
  55.6 1.6 %collective-permute-start.8 = (f32[2,2,96,128]{3,2,1,0:T(8,128)S(1)}, f32[2,2,96,128]{3,2,1,0:T(8,128)S(1)}, u32[]{:S(2)}, u32[]{:S(2)}) collective-permute-start(f32[2,2,96,128]{3,2,1,0:T(8,128)S(1)} %slice_bitcast_fusion), channel_id=1, source_target_pairs={{0,1},{1,0},{2,3},{3,2},{4,5},{5,4},{6,7},{7,6},{8,9},{9,8},{10,11... | collective-permute-start | bytes 589832 | tf_op jit(solution)/shard_map/ppermute | solution.py:200
  57.2 4.0 %collective-permute-done.2 = f32[2,384,128]{2,1,0:T(8,128)S(1)} collective-permute-done((f32[2,384,128]{2,1,0:T(8,128)S(1)}, f32[2,384,128]{2,1,0:T(8,128)S(1)}, u32[]{:S(2)}, u32[]{:S(2)}) %collective-permute-start.2) | collective-permute-done | bytes 393248 | tf_op jit(solution)/shard_map/ppermute | solution.py:194
  61.3 0.1 slice_add_fusion.3
  61.3 2.1 %collective-permute-start.3 = (f32[2,2,96,128]{3,2,1,0:T(8,128)S(1)}, f32[2,2,96,128]{3,2,1,0:T(8,128)S(1)}, u32[]{:S(2)}, u32[]{:S(2)}) collective-permute-start(f32[2,2,96,128]{3,2,1,0:T(8,128)S(1)} %slice_bitcast_fusion.2), channel_id=1, source_target_pairs={{0,1},{1,0},{2,3},{3,2},{4,5},{5,4},{6,7},{7,6},{8,9},{9,8},{10,11... | collective-permute-start | bytes 589832 | tf_op jit(solution)/shard_map/ppermute | solution.py:200
  63.5 0.0 collective-permute-done.8
  63.5 2.6 %collective-permute-start.9 = (f32[2,1,96,128]{3,2,0,1:T(8,128)S(1)}, f32[2,1,96,128]{3,2,0,1:T(8,128)S(1)}, u32[]{:S(2)}, u32[]{:S(2)}) collective-permute-start(f32[2,1,96,128]{3,2,0,1:T(8,128)S(1)} %slice_bitcast_fusion.4), channel_id=1, source_target_pairs={{0,2},{1,3},{2,0},{3,1},{4,6},{5,7},{6,4},{7,5},{8,10},{9,11},{10,... | collective-permute-start | bytes 294920 | tf_op jit(solution)/shard_map/ppermute | solution.py:200
  66.2 1.8 %collective-permute-done.3 = f32[2,2,96,128]{3,2,1,0:T(8,128)S(1)} collective-permute-done((f32[2,2,96,128]{3,2,1,0:T(8,128)S(1)}, f32[2,2,96,128]{3,2,1,0:T(8,128)S(1)}, u32[]{:S(2)}, u32[]{:S(2)}) %collective-permute-start.3) | collective-permute-done | bytes 196640 | tf_op jit(solution)/shard_map/ppermute | solution.py:200
  68.0 2.6 %collective-permute-start.4 = (f32[2,1,96,128]{3,2,0,1:T(8,128)S(1)}, f32[2,1,96,128]{3,2,0,1:T(8,128)S(1)}, u32[]{:S(2)}, u32[]{:S(2)}) collective-permute-start(f32[2,1,96,128]{3,2,0,1:T(8,128)S(1)} %slice_bitcast_fusion.6), channel_id=1, source_target_pairs={{0,2},{1,3},{2,0},{3,1},{4,6},{5,7},{6,4},{7,5},{8,10},{9,11},{10,... | collective-permute-start | bytes 294920 | tf_op jit(solution)/shard_map/ppermute | solution.py:200
  70.6 0.0 collective-permute-done.9
  70.6 3.0 %collective-permute-done.4 = f32[2,1,96,128]{3,2,0,1:T(8,128)S(1)} collective-permute-done((f32[2,1,96,128]{3,2,0,1:T(8,128)S(1)}, f32[2,1,96,128]{3,2,0,1:T(8,128)S(1)}, u32[]{:S(2)}, u32[]{:S(2)}) %collective-permute-start.4) | collective-permute-done | bytes 98336 | tf_op jit(solution)/shard_map/ppermute | solution.py:200
  73.6 0.8 %copy.10 = f32[2,2,2,2,24,128]{5,2,1,4,3,0:T(2,128)} copy(f32[2,2,2,2,24,128]{5,4,3,1,0,2:T(8,128)S(1)} %pad_maximum_fusion) | data formatting | bytes 393216 | tf_op jit(solution)/shard_map/stack | solution.py:204
  (13 shorter events, 0.2 us)
Async XLA Ops:
  0.0 0.7 copy-start
  14.5 13.0 %copy-start.2 = (f32[8,384,128]{2,1,0:T(8,128)S(1)}, f32[8,384,128]{2,1,0:T(8,128)}, u32[]{:S(2)}) copy-start(f32[8,384,128]{2,1,0:T(8,128)} %get-tuple-element.11) | copy-start | bytes 4718596
  14.5 13.0 %collective-permute-start.5 = (f32[8,384,128]{2,1,0:T(8,128)}, f32[8,384,128]{2,1,0:T(8,128)S(1)}, u32[]{:S(2)}, u32[]{:S(2)}) collective-permute-start(f32[8,384,128]{2,1,0:T(8,128)} %get-tuple-element.12), channel_id=1, source_target_pairs={{0,4},{4,0},{8,12},{12,8},{16,20},{20,16},{24,28},{28,24},{1,5},{5... | collective-permute-start | bytes 4718600 | tf_op jit(solution)/shard_map/ppermute | solution.py:191
  27.5 3.6 %collective-permute-start = (f32[8,384,128]{2,1,0:T(8,128)}, f32[8,384,128]{2,1,0:T(8,128)S(1)}, u32[]{:S(2)}, u32[]{:S(2)}) collective-permute-start(f32[8,384,128]{2,1,0:T(8,128)} %get-tuple-element.10), channel_id=1, source_target_pairs={{0,4},{4,0},{8,12},{12,8},{16,20},{20,16},{24,28},{28,24},{1,5},{5... | collective-permute-start | bytes 4718600 | tf_op jit(solution)/shard_map/ppermute | solution.py:191
  27.7 3.4 %copy-start.1 = (f32[8,384,128]{2,1,0:T(8,128)S(1)}, f32[8,384,128]{2,1,0:T(8,128)}, u32[]{:S(2)}) copy-start(f32[8,384,128]{2,1,0:T(8,128)} %get-tuple-element.9) | copy-start | bytes 4718596
  27.8 12.8 %collective-permute-start.6 = (f32[4,384,128]{2,1,0:T(8,128)S(1)}, f32[4,384,128]{2,1,0:T(8,128)S(1)}, u32[]{:S(2)}, u32[]{:S(2)}) collective-permute-start(f32[4,384,128]{2,1,0:T(8,128)S(1)} %slice.73), channel_id=1, source_target_pairs={{0,8},{4,20},{8,0},{12,28},{16,24},{20,4},{24,16},{28,12},{1,9},{5... | collective-permute-start | bytes 2359304 | tf_op jit(solution)/shard_map/ppermute | solution.py:194
  31.4 21.9 %collective-permute-start.1 = (f32[4,384,128]{2,1,0:T(8,128)S(1)}, f32[4,384,128]{2,1,0:T(8,128)S(1)}, u32[]{:S(2)}, u32[]{:S(2)}) collective-permute-start(f32[4,384,128]{2,1,0:T(8,128)S(1)} %slice.65), channel_id=1, source_target_pairs={{0,8},{4,20},{8,0},{12,28},{16,24},{20,4},{24,16},{28,12},{1,9},{5... | collective-permute-start | bytes 2359304 | tf_op jit(solution)/shard_map/ppermute | solution.py:194
  40.7 14.8 %collective-permute-start.7 = (f32[2,384,128]{2,1,0:T(8,128)S(1)}, f32[2,384,128]{2,1,0:T(8,128)S(1)}, u32[]{:S(2)}, u32[]{:S(2)}) collective-permute-start(f32[2,384,128]{2,1,0:T(8,128)S(1)} %slice.75), channel_id=1, source_target_pairs={{0,16},{4,12},{8,24},{12,4},{16,0},{20,28},{24,8},{28,20},{1,17},{... | collective-permute-start | bytes 1179656 | tf_op jit(solution)/shard_map/ppermute | solution.py:194
  53.4 7.9 %collective-permute-start.2 = (f32[2,384,128]{2,1,0:T(8,128)S(1)}, f32[2,384,128]{2,1,0:T(8,128)S(1)}, u32[]{:S(2)}, u32[]{:S(2)}) collective-permute-start(f32[2,384,128]{2,1,0:T(8,128)S(1)} %slice.67), channel_id=1, source_target_pairs={{0,16},{4,12},{8,24},{12,4},{16,0},{20,28},{24,8},{28,20},{1,17},{... | collective-permute-start | bytes 1179656 | tf_op jit(solution)/shard_map/ppermute | solution.py:194
  55.6 7.9 %collective-permute-start.8 = (f32[2,2,96,128]{3,2,1,0:T(8,128)S(1)}, f32[2,2,96,128]{3,2,1,0:T(8,128)S(1)}, u32[]{:S(2)}, u32[]{:S(2)}) collective-permute-start(f32[2,2,96,128]{3,2,1,0:T(8,128)S(1)} %slice_bitcast_fusion), channel_id=1, source_target_pairs={{0,1},{1,0},{2,3},{3,2},{4,5},{5,4},{6,7},{7,6},{8,9},{9,8},{10,11... | collective-permute-start | bytes 589832 | tf_op jit(solution)/shard_map/ppermute | solution.py:200
  61.3 6.6 %collective-permute-start.3 = (f32[2,2,96,128]{3,2,1,0:T(8,128)S(1)}, f32[2,2,96,128]{3,2,1,0:T(8,128)S(1)}, u32[]{:S(2)}, u32[]{:S(2)}) collective-permute-start(f32[2,2,96,128]{3,2,1,0:T(8,128)S(1)} %slice_bitcast_fusion.2), channel_id=1, source_target_pairs={{0,1},{1,0},{2,3},{3,2},{4,5},{5,4},{6,7},{7,6},{8,9},{9,8},{10,11... | collective-permute-start | bytes 589832 | tf_op jit(solution)/shard_map/ppermute | solution.py:200
  63.5 7.1 %collective-permute-start.9 = (f32[2,1,96,128]{3,2,0,1:T(8,128)S(1)}, f32[2,1,96,128]{3,2,0,1:T(8,128)S(1)}, u32[]{:S(2)}, u32[]{:S(2)}) collective-permute-start(f32[2,1,96,128]{3,2,0,1:T(8,128)S(1)} %slice_bitcast_fusion.4), channel_id=1, source_target_pairs={{0,2},{1,3},{2,0},{3,1},{4,6},{5,7},{6,4},{7,5},{8,10},{9,11},{10,... | collective-permute-start | bytes 294920 | tf_op jit(solution)/shard_map/ppermute | solution.py:200
  68.0 5.6 %collective-permute-start.4 = (f32[2,1,96,128]{3,2,0,1:T(8,128)S(1)}, f32[2,1,96,128]{3,2,0,1:T(8,128)S(1)}, u32[]{:S(2)}, u32[]{:S(2)}) collective-permute-start(f32[2,1,96,128]{3,2,0,1:T(8,128)S(1)} %slice_bitcast_fusion.6), channel_id=1, source_target_pairs={{0,2},{1,3},{2,0},{3,1},{4,6},{5,7},{6,4},{7,5},{8,10},{9,11},{10,... | collective-permute-start | bytes 294920 | tf_op jit(solution)/shard_map/ppermute | solution.py:200

commit v2 on v0

v2 whole, which is shorter than its diff:
```python
import math

import jax
import jax.numpy as jnp
import numpy as np
from jax import lax
from jax.experimental import pallas as pl
from jax.experimental.pallas import tpu as pltpu
from jax.sharding import PartitionSpec as P

NF = 384
TILES_DEV = 2
GROUPS = ((0, 4), (2, 6), (1, 7), (3, 5))
CHUNKS = ((0, 1), (2, 3))
ORDERS = ("csz", "csz")
CALLS = ((0,), (1,))
DEPTH = 2
VMEM_SUMS = 16 << 20
VMEM_LIMIT = 24 << 20


def bit_orders(shot_count):
    bits = list(range(1, shot_count.bit_length() - 1))
    turn = len(bits) // 2
    return bits, bits[turn:] + bits[:turn]


def dft_tables(groups, freq_count, time_len):
    freq_here = NF // freq_count
    scale = 1.0 / math.sqrt(time_len)
    tables = []
    for g in groups:
        residues = GROUPS[g]
        rows = []
        for owner in range(freq_count):
            if residues[0] % 2 == 0:
                freqs = owner * freq_here + np.arange(residues[0], freq_here, 4)
                angle = 2.0 * math.pi / time_len * (freqs[:, None] * np.arange(time_len // 4) % time_len)
                rows += [np.cos(angle), -np.sin(angle)]
            else:
                for residue in residues:
                    freqs = owner * freq_here + np.arange(residue, freq_here, 8)
                    angle = 2.0 * math.pi / time_len * (freqs[:, None] * np.arange(time_len // 8) % time_len)
                    cos, sin = np.cos(angle), np.sin(angle)
                    sign = 1.0 if residue in (1, 5) else -1.0
                    rows += [np.hstack([cos, -sign * sin]), np.hstack([-sin, -sign * cos])]
        tables.append((np.concatenate(rows) * scale).reshape(freq_count, -1, time_len // 4))
    return np.stack(tables).astype(np.float32)


def fold(x, groups):
    eighth = x.shape[1] // 8
    q0, q1, q2, q3 = (x[:, 2 * i * eighth : 2 * (i + 1) * eighth] for i in range(4))
    folded = {}
    if 0 in groups or 1 in groups:
        plus, cross = q0 + q2, q1 + q3
        folded[0], folded[1] = plus + cross, plus - cross
    if 2 in groups or 3 in groups:
        d02, d13 = q0 - q2, q1 - q3
        d0, d1, d2, d3 = d02[:, :eighth], d02[:, eighth:], d13[:, :eighth], d13[:, eighth:]
        root = math.sqrt(0.5)
        near, far = (d1 - d3) * root, (d1 + d3) * root
        folded[2] = jnp.concatenate([d0 + near, d2 + far], axis=1)
        folded[3] = jnp.concatenate([d0 - near, d2 - far], axis=1)
    return [folded[g] for g in groups]


def split(value):
    high = value.astype(jnp.bfloat16)
    return high, (value - high.astype(jnp.float32)).astype(jnp.bfloat16)


def dot_nt(a, b):
    return lax.dot_general(a, b, (((1,), (1,)), ((), ())), preferred_element_type=jnp.float32)


def slot_of(tile, me_shot, shot_count):
    owner = tile // TILES_DEV
    apart = jnp.bitwise_xor(owner, me_shot)

    def place(order):
        index = 0
        for bit in order:
            index = index * 2 + jnp.bitwise_and(jnp.right_shift(apart, bit), 1)
        return index

    first, second = bit_orders(shot_count)
    index = jnp.where(jnp.bitwise_and(owner, 1) == 0, place(first), place(second))
    half = shot_count // 2 * TILES_DEV
    return jnp.bitwise_and(apart, 1) * half + index * TILES_DEV + jnp.bitwise_and(tile, TILES_DEV - 1)


def bin_kernel(chunks, shot_count, freq_count, load, tiles, x_ref, w_ref, t_hbm, *refs):
    outs, refs = refs[: len(chunks)], refs[len(chunks) :]
    if load:
        x_hbm, w_hbm, xbuf, wbuf = x_ref, w_ref, refs[0], refs[1]
        refs = refs[2:]
    else:
        xbuf, wbuf = x_ref, w_ref
    tbuf, table, spectra, xsem, wsem, tsem = refs
    shots_here, blocks_here, block_len, tile_len = wbuf.shape
    me_shot, me_freq = lax.axis_index("shot"), lax.axis_index("freq")
    rows = t_hbm.shape[2]
    groups = [g for chunk in chunks for g in chunk]
    place, stride, start = {}, {}, 0
    for chunk in chunks:
        for j, g in enumerate(chunk):
            place[g], stride[g] = start + j * rows, len(chunk) * rows
        start += len(chunk) * freq_count * rows

    def x_copy(i):
        return pltpu.make_async_copy(x_hbm.at[i], xbuf.at[i], xsem.at[i])

    def w_copy(i):
        return pltpu.make_async_copy(w_hbm.at[i, pl.ds(me_freq * blocks_here, blocks_here)], wbuf.at[i], wsem.at[i])

    def t_copy(i):
        return pltpu.make_async_copy(t_hbm.at[:, jnp.bitwise_xor(me_freq, i)], tbuf.at[:, i], tsem.at[i])

    for i in range(freq_count):
        t_copy(i).start()
    if load:
        x_copy(0).start()
        w_copy(0).start()
        for i in range(1, DEPTH):
            x_copy(i).start()
    for out in outs:
        out[...] = jnp.zeros_like(out)
    for i in range(freq_count):
        t_copy(i).wait()
    for n in range(len(groups)):
        high, low = split(jnp.concatenate([tbuf[n, i] for i in range(freq_count)], axis=0))
        table[n] = jnp.concatenate([high, low], axis=0)

    def transform(i, n, part):
        high, low = split(part)
        wide = dot_nt(table[n], high)
        half = wide.shape[0] // 2
        result = wide[:half] + wide[half:] + dot_nt(table[n, :half], low)
        g = groups[n]
        for j in range(freq_count):
            start = place[g] + j * stride[g]
            spectra[i % 2, start : start + rows] = result[j * rows : (j + 1) * rows]

    def spread(i, b):
        if load and b == 0:
            w_copy(i).wait()
        s_high, s_low = split(spectra[i % 2, :, b * block_len : (b + 1) * block_len])
        w_high, w_low = split(wbuf[i, b])
        weights = jnp.concatenate(
            [
                jnp.concatenate([w_high, w_low], axis=1),
                jnp.concatenate([w_high, jnp.zeros_like(w_low)], axis=1),
            ],
            axis=0,
        )
        both = jnp.dot(jnp.concatenate([s_high, s_low], axis=1), weights, preferred_element_type=jnp.float32)
        value = both[:, :tile_len] + both[:, tile_len:]
        slot = slot_of(tiles[i, me_freq * blocks_here + b], me_shot, shot_count)
        start = 0
        for out in outs:
            out[slot] += value[start : start + out.shape[1]]
            start += out.shape[1]

    for i in range(shots_here + 1):
        folded = ()
        if i < shots_here:
            if load:
                x_copy(i).wait()
                if i + DEPTH < shots_here:
                    x_copy(i + DEPTH).start()
                if i + 1 < shots_here:
                    w_copy(i + 1).start()
            folded = fold(xbuf[i], groups)
        for k in range(max(len(folded), blocks_here)):
            if k < len(folded):
                transform(i, k, folded[k])
            if i and k < blocks_here:
                spread(i - 1, k)


def bin_blocks(tile_ids, traces, interp_weights, chunks, shot_count, freq_count, load, keep):
    shots_here, recs_here, time_len = traces.shape
    block_len, tile_len = interp_weights.shape[2:]
    blocks_here = recs_here // block_len
    groups = [g for chunk in chunks for g in chunk]
    tables = jnp.asarray(dft_tables(groups, freq_count, time_len))
    rows = freq_count * tables.shape[2]
    slot_count = shot_count * TILES_DEV
    kept = [
        jax.ShapeDtypeStruct(traces.shape, jnp.float32),
        jax.ShapeDtypeStruct((shots_here, blocks_here, block_len, tile_len), jnp.float32),
    ]
    total = slot_count * len(GROUPS) * rows * tile_len * 4
    sums = pltpu.VMEM if total <= VMEM_SUMS else jax.ShapeDtypeStruct
    out_shape = [sums((slot_count, rows * len(chunk), tile_len), jnp.float32) for chunk in chunks]
    scratch = [
        pltpu.VMEM(tables.shape, jnp.float32),
        pltpu.VMEM((len(groups), 2 * rows, tables.shape[3]), jnp.bfloat16),
        pltpu.VMEM((2, len(groups) * rows, recs_here), jnp.float32),
        pltpu.SemaphoreType.DMA((shots_here,)),
        pltpu.SemaphoreType.DMA((shots_here,)),
        pltpu.SemaphoreType.DMA((freq_count,)),
    ]
    if load and keep:
        out_shape += [pltpu.VMEM(k.shape, k.dtype) for k in kept]
    elif load:
        scratch = [pltpu.VMEM(k.shape, k.dtype) for k in kept] + scratch
    place = pltpu.HBM if load else pltpu.VMEM

    def body(*refs):
        bin_kernel(chunks, shot_count, freq_count, load, *refs)

    traces = pltpu.with_memory_space_constraint(traces, place)
    interp_weights = pltpu.with_memory_space_constraint(interp_weights, place)
    tables = pltpu.with_memory_space_constraint(tables, pltpu.HBM)
    return pl.pallas_call(
        body,
        in_specs=[
            pl.BlockSpec(memory_space=pltpu.SMEM),
            pl.BlockSpec(memory_space=place),
            pl.BlockSpec(memory_space=place),
            pl.BlockSpec(memory_space=pltpu.HBM),
        ],
        out_specs=[pl.BlockSpec(memory_space=pltpu.VMEM)] * len(out_shape),
        out_shape=out_shape,
        scratch_shapes=scratch,
        compiler_params=pltpu.CompilerParams(vmem_limit_bytes=VMEM_LIMIT),
        name="bin_blocks",
    )(tile_ids, traces, interp_weights, tables)


def shards(traces, interp_weights, tile_ids):
    shot_count = lax.axis_size("shot")
    freq_count = lax.axis_size("freq")
    tile_len = interp_weights.shape[3]
    levels = bit_orders(shot_count)

    def to_core(value):
        half = value.shape[0] // 2
        got = lax.ppermute(value[half:], "shot", [(i, i ^ 1) for i in range(shot_count)])
        return value[:half] + got

    def to_shot(value, level):
        half = value.shape[0] // 2
        pairs = [(i, i ^ (1 << levels[i & 1][level])) for i in range(shot_count)]
        return value[:half] + lax.ppermute(value[half:], "shot", pairs)

    def to_freq(value, flip):
        value = value.reshape(value.shape[0], -1, 2, value.shape[2], tile_len)
        got = lax.ppermute(value[:, :, 1], "freq", [(i, i ^ flip) for i in range(freq_count)])
        return value[:, :, 0] + got

    def to_freq_direct(value):
        total = value[:, 0]
        for flip in range(freq_count - 1, 0, -1):
            total += lax.ppermute(value[:, flip], "freq", [(i, i ^ flip) for i in range(freq_count)])
        return total[:, None]

    sums = [None] * len(CHUNKS)
    for n, call in enumerate(CALLS):
        chunks = tuple(CHUNKS[c] for c in call)
        made = bin_blocks(
            tile_ids, traces, interp_weights, chunks, shot_count, freq_count, n == 0, n == 0 and len(CALLS) > 1
        )
        for c, value in zip(call, made):
            sums[c] = value
        if len(made) > len(call):
            traces, interp_weights = made[len(call) :]
    parts = [None] * len(GROUPS)
    for chunk, order, value in zip(CHUNKS, ORDERS, sums):
        value = value.reshape(value.shape[0], freq_count, -1, tile_len)
        level, flip = 0, 1
        for stage in order:
            if stage == "c":
                value = to_core(value)
            elif stage == "s":
                for level in range(len(levels[0])):
                    value = to_shot(value, level)
            elif stage == "d":
                value = to_freq_direct(value)
            else:
                flip = 1
                while flip < freq_count:
                    value = to_freq(value, flip)
                    flip *= 2
        value = value.reshape(TILES_DEV, len(chunk), -1, tile_len)
        for j, g in enumerate(chunk):
            parts[g] = value[:, j]
    eighths = {}
    for g, residues in enumerate(GROUPS):
        if residues[0] % 2 == 0:
            part = parts[g].reshape(TILES_DEV, 2, -1, 2, tile_len)
            for j, residue in enumerate(residues):
                eighths[residue] = part[:, :, :, j]
        else:
            part = parts[g].reshape(TILES_DEV, 2, 2, -1, tile_len)
            for j, residue in enumerate(residues):
                eighths[residue] = part[:, j]
    return jnp.stack([eighths[r] for r in range(8)], axis=3).reshape(TILES_DEV, 2, -1, tile_len)


def solution(mesh):
    in_specs = (P("shot", "freq", None), P("shot", None, None, None), P("shot", None))
    out_specs = P("shot", None, "freq", None)
    return jax.shard_map(shards, mesh=mesh, in_specs=in_specs, out_specs=out_specs, check_vma=False)
```

time: 408 us -> 60.8 us (0.15); the launches traced: 402 us -> 60.7 us
  waiting for transfers between devices: 275 us -> 25.7 us
  matrix products: 56.1 us -> 0 us
  local copies, waits for them, and re-layouts: 47.5 us -> 2.79 us
  Pallas kernels: 0 us -> 11.2 us
  other arithmetic: 7.32 us -> 1.02 us
  starting transfers between devices: 15.6 us -> 19.7 us
    all_to_all x3 -> x0, waiting for transfers between devices: 275 us -> none  [the longest x1 138 us: shards(): lax.all_to_all(send_rows.reshape(shot_count, cap_slots, width), 'shot', s...]
    dot_general x4 -> x0, matrix products: 56.1 us -> none  [the longest x1 24.5 us: shards(): spectrum = jnp.einsum('cft,srt->scfr', tables, traces, precision=highest)]
    ppermute x0 -> x10, waiting for transfers between devices: none -> 25.7 us  [the longest x4 21.3 us: to_shot(): return value[:half] + lax.ppermute(value[half:], 'shot', pairs)]
    reshape x4 -> x0, local copies, waits for them, and re-layouts: 24.7 us -> none  [the longest x1 10.5 us: shards(): received.reshape(shot_count * cap_slots, width)]
    ppermute x0 -> x10, starting transfers between devices: none -> 19.7 us  [the longest x4 9.92 us: to_shot(): return value[:half] + lax.ppermute(value[half:], 'shot', pairs)]
    all_to_all x3 -> x0, starting transfers between devices: 15.6 us -> none  [the longest x1 6.45 us: shards(): lax.all_to_all(spectrum, 'freq', split_axis=2, concat_axis=3, tiled=True)]
    pallas_call x0 -> x2, Pallas kernels: none -> 11.2 us  [bin_blocks(): pl.pallas_call(body, in_specs=[pl.BlockSpec(memory_space=pltpu.SMEM), pl....]
    all_to_all x2 -> x0, local copies, waits for them, and re-layouts: 10 us -> none  [the longest x1 9.48 us: shards(): lax.all_to_all(spectrum, 'freq', split_axis=2, concat_axis=3, tiled=True)]
  transfers between devices with their start and end apart: 3 -> 10, of which waited for: 2 -> 7; matrix products, arithmetic and copies ran while one was open for 13% -> 3% of each run, Pallas kernels for 0% -> 8%
where the time goes in v2:
time: 60.8 us; the launch traced here: 60.7 us
  waiting for transfers between devices  25.7 us (42%)
  starting transfers between devices  19.7 us (32%)
  Pallas kernels  11.2 us (18%)
  local copies, waits for them, and re-layouts  2.79 us (5%)
  other arithmetic  1.02 us (2%)
    ppermute x4, waiting for transfers between devices, to_shot(): return value[:half] + lax.ppermute(value[half:], 'shot', pairs)  21.3 us
    pallas_call x2, Pallas kernels, bin_blocks(): pl.pallas_call(body, in_specs=[pl.BlockSpec(memory_space=pltpu.SMEM), pl....  11.2 us
    ppermute x4, starting transfers between devices, to_shot(): return value[:half] + lax.ppermute(value[half:], 'shot', pairs)  9.92 us
    ppermute x4, starting transfers between devices, to_freq(): lax.ppermute(value[:, :, 1], 'freq', [(i, i ^ flip) for i in range(freq_c...  9.16 us
    ppermute x4, waiting for transfers between devices, to_freq(): lax.ppermute(value[:, :, 1], 'freq', [(i, i ^ flip) for i in range(freq_c...  4.34 us
  transfers between devices with their start and end apart: 10, of which 7 were waited for; matrix products, arithmetic and copies ran while one was open for 3% of the time, Pallas kernels for 8%

profile of v2, /device:TPU:0, one launch (start us, length us, event | category | flops | bytes accessed | tf_op | source)
XLA Modules:
  0.0 60.7 jit_solution(3346929570812245441)
XLA Ops:
  0.0 0.0 copy-start
  0.0 0.7 %copy-done = s32[4,16]{1,0:T(4,128)S(1)} copy-done((s32[4,16]{1,0:T(4,128)S(1)}, s32[4,16]{1,0:T(4,128)}, u32[]{:S(2)}) %copy-start) | copy-done | bytes 280
  0.7 6.5 %bin_blocks.2 = (f32[16,384,128]{2,1,0:T(8,128)S(1)}, f32[4,512,1024]{2,1,0:T(8,128)S(1)}, f32[4,4,128,128]{3,2,1,0:T(8,128)S(1)}) custom-call(s32[4,16]{1,0:T(4,128)S(1)} %copy-done, f32[4,512,1024]{2,1,0:T(8,128)} %refs_1_.1, f32[4,16,128,128]{3,2,1,0:T(8,128)} %refs_2_.1, f32[2,4,48,256]{3,2,1,0:T(8,128)} %constant.4.clone.refs_3_), custom_call_target="tpu_custom_call" | custom-call | tf_op jit(solution)/shard_map/bin_blocks/pallas_call | solution.py:217
  7.2 0.3 fusion.7
  7.5 0.5 collective-permute-start
  8.0 4.7 %bin_blocks.3 = f32[16,384,128]{2,1,0:T(8,128)S(1)} custom-call(s32[4,16]{1,0:T(4,128)S(1)} %copy-done, f32[4,512,1024]{2,1,0:T(8,128)S(1)} %get-tuple-element.9.refs_1_, f32[4,4,128,128]{3,2,1,0:T(8,128)S(1)} %get-tuple-element.10.refs_2_, f32[2,4,48,256]{3,2,1,0:T(8,128)} %constant.5.clone.refs_3_), custom_call_target="tpu_custom_call" | custom-call | tf_op jit(solution)/shard_map/bin_blocks/pallas_call | solution.py:217
  12.7 0.3 fusion.6
  13.0 0.1 collective-permute-start.5
  13.1 0.0 collective-permute-done
  13.1 0.2 add.30
  13.3 0.1 slice.145
  13.4 3.0 %collective-permute-start.1 = (f32[4,4,96,128]{3,2,1,0:T(8,128)S(1)}, f32[4,4,96,128]{3,2,1,0:T(8,128)S(1)}, u32[]{:S(2)}, u32[]{:S(2)}) collective-permute-start(f32[4,4,96,128]{3,2,1,0:T(8,128)S(1)} %slice.145), channel_id=1, source_target_pairs={{0,8},{4,20},{8,0},{12,28},{16,24},{20,4},{24,16},{28,12},{1,9},{5... | collective-permute-start | bytes 2359304 | tf_op jit(solution)/shard_map/ppermute | solution.py:247
  16.4 0.1 collective-permute-done.5
  16.5 0.2 add.35
  16.7 0.1 slice.157
  16.7 2.7 %collective-permute-start.6 = (f32[4,4,96,128]{3,2,1,0:T(8,128)S(1)}, f32[4,4,96,128]{3,2,1,0:T(8,128)S(1)}, u32[]{:S(2)}, u32[]{:S(2)}) collective-permute-start(f32[4,4,96,128]{3,2,1,0:T(8,128)S(1)} %slice.157), channel_id=1, source_target_pairs={{0,8},{4,20},{8,0},{12,28},{16,24},{20,4},{24,16},{28,12},{1,9},{5... | collective-permute-start | bytes 2359304 | tf_op jit(solution)/shard_map/ppermute | solution.py:247
  19.4 6.9 %collective-permute-done.1 = f32[4,4,96,128]{3,2,1,0:T(8,128)S(1)} collective-permute-done((f32[4,4,96,128]{3,2,1,0:T(8,128)S(1)}, f32[4,4,96,128]{3,2,1,0:T(8,128)S(1)}, u32[]{:S(2)}, u32[]{:S(2)}) %collective-permute-start.1) | collective-permute-done | bytes 786464 | tf_op jit(solution)/shard_map/ppermute | solution.py:247
  26.4 0.1 slice_add_fusion.1
  26.5 2.1 %collective-permute-start.2 = (f32[2,4,96,128]{3,2,1,0:T(8,128)S(1)}, f32[2,4,96,128]{3,2,1,0:T(8,128)S(1)}, u32[]{:S(2)}, u32[]{:S(2)}) collective-permute-start(f32[2,4,96,128]{3,2,1,0:T(8,128)S(1)} %slice.147), channel_id=1, source_target_pairs={{0,16},{4,12},{8,24},{12,4},{16,0},{20,28},{24,8},{28,20},{1,17},{... | collective-permute-start | bytes 1179656 | tf_op jit(solution)/shard_map/ppermute | solution.py:247
  28.6 10.4 %collective-permute-done.6 = f32[4,4,96,128]{3,2,1,0:T(8,128)S(1)} collective-permute-done((f32[4,4,96,128]{3,2,1,0:T(8,128)S(1)}, f32[4,4,96,128]{3,2,1,0:T(8,128)S(1)}, u32[]{:S(2)}, u32[]{:S(2)}) %collective-permute-start.6) | collective-permute-done | bytes 786464 | tf_op jit(solution)/shard_map/ppermute | solution.py:247
  39.0 0.1 slice_add_fusion
  39.2 2.1 %collective-permute-start.7 = (f32[2,4,96,128]{3,2,1,0:T(8,128)S(1)}, f32[2,4,96,128]{3,2,1,0:T(8,128)S(1)}, u32[]{:S(2)}, u32[]{:S(2)}) collective-permute-start(f32[2,4,96,128]{3,2,1,0:T(8,128)S(1)} %slice.159), channel_id=1, source_target_pairs={{0,16},{4,12},{8,24},{12,4},{16,0},{20,28},{24,8},{28,20},{1,17},{... | collective-permute-start | bytes 1179656 | tf_op jit(solution)/shard_map/ppermute | solution.py:247
  41.3 0.0 collective-permute-done.2
  41.3 1.7 %collective-permute-start.3 = (f32[2,2,96,128]{3,2,1,0:T(8,128)S(1)}, f32[2,2,96,128]{3,2,1,0:T(8,128)S(1)}, u32[]{:S(2)}, u32[]{:S(2)}) collective-permute-start(f32[2,2,96,128]{3,2,1,0:T(8,128)S(1)} %slice_bitcast_fusion), channel_id=1, source_target_pairs={{0,1},{1,0},{2,3},{3,2},{4,5},{5,4},{6,7},{7,6},{8,9},{9,8},{10,11... | collective-permute-start | bytes 589832 | tf_op jit(solution)/shard_map/ppermute | solution.py:251
  43.0 4.0 %collective-permute-done.7 = f32[2,4,96,128]{3,2,1,0:T(8,128)S(1)} collective-permute-done((f32[2,4,96,128]{3,2,1,0:T(8,128)S(1)}, f32[2,4,96,128]{3,2,1,0:T(8,128)S(1)}, u32[]{:S(2)}, u32[]{:S(2)}) %collective-permute-start.7) | collective-permute-done | bytes 393248 | tf_op jit(solution)/shard_map/ppermute | solution.py:247
  47.1 0.2 copy.56
  47.3 2.1 %collective-permute-start.8 = (f32[2,2,96,128]{3,0,2,1:T(2,128)S(1)}, f32[2,2,96,128]{3,0,2,1:T(2,128)S(1)}, u32[]{:S(2)}, u32[]{:S(2)}) collective-permute-start(f32[2,2,96,128]{3,0,2,1:T(2,128)S(1)} %bitcast.67), channel_id=1, source_target_pairs={{0,1},{1,0},{2,3},{3,2},{4,5},{5,4},{6,7},{7,6},{8,9},{9,8},{10,11... | collective-permute-start | bytes 589832 | tf_op jit(solution)/shard_map/ppermute | solution.py:251
  49.4 0.0 collective-permute-done.3
  49.4 2.7 %collective-permute-start.4 = (f32[2,1,96,128]{3,2,0,1:T(8,128)S(1)}, f32[2,1,96,128]{3,2,0,1:T(8,128)S(1)}, u32[]{:S(2)}, u32[]{:S(2)}) collective-permute-start(f32[2,1,96,128]{3,2,0,1:T(8,128)S(1)} %slice_bitcast_fusion.4), channel_id=1, source_target_pairs={{0,2},{1,3},{2,0},{3,1},{4,6},{5,7},{6,4},{7,5},{8,10},{9,11},{10,... | collective-permute-start | bytes 294920 | tf_op jit(solution)/shard_map/ppermute | solution.py:251
  52.1 1.5 %collective-permute-done.8 = f32[2,2,96,128]{3,0,2,1:T(2,128)S(1)} collective-permute-done((f32[2,2,96,128]{3,0,2,1:T(2,128)S(1)}, f32[2,2,96,128]{3,0,2,1:T(2,128)S(1)}, u32[]{:S(2)}, u32[]{:S(2)}) %collective-permute-start.8) | collective-permute-done | bytes 196640 | tf_op jit(solution)/shard_map/ppermute | solution.py:251
  53.6 0.2 fusion.3
  53.8 2.7 %collective-permute-start.9 = (f32[2,1,96,128]{3,0,2,1:T(2,128)S(1)}, f32[2,1,96,128]{3,0,2,1:T(2,128)S(1)}, u32[]{:S(2)}, u32[]{:S(2)}) collective-permute-start(f32[2,1,96,128]{3,0,2,1:T(2,128)S(1)} %slice_bitcast_fusion.2), channel_id=1, source_target_pairs={{0,2},{1,3},{2,0},{3,1},{4,6},{5,7},{6,4},{7,5},{8,10},{9,11},{10,... | collective-permute-start | bytes 294920 | tf_op jit(solution)/shard_map/ppermute | solution.py:251
  56.5 1.4 %collective-permute-done.4 = f32[2,1,96,128]{3,2,0,1:T(8,128)S(1)} collective-permute-done((f32[2,1,96,128]{3,2,0,1:T(8,128)S(1)}, f32[2,1,96,128]{3,2,0,1:T(8,128)S(1)}, u32[]{:S(2)}, u32[]{:S(2)}) %collective-permute-start.4) | collective-permute-done | bytes 98336 | tf_op jit(solution)/shard_map/ppermute | solution.py:251
  57.9 1.5 %collective-permute-done.9 = f32[2,1,96,128]{3,0,2,1:T(2,128)S(1)} collective-permute-done((f32[2,1,96,128]{3,0,2,1:T(2,128)S(1)}, f32[2,1,96,128]{3,0,2,1:T(2,128)S(1)}, u32[]{:S(2)}, u32[]{:S(2)}) %collective-permute-start.9) | collective-permute-done | bytes 98336 | tf_op jit(solution)/shard_map/ppermute | solution.py:251
  59.4 0.1 fusion.4
  59.5 0.1 fusion.12
  59.6 0.1 copy_bitcast_fusion.2
  59.7 0.1 copy_bitcast_fusion.3
  59.7 1.0 %stack.3 = f32[2,2,12,8,128]{4,3,2,1,0:T(8,128)} concatenate(f32[2,2,12,1,128]{4,3,2,1,0:T(1,128)S(1)} %get-tuple-element.33, f32[2,2,12,1,128]{4,3,2,1,0:T(1,128)S(1)} %get-tuple-element.30, f32[2,2,12,1,128]{4,3,2,1,0:T(1,128)S(1)} %get-tuple-element.24, f32[2,2,12,1,128]{4,3,2,1,0:T(1,128)S(1)} %get-tuple-element.32, f32[2,2,12,1,128]{4,3,2,1,0:T(1,128)S(1)} %get-tuple-element.34, ...), dimensions={3} | concatenate | bytes 393216 | tf_op jit(solution)/shard_map/stack | solution.py:300
  (14 shorter events, 0.3 us)
Async XLA Ops:
  0.0 0.7 %copy-start = (s32[4,16]{1,0:T(4,128)S(1)}, s32[4,16]{1,0:T(4,128)}, u32[]{:S(2)}) copy-start(s32[4,16]{1,0:T(4,128)} %refs_0_.3) | copy-start | bytes 772
  7.5 5.7 %collective-permute-start = (f32[8,4,96,128]{3,2,1,0:T(8,128)S(1)}, f32[8,4,96,128]{3,2,1,0:T(8,128)S(1)}, u32[]{:S(2)}, u32[]{:S(2)}) collective-permute-start(f32[8,4,96,128]{3,2,1,0:T(8,128)S(1)} %bitcast.61), channel_id=1, source_target_pairs={{0,4},{4,0},{8,12},{12,8},{16,20},{20,16},{24,28},{28,24},{1,5},{5... | collective-permute-start | bytes 4718600 | tf_op jit(solution)/shard_map/ppermute | solution.py:241
  13.0 3.5 %collective-permute-start.5 = (f32[8,4,96,128]{3,2,1,0:T(8,128)S(1)}, f32[8,4,96,128]{3,2,1,0:T(8,128)S(1)}, u32[]{:S(2)}, u32[]{:S(2)}) collective-permute-start(f32[8,4,96,128]{3,2,1,0:T(8,128)S(1)} %bitcast.62), channel_id=1, source_target_pairs={{0,4},{4,0},{8,12},{12,8},{16,20},{20,16},{24,28},{28,24},{1,5},{5... | collective-permute-start | bytes 4718600 | tf_op jit(solution)/shard_map/ppermute | solution.py:241
  13.4 13.0 %collective-permute-start.1 = (f32[4,4,96,128]{3,2,1,0:T(8,128)S(1)}, f32[4,4,96,128]{3,2,1,0:T(8,128)S(1)}, u32[]{:S(2)}, u32[]{:S(2)}) collective-permute-start(f32[4,4,96,128]{3,2,1,0:T(8,128)S(1)} %slice.145), channel_id=1, source_target_pairs={{0,8},{4,20},{8,0},{12,28},{16,24},{20,4},{24,16},{28,12},{1,9},{5... | collective-permute-start | bytes 2359304 | tf_op jit(solution)/shard_map/ppermute | solution.py:247
  16.7 22.3 %collective-permute-start.6 = (f32[4,4,96,128]{3,2,1,0:T(8,128)S(1)}, f32[4,4,96,128]{3,2,1,0:T(8,128)S(1)}, u32[]{:S(2)}, u32[]{:S(2)}) collective-permute-start(f32[4,4,96,128]{3,2,1,0:T(8,128)S(1)} %slice.157), channel_id=1, source_target_pairs={{0,8},{4,20},{8,0},{12,28},{16,24},{20,4},{24,16},{28,12},{1,9},{5... | collective-permute-start | bytes 2359304 | tf_op jit(solution)/shard_map/ppermute | solution.py:247
  26.5 14.8 %collective-permute-start.2 = (f32[2,4,96,128]{3,2,1,0:T(8,128)S(1)}, f32[2,4,96,128]{3,2,1,0:T(8,128)S(1)}, u32[]{:S(2)}, u32[]{:S(2)}) collective-permute-start(f32[2,4,96,128]{3,2,1,0:T(8,128)S(1)} %slice.147), channel_id=1, source_target_pairs={{0,16},{4,12},{8,24},{12,4},{16,0},{20,28},{24,8},{28,20},{1,17},{... | collective-permute-start | bytes 1179656 | tf_op jit(solution)/shard_map/ppermute | solution.py:247
  39.2 7.9 %collective-permute-start.7 = (f32[2,4,96,128]{3,2,1,0:T(8,128)S(1)}, f32[2,4,96,128]{3,2,1,0:T(8,128)S(1)}, u32[]{:S(2)}, u32[]{:S(2)}) collective-permute-start(f32[2,4,96,128]{3,2,1,0:T(8,128)S(1)} %slice.159), channel_id=1, source_target_pairs={{0,16},{4,12},{8,24},{12,4},{16,0},{20,28},{24,8},{28,20},{1,17},{... | collective-permute-start | bytes 1179656 | tf_op jit(solution)/shard_map/ppermute | solution.py:247
  41.3 8.1 %collective-permute-start.3 = (f32[2,2,96,128]{3,2,1,0:T(8,128)S(1)}, f32[2,2,96,128]{3,2,1,0:T(8,128)S(1)}, u32[]{:S(2)}, u32[]{:S(2)}) collective-permute-start(f32[2,2,96,128]{3,2,1,0:T(8,128)S(1)} %slice_bitcast_fusion), channel_id=1, source_target_pairs={{0,1},{1,0},{2,3},{3,2},{4,5},{5,4},{6,7},{7,6},{8,9},{9,8},{10,11... | collective-permute-start | bytes 589832 | tf_op jit(solution)/shard_map/ppermute | solution.py:251
  47.3 6.3 %collective-permute-start.8 = (f32[2,2,96,128]{3,0,2,1:T(2,128)S(1)}, f32[2,2,96,128]{3,0,2,1:T(2,128)S(1)}, u32[]{:S(2)}, u32[]{:S(2)}) collective-permute-start(f32[2,2,96,128]{3,0,2,1:T(2,128)S(1)} %bitcast.67), channel_id=1, source_target_pairs={{0,1},{1,0},{2,3},{3,2},{4,5},{5,4},{6,7},{7,6},{8,9},{9,8},{10,11... | collective-permute-start | bytes 589832 | tf_op jit(solution)/shard_map/ppermute | solution.py:251
  49.4 8.5 %collective-permute-start.4 = (f32[2,1,96,128]{3,2,0,1:T(8,128)S(1)}, f32[2,1,96,128]{3,2,0,1:T(8,128)S(1)}, u32[]{:S(2)}, u32[]{:S(2)}) collective-permute-start(f32[2,1,96,128]{3,2,0,1:T(8,128)S(1)} %slice_bitcast_fusion.4), channel_id=1, source_target_pairs={{0,2},{1,3},{2,0},{3,1},{4,6},{5,7},{6,4},{7,5},{8,10},{9,11},{10,... | collective-permute-start | bytes 294920 | tf_op jit(solution)/shard_map/ppermute | solution.py:251
  53.8 5.6 %collective-permute-start.9 = (f32[2,1,96,128]{3,0,2,1:T(2,128)S(1)}, f32[2,1,96,128]{3,0,2,1:T(2,128)S(1)}, u32[]{:S(2)}, u32[]{:S(2)}) collective-permute-start(f32[2,1,96,128]{3,0,2,1:T(2,128)S(1)} %slice_bitcast_fusion.2), channel_id=1, source_target_pairs={{0,2},{1,3},{2,0},{3,1},{4,6},{5,7},{6,4},{7,5},{8,10},{9,11},{10,... | collective-permute-start | bytes 294920 | tf_op jit(solution)/shard_map/ppermute | solution.py:251

commit v3 on v2

--- a/solution.py
+++ b/solution.py
@@ -12,17 +12,19 @@
 TILES_DEV = 2
 GROUPS = ((0, 4), (2, 6), (1, 7), (3, 5))
 CHUNKS = ((0, 1), (2, 3))
-ORDERS = ("csz", "csz")
+ORDERS = (("axyb", "yaxb"), ("xayb", "yaxb"))
 CALLS = ((0,), (1,))
 DEPTH = 2
 VMEM_SUMS = 16 << 20
 VMEM_LIMIT = 24 << 20
 
 
-def bit_orders(shot_count):
-    bits = list(range(1, shot_count.bit_length() - 1))
-    turn = len(bits) // 2
-    return bits, bits[turn:] + bits[:turn]
+def halvings(shot_count, freq_count):
+    shot_bits = [("shot", bit) for bit in range(1, shot_count.bit_length() - 1)]
+    freq_bits = [("freq", bit) for bit in range(freq_count.bit_length() - 1)]
+    x, a = len(shot_bits) // 2, len(freq_bits) // 2
+    steps = dict(x=shot_bits[:x], y=shot_bits[x:], a=freq_bits[:a], b=freq_bits[a:])
+    return [[[step for name in order for step in steps[name]] for order in orders] for orders in ORDERS]
 
 
 def dft_tables(groups, freq_count, time_len):
@@ -74,30 +76,35 @@
     return lax.dot_general(a, b, (((1,), (1,)), ((), ())), preferred_element_type=jnp.float32)
 
 
-def slot_of(tile, me_shot, shot_count):
+def slots_of(tile, me_shot, steps, freq_count):
     owner = tile // TILES_DEV
     apart = jnp.bitwise_xor(owner, me_shot)
-
-    def place(order):
-        index = 0
-        for bit in order:
-            index = index * 2 + jnp.bitwise_and(jnp.right_shift(apart, bit), 1)
-        return index
-
-    first, second = bit_orders(shot_count)
-    index = jnp.where(jnp.bitwise_and(owner, 1) == 0, place(first), place(second))
-    half = shot_count // 2 * TILES_DEV
-    return jnp.bitwise_and(apart, 1) * half + index * TILES_DEV + jnp.bitwise_and(tile, TILES_DEV - 1)
-
-
-def bin_kernel(chunks, shot_count, freq_count, load, tiles, x_ref, w_ref, t_hbm, *refs):
+    second = jnp.bitwise_and(owner, 1) == 1
+    count = len(steps[0])
+    base = jnp.bitwise_and(apart, 1) << count
+    for axis, bit in steps[0]:
+        if axis == "shot":
+            flag = jnp.bitwise_and(jnp.right_shift(apart, bit), 1)
+            places = [count - 1 - order.index((axis, bit)) for order in steps]
+            base += jnp.where(second, flag << places[1], flag << places[0])
+    slots = []
+    for far in range(freq_count):
+        places = [
+            sum((far >> bit & 1) << (count - 1 - i) for i, (axis, bit) in enumerate(order) if axis == "freq")
+            for order in steps
+        ]
+        slots.append((base + jnp.where(second, places[1], places[0])) * TILES_DEV + tile % TILES_DEV)
+    return slots
+
+
+def bin_kernel(chunks, steps, freq_count, load, tiles_hbm, x_ref, w_ref, t_hbm, *refs):
     outs, refs = refs[: len(chunks)], refs[len(chunks) :]
     if load:
         x_hbm, w_hbm, xbuf, wbuf = x_ref, w_ref, refs[0], refs[1]
         refs = refs[2:]
     else:
         xbuf, wbuf = x_ref, w_ref
-    tbuf, table, spectra, xsem, wsem, tsem = refs
+    tiles, tbuf, table, spectra, tilesem, xsem, wsem, tsem = refs
     shots_here, blocks_here, block_len, tile_len = wbuf.shape
     me_shot, me_freq = lax.axis_index("shot"), lax.axis_index("freq")
     rows = t_hbm.shape[2]
@@ -117,6 +124,8 @@
     def t_copy(i):
         return pltpu.make_async_copy(t_hbm.at[:, jnp.bitwise_xor(me_freq, i)], tbuf.at[:, i], tsem.at[i])
 
+    tile_copy = pltpu.make_async_copy(tiles_hbm, tiles, tilesem)
+    tile_copy.start()
     for i in range(freq_count):
         t_copy(i).start()
     if load:
@@ -126,6 +135,7 @@
             x_copy(i).start()
     for out in outs:
         out[...] = jnp.zeros_like(out)
+    tile_copy.wait()
     for i in range(freq_count):
         t_copy(i).wait()
     for n in range(len(groups)):
@@ -156,11 +166,12 @@
         )
         both = jnp.dot(jnp.concatenate([s_high, s_low], axis=1), weights, preferred_element_type=jnp.float32)
         value = both[:, :tile_len] + both[:, tile_len:]
-        slot = slot_of(tiles[i, me_freq * blocks_here + b], me_shot, shot_count)
+        tile = tiles[i, me_freq * blocks_here + b]
         start = 0
-        for out in outs:
-            out[slot] += value[start : start + out.shape[1]]
-            start += out.shape[1]
+        for out, orders in zip(outs, steps):
+            for slot in slots_of(tile, me_shot, orders, freq_count):
+                out[slot] += value[start : start + out.shape[1]]
+                start += out.shape[1]
 
     for i in range(shots_here + 1):
         folded = ()
@@ -179,25 +190,27 @@
                 spread(i - 1, k)
 
 
-def bin_blocks(tile_ids, traces, interp_weights, chunks, shot_count, freq_count, load, keep):
+def bin_blocks(tile_ids, traces, interp_weights, chunks, steps, shot_count, freq_count, load, keep):
     shots_here, recs_here, time_len = traces.shape
     block_len, tile_len = interp_weights.shape[2:]
     blocks_here = recs_here // block_len
     groups = [g for chunk in chunks for g in chunk]
     tables = jnp.asarray(dft_tables(groups, freq_count, time_len))
     rows = freq_count * tables.shape[2]
-    slot_count = shot_count * TILES_DEV
+    slot_count = shot_count * freq_count * TILES_DEV
     kept = [
         jax.ShapeDtypeStruct(traces.shape, jnp.float32),
         jax.ShapeDtypeStruct((shots_here, blocks_here, block_len, tile_len), jnp.float32),
     ]
-    total = slot_count * len(GROUPS) * rows * tile_len * 4
+    total = slot_count * len(GROUPS) * tables.shape[2] * tile_len * 4
     sums = pltpu.VMEM if total <= VMEM_SUMS else jax.ShapeDtypeStruct
-    out_shape = [sums((slot_count, rows * len(chunk), tile_len), jnp.float32) for chunk in chunks]
+    out_shape = [sums((slot_count, tables.shape[2] * len(chunk), tile_len), jnp.float32) for chunk in chunks]
     scratch = [
+        pltpu.SMEM(tile_ids.shape, jnp.int32),
         pltpu.VMEM(tables.shape, jnp.float32),
         pltpu.VMEM((len(groups), 2 * rows, tables.shape[3]), jnp.bfloat16),
         pltpu.VMEM((2, len(groups) * rows, recs_here), jnp.float32),
+        pltpu.SemaphoreType.DMA,
         pltpu.SemaphoreType.DMA((shots_here,)),
         pltpu.SemaphoreType.DMA((shots_here,)),
         pltpu.SemaphoreType.DMA((freq_count,)),
@@ -209,15 +222,16 @@
     place = pltpu.HBM if load else pltpu.VMEM
 
     def body(*refs):
-        bin_kernel(chunks, shot_count, freq_count, load, *refs)
-
+        bin_kernel(chunks, steps, freq_count, load, *refs)
+
+    tile_ids = pltpu.with_memory_space_constraint(tile_ids, pltpu.HBM)
     traces = pltpu.with_memory_space_constraint(traces, place)
     interp_weights = pltpu.with_memory_space_constraint(interp_weights, place)
     tables = pltpu.with_memory_space_constraint(tables, pltpu.HBM)
     return pl.pallas_call(
         body,
         in_specs=[
-            pl.BlockSpec(memory_space=pltpu.SMEM),
+            pl.BlockSpec(memory_space=pltpu.HBM),
             pl.BlockSpec(memory_space=place),
             pl.BlockSpec(memory_space=place),
             pl.BlockSpec(memory_space=pltpu.HBM),
@@ -234,56 +248,40 @@
     shot_count = lax.axis_size("shot")
     freq_count = lax.axis_size("freq")
     tile_len = interp_weights.shape[3]
-    levels = bit_orders(shot_count)
-
-    def to_core(value):
+    steps = halvings(shot_count, freq_count)
+
+    def halve(value, ways):
+        pairs = []
+        for shot in range(shot_count):
+            for freq in range(freq_count):
+                axis, bit = ways[shot & 1]
+                to = (shot ^ (1 << bit), freq) if axis == "shot" else (shot, freq ^ (1 << bit))
+                pairs.append((shot * freq_count + freq, to[0] * freq_count + to[1]))
         half = value.shape[0] // 2
-        got = lax.ppermute(value[half:], "shot", [(i, i ^ 1) for i in range(shot_count)])
-        return value[:half] + got
-
-    def to_shot(value, level):
-        half = value.shape[0] // 2
-        pairs = [(i, i ^ (1 << levels[i & 1][level])) for i in range(shot_count)]
-        return value[:half] + lax.ppermute(value[half:], "shot", pairs)
-
-    def to_freq(value, flip):
-        value = value.reshape(value.shape[0], -1, 2, value.shape[2], tile_len)
-        got = lax.ppermute(value[:, :, 1], "freq", [(i, i ^ flip) for i in range(freq_count)])
-        return value[:, :, 0] + got
-
-    def to_freq_direct(value):
-        total = value[:, 0]
-        for flip in range(freq_count - 1, 0, -1):
-            total += lax.ppermute(value[:, flip], "freq", [(i, i ^ flip) for i in range(freq_count)])
-        return total[:, None]
+        return value[:half] + lax.ppermute(value[half:], ("shot", "freq"), pairs)
 
     sums = [None] * len(CHUNKS)
     for n, call in enumerate(CALLS):
         chunks = tuple(CHUNKS[c] for c in call)
         made = bin_blocks(
-            tile_ids, traces, interp_weights, chunks, shot_count, freq_count, n == 0, n == 0 and len(CALLS) > 1
+            tile_ids,
+            traces,
+            interp_weights,
+            chunks,
+            [steps[c] for c in call],
+            shot_count,
+            freq_count,
+            n == 0,
+            n == 0 and len(CALLS) > 1,
         )
         for c, value in zip(call, made):
             sums[c] = value
         if len(made) > len(call):
             traces, interp_weights = made[len(call) :]
     parts = [None] * len(GROUPS)
-    for chunk, order, value in zip(CHUNKS, ORDERS, sums):
-        value = value.reshape(value.shape[0], freq_count, -1, tile_len)
-        level, flip = 0, 1
-        for stage in order:
-            if stage == "c":
-                value = to_core(value)
-            elif stage == "s":
-                for level in range(len(levels[0])):
-                    value = to_shot(value, level)
-            elif stage == "d":
-                value = to_freq_direct(value)
-            else:
-                flip = 1
-                while flip < freq_count:
-                    value = to_freq(value, flip)
-                    flip *= 2
+    for chunk, orders, value in zip(CHUNKS, steps, sums):
+        for ways in [(("shot", 0), ("shot", 0)), *zip(*orders)]:
+            value = halve(value, ways)
         value = value.reshape(TILES_DEV, len(chunk), -1, tile_len)
         for j, g in enumerate(chunk):
             parts[g] = value[:, j]

time: 60.8 us -> 52.1 us (0.86)
  the two profiles are of different devices: /device:TPU:0 before, /device:TPU:1 now
where the time goes in v3:
time: 52.1 us; the launch traced here: 52 us
  waiting for transfers between devices  22.6 us (43%)
  starting transfers between devices  16.8 us (32%)
  Pallas kernels  9.95 us (19%)
  local copies, waits for them, and re-layouts  1.64 us (3%)
  other arithmetic  0.79 us (2%)
    ppermute x10, waiting for transfers between devices, halve(): return value[:half] + lax.ppermute(value[half:], ('shot', 'freq'), pairs)  22.6 us
    ppermute x10, starting transfers between devices, halve(): return value[:half] + lax.ppermute(value[half:], ('shot', 'freq'), pairs)  16.8 us
    pallas_call x2, Pallas kernels, bin_blocks(): pl.pallas_call(body, in_specs=[pl.BlockSpec(memory_space=pltpu.HBM), pl.B...  9.95 us
    another operation x3, local copies, waits for them, and re-layouts, shards(): jnp.stack([eighths[r] for r in range(8)], axis=3)  1.06 us
  transfers between devices with their start and end apart: 10, of which 7 were waited for; matrix products, arithmetic and copies ran while one was open for 2% of the time, Pallas kernels for 8%

profile of v3, /device:TPU:1, one launch (start us, length us, event | category | flops | bytes accessed | tf_op | source)
XLA Modules:
  0.0 52.0 jit_solution(2864932080090746470)
XLA Ops:
  0.0 5.9 %bin_blocks.2 = (f32[64,96,128]{2,1,0:T(8,128)S(1)}, f32[4,512,1024]{2,1,0:T(8,128)S(1)}, f32[4,4,128,128]{3,2,1,0:T(8,128)S(1)}) custom-call(s32[4,16]{1,0:T(4,128)} %refs_0_.3, f32[4,512,1024]{2,1,0:T(8,128)} %refs_1_.1, f32[4,16,128,128]{3,2,1,0:T(8,128)} %refs_2_.1, f32[2,4,48,256]{3,2,1,0:T(8,128)} %constant.4.clone.refs_3_), custom_call_target="tpu_custom_call" | custom-call | tf_op jit(solution)/shard_map/bin_blocks/pallas_call | solution.py:231
  5.9 0.1 slice.97
  6.0 0.1 collective-permute-start
  6.1 4.0 %bin_blocks.3 = f32[64,96,128]{2,1,0:T(8,128)S(1)} custom-call(s32[4,16]{1,0:T(4,128)} %refs_0_.3, f32[4,512,1024]{2,1,0:T(8,128)S(1)} %get-tuple-element.9.refs_1_, f32[4,4,128,128]{3,2,1,0:T(8,128)S(1)} %get-tuple-element.10.refs_2_, f32[2,4,48,256]{3,2,1,0:T(8,128)} %constant.5.clone.refs_3_), custom_call_target="tpu_custom_call" | custom-call | tf_op jit(solution)/shard_map/bin_blocks/pallas_call | solution.py:231
  10.2 0.1 slice.139
  10.3 0.5 %collective-permute-start.5 = (f32[32,96,128]{2,1,0:T(8,128)S(1)}, f32[32,96,128]{2,1,0:T(8,128)S(1)}, u32[]{:S(2)}, u32[]{:S(2)}) collective-permute-start(f32[32,96,128]{2,1,0:T(8,128)S(1)} %slice.139), channel_id=1, source_target_pairs={{0,4},{1,5},{2,6},{3,7},{4,0},{5,1},{6,2},{7,3},{8,12},{9,13},{10,... | collective-permute-start | bytes 4718600 | tf_op jit(solution)/shard_map/ppermute | solution.py:261
  10.8 0.0 collective-permute-done
  10.8 0.2 slice_add_fusion.1
  11.0 0.1 slice.129
  11.1 2.3 %collective-permute-start.1 = (f32[16,96,128]{2,1,0:T(8,128)S(1)}, f32[16,96,128]{2,1,0:T(8,128)S(1)}, u32[]{:S(2)}, u32[]{:S(2)}) collective-permute-start(f32[16,96,128]{2,1,0:T(8,128)S(1)} %slice.129), channel_id=1, source_target_pairs={{0,1},{1,0},{2,3},{3,2},{4,20},{5,21},{6,22},{7,23},{8,9},{9,8},{1... | collective-permute-start | bytes 2359304 | tf_op jit(solution)/shard_map/ppermute | solution.py:261
  13.4 0.5 collective-permute-done.5
  13.9 0.2 slice_add_fusion
  14.1 0.1 slice.141
  14.2 2.7 %collective-permute-start.6 = (f32[16,96,128]{2,1,0:T(8,128)S(1)}, f32[16,96,128]{2,1,0:T(8,128)S(1)}, u32[]{:S(2)}, u32[]{:S(2)}) collective-permute-start(f32[16,96,128]{2,1,0:T(8,128)S(1)} %slice.141), channel_id=1, source_target_pairs={{0,8},{1,9},{2,10},{3,11},{4,20},{5,21},{6,22},{7,23},{8,0},{9,1},... | collective-permute-start | bytes 2359304 | tf_op jit(solution)/shard_map/ppermute | solution.py:261
  16.8 6.2 %collective-permute-done.1 = f32[16,96,128]{2,1,0:T(8,128)S(1)} collective-permute-done((f32[16,96,128]{2,1,0:T(8,128)S(1)}, f32[16,96,128]{2,1,0:T(8,128)S(1)}, u32[]{:S(2)}, u32[]{:S(2)}) %collective-permute-start.1) | collective-permute-done | bytes 786464 | tf_op jit(solution)/shard_map/ppermute | solution.py:261
  23.1 0.1 slice_add_fusion.3
  23.2 1.6 %collective-permute-start.2 = (f32[8,96,128]{2,1,0:T(8,128)S(1)}, f32[8,96,128]{2,1,0:T(8,128)S(1)}, u32[]{:S(2)}, u32[]{:S(2)}) collective-permute-start(f32[8,96,128]{2,1,0:T(8,128)S(1)} %slice.131), channel_id=1, source_target_pairs={{0,8},{1,9},{2,10},{3,11},{4,5},{5,4},{6,7},{7,6},{8,0},{9,1},{10,... | collective-permute-start | bytes 1179656 | tf_op jit(solution)/shard_map/ppermute | solution.py:261
  24.8 6.7 %collective-permute-done.6 = f32[16,96,128]{2,1,0:T(8,128)S(1)} collective-permute-done((f32[16,96,128]{2,1,0:T(8,128)S(1)}, f32[16,96,128]{2,1,0:T(8,128)S(1)}, u32[]{:S(2)}, u32[]{:S(2)}) %collective-permute-start.6) | collective-permute-done | bytes 786464 | tf_op jit(solution)/shard_map/ppermute | solution.py:261
  31.5 0.1 slice_add_fusion.2
  31.6 1.6 %collective-permute-start.7 = (f32[8,96,128]{2,1,0:T(8,128)S(1)}, f32[8,96,128]{2,1,0:T(8,128)S(1)}, u32[]{:S(2)}, u32[]{:S(2)}) collective-permute-start(f32[8,96,128]{2,1,0:T(8,128)S(1)} %slice.143), channel_id=1, source_target_pairs={{0,1},{1,0},{2,3},{3,2},{4,5},{5,4},{6,7},{7,6},{8,9},{9,8},{10,11... | collective-permute-start | bytes 1179656 | tf_op jit(solution)/shard_map/ppermute | solution.py:261
  33.2 0.0 collective-permute-done.2
  33.3 1.3 %collective-permute-start.3 = (f32[4,96,128]{2,1,0:T(8,128)S(1)}, f32[4,96,128]{2,1,0:T(8,128)S(1)}, u32[]{:S(2)}, u32[]{:S(2)}) collective-permute-start(f32[4,96,128]{2,1,0:T(8,128)S(1)} %slice.133), channel_id=1, source_target_pairs={{0,16},{1,17},{2,18},{3,19},{4,12},{5,13},{6,14},{7,15},{8,24},{9,... | collective-permute-start | bytes 589832 | tf_op jit(solution)/shard_map/ppermute | solution.py:261
  34.6 4.2 %collective-permute-done.7 = f32[8,96,128]{2,1,0:T(8,128)S(1)} collective-permute-done((f32[8,96,128]{2,1,0:T(8,128)S(1)}, f32[8,96,128]{2,1,0:T(8,128)S(1)}, u32[]{:S(2)}, u32[]{:S(2)}) %collective-permute-start.7) | collective-permute-done | bytes 393248 | tf_op jit(solution)/shard_map/ppermute | solution.py:261
  38.8 0.1 slice_add_fusion.4
  38.9 1.7 %collective-permute-start.8 = (f32[4,96,128]{2,1,0:T(8,128)S(1)}, f32[4,96,128]{2,1,0:T(8,128)S(1)}, u32[]{:S(2)}, u32[]{:S(2)}) collective-permute-start(f32[4,96,128]{2,1,0:T(8,128)S(1)} %slice.145), channel_id=1, source_target_pairs={{0,16},{1,17},{2,18},{3,19},{4,12},{5,13},{6,14},{7,15},{8,24},{9,... | collective-permute-start | bytes 589832 | tf_op jit(solution)/shard_map/ppermute | solution.py:261
  40.6 0.0 collective-permute-done.3
  40.6 2.4 %collective-permute-start.4 = (f32[2,96,128]{2,1,0:T(8,128)S(1)}, f32[2,96,128]{2,1,0:T(8,128)S(1)}, u32[]{:S(2)}, u32[]{:S(2)}) collective-permute-start(f32[2,96,128]{2,1,0:T(8,128)S(1)} %slice.135), channel_id=1, source_target_pairs={{0,2},{1,3},{2,0},{3,1},{4,6},{5,7},{6,4},{7,5},{8,10},{9,11},{10,... | collective-permute-start | bytes 294920 | tf_op jit(solution)/shard_map/ppermute | solution.py:261
  43.0 0.7 %collective-permute-done.8 = f32[4,96,128]{2,1,0:T(8,128)S(1)} collective-permute-done((f32[4,96,128]{2,1,0:T(8,128)S(1)}, f32[4,96,128]{2,1,0:T(8,128)S(1)}, u32[]{:S(2)}, u32[]{:S(2)}) %collective-permute-start.8) | collective-permute-done | bytes 196640 | tf_op jit(solution)/shard_map/ppermute | solution.py:261
  43.7 2.6 %collective-permute-start.9 = (f32[2,96,128]{2,1,0:T(8,128)S(1)}, f32[2,96,128]{2,1,0:T(8,128)S(1)}, u32[]{:S(2)}, u32[]{:S(2)}) collective-permute-start(f32[2,96,128]{2,1,0:T(8,128)S(1)} %slice.147), channel_id=1, source_target_pairs={{0,2},{1,3},{2,0},{3,1},{4,6},{5,7},{6,4},{7,5},{8,10},{9,11},{10,... | collective-permute-start | bytes 294920 | tf_op jit(solution)/shard_map/ppermute | solution.py:261
  46.3 0.7 %collective-permute-done.4 = f32[2,96,128]{2,1,0:T(8,128)S(1)} collective-permute-done((f32[2,96,128]{2,1,0:T(8,128)S(1)}, f32[2,96,128]{2,1,0:T(8,128)S(1)}, u32[]{:S(2)}, u32[]{:S(2)}) %collective-permute-start.4) | collective-permute-done | bytes 98336 | tf_op jit(solution)/shard_map/ppermute | solution.py:261
  47.0 3.7 %collective-permute-done.9 = f32[2,96,128]{2,1,0:T(8,128)S(1)} collective-permute-done((f32[2,96,128]{2,1,0:T(8,128)S(1)}, f32[2,96,128]{2,1,0:T(8,128)S(1)}, u32[]{:S(2)}, u32[]{:S(2)}) %collective-permute-start.9) | collective-permute-done | bytes 98336 | tf_op jit(solution)/shard_map/ppermute | solution.py:261
  50.8 0.1 fusion.3
  50.9 0.1 copy_bitcast_fusion.1
  51.0 0.1 copy_bitcast_fusion
  51.0 1.0 %stack.3 = f32[2,2,12,8,128]{4,3,2,1,0:T(8,128)} concatenate(f32[2,2,12,1,128]{4,3,2,1,0:T(1,128)S(1)} %get-tuple-element.27, f32[2,2,12,1,128]{4,3,2,1,0:T(1,128)S(1)} %get-tuple-element.24, f32[2,2,12,1,128]{4,3,2,1,0:T(1,128)S(1)} %get-tuple-element.18, f32[2,2,12,1,128]{4,3,2,1,0:T(1,128)S(1)} %get-tuple-element.26, f32[2,2,12,1,128]{4,3,2,1,0:T(1,128)S(1)} %get-tuple-element.28, ...), dimensions={3} | concatenate | bytes 393216 | tf_op jit(solution)/shard_map/stack | solution.py:298
  (17 shorter events, 0.3 us)
Async XLA Ops:
  6.0 4.8 %collective-permute-start = (f32[32,96,128]{2,1,0:T(8,128)S(1)}, f32[32,96,128]{2,1,0:T(8,128)S(1)}, u32[]{:S(2)}, u32[]{:S(2)}) collective-permute-start(f32[32,96,128]{2,1,0:T(8,128)S(1)} %slice.97), channel_id=1, source_target_pairs={{0,4},{1,5},{2,6},{3,7},{4,0},{5,1},{6,2},{7,3},{8,12},{9,13},{10,... | collective-permute-start | bytes 4718600 | tf_op jit(solution)/shard_map/ppermute | solution.py:261
  10.3 3.6 %collective-permute-start.5 = (f32[32,96,128]{2,1,0:T(8,128)S(1)}, f32[32,96,128]{2,1,0:T(8,128)S(1)}, u32[]{:S(2)}, u32[]{:S(2)}) collective-permute-start(f32[32,96,128]{2,1,0:T(8,128)S(1)} %slice.139), channel_id=1, source_target_pairs={{0,4},{1,5},{2,6},{3,7},{4,0},{5,1},{6,2},{7,3},{8,12},{9,13},{10,... | collective-permute-start | bytes 4718600 | tf_op jit(solution)/shard_map/ppermute | solution.py:261
  11.1 12.0 %collective-permute-start.1 = (f32[16,96,128]{2,1,0:T(8,128)S(1)}, f32[16,96,128]{2,1,0:T(8,128)S(1)}, u32[]{:S(2)}, u32[]{:S(2)}) collective-permute-start(f32[16,96,128]{2,1,0:T(8,128)S(1)} %slice.129), channel_id=1, source_target_pairs={{0,1},{1,0},{2,3},{3,2},{4,20},{5,21},{6,22},{7,23},{8,9},{9,8},{1... | collective-permute-start | bytes 2359304 | tf_op jit(solution)/shard_map/ppermute | solution.py:261
  14.2 17.3 %collective-permute-start.6 = (f32[16,96,128]{2,1,0:T(8,128)S(1)}, f32[16,96,128]{2,1,0:T(8,128)S(1)}, u32[]{:S(2)}, u32[]{:S(2)}) collective-permute-start(f32[16,96,128]{2,1,0:T(8,128)S(1)} %slice.141), channel_id=1, source_target_pairs={{0,8},{1,9},{2,10},{3,11},{4,20},{5,21},{6,22},{7,23},{8,0},{9,1},... | collective-permute-start | bytes 2359304 | tf_op jit(solution)/shard_map/ppermute | solution.py:261
  23.2 10.0 %collective-permute-start.2 = (f32[8,96,128]{2,1,0:T(8,128)S(1)}, f32[8,96,128]{2,1,0:T(8,128)S(1)}, u32[]{:S(2)}, u32[]{:S(2)}) collective-permute-start(f32[8,96,128]{2,1,0:T(8,128)S(1)} %slice.131), channel_id=1, source_target_pairs={{0,8},{1,9},{2,10},{3,11},{4,5},{5,4},{6,7},{7,6},{8,0},{9,1},{10,... | collective-permute-start | bytes 1179656 | tf_op jit(solution)/shard_map/ppermute | solution.py:261
  31.6 7.1 %collective-permute-start.7 = (f32[8,96,128]{2,1,0:T(8,128)S(1)}, f32[8,96,128]{2,1,0:T(8,128)S(1)}, u32[]{:S(2)}, u32[]{:S(2)}) collective-permute-start(f32[8,96,128]{2,1,0:T(8,128)S(1)} %slice.143), channel_id=1, source_target_pairs={{0,1},{1,0},{2,3},{3,2},{4,5},{5,4},{6,7},{7,6},{8,9},{9,8},{10,11... | collective-permute-start | bytes 1179656 | tf_op jit(solution)/shard_map/ppermute | solution.py:261
  33.3 7.3 %collective-permute-start.3 = (f32[4,96,128]{2,1,0:T(8,128)S(1)}, f32[4,96,128]{2,1,0:T(8,128)S(1)}, u32[]{:S(2)}, u32[]{:S(2)}) collective-permute-start(f32[4,96,128]{2,1,0:T(8,128)S(1)} %slice.133), channel_id=1, source_target_pairs={{0,16},{1,17},{2,18},{3,19},{4,12},{5,13},{6,14},{7,15},{8,24},{9,... | collective-permute-start | bytes 589832 | tf_op jit(solution)/shard_map/ppermute | solution.py:261
  38.9 4.8 %collective-permute-start.8 = (f32[4,96,128]{2,1,0:T(8,128)S(1)}, f32[4,96,128]{2,1,0:T(8,128)S(1)}, u32[]{:S(2)}, u32[]{:S(2)}) collective-permute-start(f32[4,96,128]{2,1,0:T(8,128)S(1)} %slice.145), channel_id=1, source_target_pairs={{0,16},{1,17},{2,18},{3,19},{4,12},{5,13},{6,14},{7,15},{8,24},{9,... | collective-permute-start | bytes 589832 | tf_op jit(solution)/shard_map/ppermute | solution.py:261
  40.6 6.4 %collective-permute-start.4 = (f32[2,96,128]{2,1,0:T(8,128)S(1)}, f32[2,96,128]{2,1,0:T(8,128)S(1)}, u32[]{:S(2)}, u32[]{:S(2)}) collective-permute-start(f32[2,96,128]{2,1,0:T(8,128)S(1)} %slice.135), channel_id=1, source_target_pairs={{0,2},{1,3},{2,0},{3,1},{4,6},{5,7},{6,4},{7,5},{8,10},{9,11},{10,... | collective-permute-start | bytes 294920 | tf_op jit(solution)/shard_map/ppermute | solution.py:261
  43.7 7.0 %collective-permute-start.9 = (f32[2,96,128]{2,1,0:T(8,128)S(1)}, f32[2,96,128]{2,1,0:T(8,128)S(1)}, u32[]{:S(2)}, u32[]{:S(2)}) collective-permute-start(f32[2,96,128]{2,1,0:T(8,128)S(1)} %slice.147), channel_id=1, source_target_pairs={{0,2},{1,3},{2,0},{3,1},{4,6},{5,7},{6,4},{7,5},{8,10},{9,11},{10,... | collective-permute-start | bytes 294920 | tf_op jit(solution)/shard_map/ppermute | solution.py:261

commit v4 on v3

--- a/solution.py
+++ b/solution.py
@@ -97,7 +97,7 @@
     return slots
 
 
-def bin_kernel(chunks, steps, freq_count, load, tiles_hbm, x_ref, w_ref, t_hbm, *refs):
+def bin_kernel(chunks, steps, freq_count, load, tiles_hbm, x_ref, w_ref, t_ref, *refs):
     outs, refs = refs[: len(chunks)], refs[len(chunks) :]
     if load:
         x_hbm, w_hbm, xbuf, wbuf = x_ref, w_ref, refs[0], refs[1]
@@ -107,7 +107,7 @@
     tiles, tbuf, table, spectra, tilesem, xsem, wsem, tsem = refs
     shots_here, blocks_here, block_len, tile_len = wbuf.shape
     me_shot, me_freq = lax.axis_index("shot"), lax.axis_index("freq")
-    rows = t_hbm.shape[2]
+    rows = t_ref.shape[2]
     groups = [g for chunk in chunks for g in chunk]
     place, stride, start = {}, {}, 0
     for chunk in chunks:
@@ -122,24 +122,27 @@
         return pltpu.make_async_copy(w_hbm.at[i, pl.ds(me_freq * blocks_here, blocks_here)], wbuf.at[i], wsem.at[i])
 
     def t_copy(i):
-        return pltpu.make_async_copy(t_hbm.at[:, jnp.bitwise_xor(me_freq, i)], tbuf.at[:, i], tsem.at[i])
+        return pltpu.make_async_copy(t_ref.at[:, jnp.bitwise_xor(me_freq, i)], tbuf.at[:, i], tsem.at[i])
+
+    def near_table(n, i):
+        return tbuf[n, i] if load else t_ref[n, jnp.bitwise_xor(me_freq, i)]
 
     tile_copy = pltpu.make_async_copy(tiles_hbm, tiles, tilesem)
     tile_copy.start()
-    for i in range(freq_count):
-        t_copy(i).start()
     if load:
+        for i in range(freq_count):
+            t_copy(i).start()
         x_copy(0).start()
         w_copy(0).start()
         for i in range(1, DEPTH):
             x_copy(i).start()
     for out in outs:
         out[...] = jnp.zeros_like(out)
-    tile_copy.wait()
-    for i in range(freq_count):
-        t_copy(i).wait()
+    if load:
+        for i in range(freq_count):
+            t_copy(i).wait()
     for n in range(len(groups)):
-        high, low = split(jnp.concatenate([tbuf[n, i] for i in range(freq_count)], axis=0))
+        high, low = split(jnp.concatenate([near_table(n, i) for i in range(freq_count)], axis=0))
         table[n] = jnp.concatenate([high, low], axis=0)
 
     def transform(i, n, part):
@@ -155,6 +158,8 @@
     def spread(i, b):
         if load and b == 0:
             w_copy(i).wait()
+        if i == 0 and b == 0:
+            tile_copy.wait()
         s_high, s_low = split(spectra[i % 2, :, b * block_len : (b + 1) * block_len])
         w_high, w_low = split(wbuf[i, b])
         weights = jnp.concatenate(
@@ -227,14 +232,14 @@
     tile_ids = pltpu.with_memory_space_constraint(tile_ids, pltpu.HBM)
     traces = pltpu.with_memory_space_constraint(traces, place)
     interp_weights = pltpu.with_memory_space_constraint(interp_weights, place)
-    tables = pltpu.with_memory_space_constraint(tables, pltpu.HBM)
+    tables = pltpu.with_memory_space_constraint(tables, place)
     return pl.pallas_call(
         body,
         in_specs=[
             pl.BlockSpec(memory_space=pltpu.HBM),
             pl.BlockSpec(memory_space=place),
             pl.BlockSpec(memory_space=place),
-            pl.BlockSpec(memory_space=pltpu.HBM),
+            pl.BlockSpec(memory_space=place),
         ],
         out_specs=[pl.BlockSpec(memory_space=pltpu.VMEM)] * len(out_shape),
         out_shape=out_shape,
@@ -242,6 +247,35 @@
         compiler_params=pltpu.CompilerParams(vmem_limit_bytes=VMEM_LIMIT),
         name="bin_blocks",
     )(tile_ids, traces, interp_weights, tables)
+
+
+def assemble_kernel(*refs):
+    out = refs[-1]
+    freq_here = out.shape[2]
+    for n, chunk in enumerate(CHUNKS):
+        rows = refs[2 * n].shape[1] // len(chunk)
+        for tile in range(TILES_DEV):
+            value = refs[2 * n][tile] + refs[2 * n + 1][tile]
+            for j, g in enumerate(chunk):
+                stride = 4 if GROUPS[g][0] % 2 == 0 else 8
+                residues = GROUPS[g][:1] if stride == 4 else GROUPS[g]
+                size = freq_here // stride
+                start = j * rows
+                for residue in residues:
+                    for part in range(2):
+                        out[tile, part, pl.ds(residue, size, stride)] = value[start : start + size]
+                        start += size
+
+
+def assemble(last, freq_here, tile_len):
+    last = [pltpu.with_memory_space_constraint(value, pltpu.VMEM) for value in last]
+    return pl.pallas_call(
+        assemble_kernel,
+        in_specs=[pl.BlockSpec(memory_space=pltpu.VMEM)] * len(last),
+        out_specs=pl.BlockSpec(memory_space=pltpu.VMEM),
+        out_shape=jax.ShapeDtypeStruct((TILES_DEV, 2, freq_here, tile_len), jnp.float32),
+        name="assemble",
+    )(*last)
 
 
 def shards(traces, interp_weights, tile_ids):
@@ -258,7 +292,7 @@
                 to = (shot ^ (1 << bit), freq) if axis == "shot" else (shot, freq ^ (1 << bit))
                 pairs.append((shot * freq_count + freq, to[0] * freq_count + to[1]))
         half = value.shape[0] // 2
-        return value[:half] + lax.ppermute(value[half:], ("shot", "freq"), pairs)
+        return value[:half], lax.ppermute(value[half:], ("shot", "freq"), pairs)
 
     sums = [None] * len(CHUNKS)
     for n, call in enumerate(CALLS):
@@ -278,24 +312,13 @@
             sums[c] = value
         if len(made) > len(call):
             traces, interp_weights = made[len(call) :]
-    parts = [None] * len(GROUPS)
-    for chunk, orders, value in zip(CHUNKS, steps, sums):
+    last = []
+    for orders, value in zip(steps, sums):
         for ways in [(("shot", 0), ("shot", 0)), *zip(*orders)]:
-            value = halve(value, ways)
-        value = value.reshape(TILES_DEV, len(chunk), -1, tile_len)
-        for j, g in enumerate(chunk):
-            parts[g] = value[:, j]
-    eighths = {}
-    for g, residues in enumerate(GROUPS):
-        if residues[0] % 2 == 0:
-            part = parts[g].reshape(TILES_DEV, 2, -1, 2, tile_len)
-            for j, residue in enumerate(residues):
-                eighths[residue] = part[:, :, :, j]
-        else:
-            part = parts[g].reshape(TILES_DEV, 2, 2, -1, tile_len)
-            for j, residue in enumerate(residues):
-                eighths[residue] = part[:, j]
-    return jnp.stack([eighths[r] for r in range(8)], axis=3).reshape(TILES_DEV, 2, -1, tile_len)
+            kept, got = halve(value, ways)
+            value = kept + got
+        last += [kept, got]
+    return assemble(last, NF // freq_count, tile_len)
 
 
 def solution(mesh):

time: 52.1 us -> 51.3 us (0.985)
    another operation x3 -> x0, local copies, waits for them, and re-layouts: 1.06 us -> none  [shards(): jnp.stack([eighths[r] for r in range(8)], axis=3)]
    pallas_call x2, Pallas kernels: 9.95 us -> 8.96 us  [bin_blocks(): pl.pallas_call(body, in_specs=[pl.BlockSpec(memory_space=pltpu.HBM), pl.B...]
    pallas_call x0 -> x1, Pallas kernels: none -> 0.71 us  [assemble(): pl.pallas_call(assemble_kernel, in_specs=[pl.BlockSpec(memory_space=pltpu...]
    unnamed x2, local copies, waits for them, and re-layouts: 0.05 us -> 0.76 us
  transfers between devices with their start and end apart: 10 -> 10, of which waited for: 7 -> 6; matrix products, arithmetic and copies ran while one was open for 2% -> 2% of each run, Pallas kernels for 8% -> 6%
where the time goes in v4:
time: 51.3 us; the launch traced here: 51 us
  waiting for transfers between devices  22.7 us (44%)
  starting transfers between devices  16.6 us (32%)
  Pallas kernels  9.67 us (19%)
  local copies, waits for them, and re-layouts  1.19 us (2%)
  other arithmetic  0.76 us (1%)
    ppermute x10, waiting for transfers between devices, halve(): return (value[:half], lax.ppermute(value[half:], ('shot', 'freq'), pairs))  22.7 us
    ppermute x10, starting transfers between devices, halve(): return (value[:half], lax.ppermute(value[half:], ('shot', 'freq'), pairs))  16.6 us
    pallas_call x2, Pallas kernels, bin_blocks(): pl.pallas_call(body, in_specs=[pl.BlockSpec(memory_space=pltpu.HBM), pl.B...  8.96 us
  transfers between devices with their start and end apart: 10, of which 6 were waited for; matrix products, arithmetic and copies ran while one was open for 2% of the time, Pallas kernels for 6%

profile of v4, /device:TPU:1, one launch (start us, length us, event | category | flops | bytes accessed | tf_op | source)
XLA Modules:
  0.0 51.0 jit_solution(6969480488603923522)
XLA Ops:
  0.0 5.9 %bin_blocks.2 = (f32[64,96,128]{2,1,0:T(8,128)S(1)}, f32[4,512,1024]{2,1,0:T(8,128)S(1)}, f32[4,4,128,128]{3,2,1,0:T(8,128)S(1)}) custom-call(s32[4,16]{1,0:T(4,128)} %refs_0_.3, f32[4,512,1024]{2,1,0:T(8,128)} %refs_1_.1, f32[4,16,128,128]{3,2,1,0:T(8,128)} %refs_2_.1, f32[2,4,48,256]{3,2,1,0:T(8,128)} %constant.4.clone.refs_3_), custom_call_target="tpu_custom_call" | custom-call | tf_op jit(solution)/shard_map/bin_blocks/pallas_call | solution.py:236
  5.9 0.0 copy-start
  5.9 0.1 slice.61
  6.0 0.1 collective-permute-start
  6.2 0.8 %copy-done = f32[2,4,48,256]{3,2,1,0:T(8,128)S(1)} copy-done((f32[2,4,48,256]{3,2,1,0:T(8,128)S(1)}, f32[2,4,48,256]{3,2,1,0:T(8,128)}, u32[]{:S(2)}) %copy-start) | copy-done | bytes 393240
  6.9 3.0 %bin_blocks.3 = f32[64,96,128]{2,1,0:T(8,128)S(1)} custom-call(s32[4,16]{1,0:T(4,128)} %refs_0_.3, f32[4,512,1024]{2,1,0:T(8,128)S(1)} %get-tuple-element.9.refs_1_, f32[4,4,128,128]{3,2,1,0:T(8,128)S(1)} %get-tuple-element.10.refs_2_, f32[2,4,48,256]{3,2,1,0:T(8,128)S(1)} %copy-done), custom_call_target="tpu_custom_call" | custom-call | tf_op jit(solution)/shard_map/bin_blocks/pallas_call | solution.py:236
  10.0 0.1 slice.89
  10.1 0.1 collective-permute-start.5
  10.2 0.0 collective-permute-done
  10.2 0.2 slice_add_fusion.1
  10.4 0.1 slice.81
  10.5 2.8 %collective-permute-start.1 = (f32[16,96,128]{2,1,0:T(8,128)S(1)}, f32[16,96,128]{2,1,0:T(8,128)S(1)}, u32[]{:S(2)}, u32[]{:S(2)}) collective-permute-start(f32[16,96,128]{2,1,0:T(8,128)S(1)} %slice.81), channel_id=1, source_target_pairs={{0,1},{1,0},{2,3},{3,2},{4,20},{5,21},{6,22},{7,23},{8,9},{9,8},{1... | collective-permute-start | bytes 2359304 | tf_op jit(solution)/shard_map/ppermute | solution.py:295
  13.2 0.3 collective-permute-done.5
  13.6 0.2 slice_add_fusion
  13.8 0.1 slice.91
  13.9 2.4 %collective-permute-start.6 = (f32[16,96,128]{2,1,0:T(8,128)S(1)}, f32[16,96,128]{2,1,0:T(8,128)S(1)}, u32[]{:S(2)}, u32[]{:S(2)}) collective-permute-start(f32[16,96,128]{2,1,0:T(8,128)S(1)} %slice.91), channel_id=1, source_target_pairs={{0,8},{1,9},{2,10},{3,11},{4,20},{5,21},{6,22},{7,23},{8,0},{9,1},... | collective-permute-start | bytes 2359304 | tf_op jit(solution)/shard_map/ppermute | solution.py:295
  16.3 6.6 %collective-permute-done.1 = f32[16,96,128]{2,1,0:T(8,128)S(1)} collective-permute-done((f32[16,96,128]{2,1,0:T(8,128)S(1)}, f32[16,96,128]{2,1,0:T(8,128)S(1)}, u32[]{:S(2)}, u32[]{:S(2)}) %collective-permute-start.1) | collective-permute-done | bytes 786464 | tf_op jit(solution)/shard_map/ppermute | solution.py:295
  22.9 0.1 slice_add_fusion.3
  23.0 1.6 %collective-permute-start.2 = (f32[8,96,128]{2,1,0:T(8,128)S(1)}, f32[8,96,128]{2,1,0:T(8,128)S(1)}, u32[]{:S(2)}, u32[]{:S(2)}) collective-permute-start(f32[8,96,128]{2,1,0:T(8,128)S(1)} %slice.83), channel_id=1, source_target_pairs={{0,8},{1,9},{2,10},{3,11},{4,5},{5,4},{6,7},{7,6},{8,0},{9,1},{10,... | collective-permute-start | bytes 1179656 | tf_op jit(solution)/shard_map/ppermute | solution.py:295
  24.6 6.7 %collective-permute-done.6 = f32[16,96,128]{2,1,0:T(8,128)S(1)} collective-permute-done((f32[16,96,128]{2,1,0:T(8,128)S(1)}, f32[16,96,128]{2,1,0:T(8,128)S(1)}, u32[]{:S(2)}, u32[]{:S(2)}) %collective-permute-start.6) | collective-permute-done | bytes 786464 | tf_op jit(solution)/shard_map/ppermute | solution.py:295
  31.3 0.1 slice_add_fusion.2
  31.5 1.6 %collective-permute-start.7 = (f32[8,96,128]{2,1,0:T(8,128)S(1)}, f32[8,96,128]{2,1,0:T(8,128)S(1)}, u32[]{:S(2)}, u32[]{:S(2)}) collective-permute-start(f32[8,96,128]{2,1,0:T(8,128)S(1)} %slice.93), channel_id=1, source_target_pairs={{0,1},{1,0},{2,3},{3,2},{4,5},{5,4},{6,7},{7,6},{8,9},{9,8},{10,11... | collective-permute-start | bytes 1179656 | tf_op jit(solution)/shard_map/ppermute | solution.py:295
  33.0 0.0 collective-permute-done.2
  33.1 1.3 %collective-permute-start.3 = (f32[4,96,128]{2,1,0:T(8,128)S(1)}, f32[4,96,128]{2,1,0:T(8,128)S(1)}, u32[]{:S(2)}, u32[]{:S(2)}) collective-permute-start(f32[4,96,128]{2,1,0:T(8,128)S(1)} %slice.85), channel_id=1, source_target_pairs={{0,16},{1,17},{2,18},{3,19},{4,12},{5,13},{6,14},{7,15},{8,24},{9,... | collective-permute-start | bytes 589832 | tf_op jit(solution)/shard_map/ppermute | solution.py:295
  34.4 4.4 %collective-permute-done.7 = f32[8,96,128]{2,1,0:T(8,128)S(1)} collective-permute-done((f32[8,96,128]{2,1,0:T(8,128)S(1)}, f32[8,96,128]{2,1,0:T(8,128)S(1)}, u32[]{:S(2)}, u32[]{:S(2)}) %collective-permute-start.7) | collective-permute-done | bytes 393248 | tf_op jit(solution)/shard_map/ppermute | solution.py:295
  38.8 0.1 slice_add_fusion.4
  38.9 1.7 %collective-permute-start.8 = (f32[4,96,128]{2,1,0:T(8,128)S(1)}, f32[4,96,128]{2,1,0:T(8,128)S(1)}, u32[]{:S(2)}, u32[]{:S(2)}) collective-permute-start(f32[4,96,128]{2,1,0:T(8,128)S(1)} %slice.95), channel_id=1, source_target_pairs={{0,16},{1,17},{2,18},{3,19},{4,12},{5,13},{6,14},{7,15},{8,24},{9,... | collective-permute-start | bytes 589832 | tf_op jit(solution)/shard_map/ppermute | solution.py:295
  40.6 0.0 collective-permute-done.3
  40.6 2.4 %collective-permute-start.4 = (f32[2,96,128]{2,1,0:T(8,128)S(1)}, f32[2,96,128]{2,1,0:T(8,128)S(1)}, u32[]{:S(2)}, u32[]{:S(2)}) collective-permute-start(f32[2,96,128]{2,1,0:T(8,128)S(1)} %get-tuple-element.13), channel_id=1, source_target_pairs={{0,2},{1,3},{2,0},{3,1},{4,6},{5,7},{6,4},{7,5},{8,10},{9,11},{10,... | collective-permute-start | bytes 294920 | tf_op jit(solution)/shard_map/ppermute | solution.py:295
  43.0 0.6 %collective-permute-done.8 = f32[4,96,128]{2,1,0:T(8,128)S(1)} collective-permute-done((f32[4,96,128]{2,1,0:T(8,128)S(1)}, f32[4,96,128]{2,1,0:T(8,128)S(1)}, u32[]{:S(2)}, u32[]{:S(2)}) %collective-permute-start.8) | collective-permute-done | bytes 196640 | tf_op jit(solution)/shard_map/ppermute | solution.py:295
  43.7 2.6 %collective-permute-start.9 = (f32[2,96,128]{2,1,0:T(8,128)S(1)}, f32[2,96,128]{2,1,0:T(8,128)S(1)}, u32[]{:S(2)}, u32[]{:S(2)}) collective-permute-start(f32[2,96,128]{2,1,0:T(8,128)S(1)} %get-tuple-element.11), channel_id=1, source_target_pairs={{0,2},{1,3},{2,0},{3,1},{4,6},{5,7},{6,4},{7,5},{8,10},{9,11},{10,... | collective-permute-start | bytes 294920 | tf_op jit(solution)/shard_map/ppermute | solution.py:295
  46.3 0.0 collective-permute-done.4.refs_1_
  46.3 4.0 %collective-permute-done.9.refs_3_ = f32[2,96,128]{2,1,0:T(8,128)S(1)} collective-permute-done((f32[2,96,128]{2,1,0:T(8,128)S(1)}, f32[2,96,128]{2,1,0:T(8,128)S(1)}, u32[]{:S(2)}, u32[]{:S(2)}) %collective-permute-start.9) | collective-permute-done | bytes 98336 | tf_op jit(solution)/shard_map/ppermute | solution.py:295
  50.3 0.7 %assemble.1 = f32[2,2,96,128]{3,2,1,0:T(8,128)} custom-call(f32[2,96,128]{2,1,0:T(8,128)S(1)} %get-tuple-element.14.refs_0_, f32[2,96,128]{2,1,0:T(8,128)S(1)} %collective-permute-done.4.refs_1_, f32[2,96,128]{2,1,0:T(8,128)S(1)} %get-tuple-element.12.refs_2_, f32[2,96,128]{2,1,0:T(8,128)S(1)} %collective-permute-done.9.refs_3_), custom_call_target="tpu_custom_call" | custom-call | tf_op jit(solution)/shard_map/assemble/pallas_call | solution.py:272
  (9 shorter events, 0.2 us)
Async XLA Ops:
  5.9 1.0 %copy-start = (f32[2,4,48,256]{3,2,1,0:T(8,128)S(1)}, f32[2,4,48,256]{3,2,1,0:T(8,128)}, u32[]{:S(2)}) copy-start(f32[2,4,48,256]{3,2,1,0:T(8,128)} %constant.5.clone.refs_3_) | copy-start | bytes 1179652
  6.0 4.2 %collective-permute-start = (f32[32,96,128]{2,1,0:T(8,128)S(1)}, f32[32,96,128]{2,1,0:T(8,128)S(1)}, u32[]{:S(2)}, u32[]{:S(2)}) collective-permute-start(f32[32,96,128]{2,1,0:T(8,128)S(1)} %slice.61), channel_id=1, source_target_pairs={{0,4},{1,5},{2,6},{3,7},{4,0},{5,1},{6,2},{7,3},{8,12},{9,13},{10,... | collective-permute-start | bytes 4718600 | tf_op jit(solution)/shard_map/ppermute | solution.py:295
  10.1 3.5 %collective-permute-start.5 = (f32[32,96,128]{2,1,0:T(8,128)S(1)}, f32[32,96,128]{2,1,0:T(8,128)S(1)}, u32[]{:S(2)}, u32[]{:S(2)}) collective-permute-start(f32[32,96,128]{2,1,0:T(8,128)S(1)} %slice.89), channel_id=1, source_target_pairs={{0,4},{1,5},{2,6},{3,7},{4,0},{5,1},{6,2},{7,3},{8,12},{9,13},{10,... | collective-permute-start | bytes 4718600 | tf_op jit(solution)/shard_map/ppermute | solution.py:295
  10.5 12.4 %collective-permute-start.1 = (f32[16,96,128]{2,1,0:T(8,128)S(1)}, f32[16,96,128]{2,1,0:T(8,128)S(1)}, u32[]{:S(2)}, u32[]{:S(2)}) collective-permute-start(f32[16,96,128]{2,1,0:T(8,128)S(1)} %slice.81), channel_id=1, source_target_pairs={{0,1},{1,0},{2,3},{3,2},{4,20},{5,21},{6,22},{7,23},{8,9},{9,8},{1... | collective-permute-start | bytes 2359304 | tf_op jit(solution)/shard_map/ppermute | solution.py:295
  13.9 17.5 %collective-permute-start.6 = (f32[16,96,128]{2,1,0:T(8,128)S(1)}, f32[16,96,128]{2,1,0:T(8,128)S(1)}, u32[]{:S(2)}, u32[]{:S(2)}) collective-permute-start(f32[16,96,128]{2,1,0:T(8,128)S(1)} %slice.91), channel_id=1, source_target_pairs={{0,8},{1,9},{2,10},{3,11},{4,20},{5,21},{6,22},{7,23},{8,0},{9,1},... | collective-permute-start | bytes 2359304 | tf_op jit(solution)/shard_map/ppermute | solution.py:295
  23.0 10.0 %collective-permute-start.2 = (f32[8,96,128]{2,1,0:T(8,128)S(1)}, f32[8,96,128]{2,1,0:T(8,128)S(1)}, u32[]{:S(2)}, u32[]{:S(2)}) collective-permute-start(f32[8,96,128]{2,1,0:T(8,128)S(1)} %slice.83), channel_id=1, source_target_pairs={{0,8},{1,9},{2,10},{3,11},{4,5},{5,4},{6,7},{7,6},{8,0},{9,1},{10,... | collective-permute-start | bytes 1179656 | tf_op jit(solution)/shard_map/ppermute | solution.py:295
  31.5 7.3 %collective-permute-start.7 = (f32[8,96,128]{2,1,0:T(8,128)S(1)}, f32[8,96,128]{2,1,0:T(8,128)S(1)}, u32[]{:S(2)}, u32[]{:S(2)}) collective-permute-start(f32[8,96,128]{2,1,0:T(8,128)S(1)} %slice.93), channel_id=1, source_target_pairs={{0,1},{1,0},{2,3},{3,2},{4,5},{5,4},{6,7},{7,6},{8,9},{9,8},{10,11... | collective-permute-start | bytes 1179656 | tf_op jit(solution)/shard_map/ppermute | solution.py:295
  33.1 7.5 %collective-permute-start.3 = (f32[4,96,128]{2,1,0:T(8,128)S(1)}, f32[4,96,128]{2,1,0:T(8,128)S(1)}, u32[]{:S(2)}, u32[]{:S(2)}) collective-permute-start(f32[4,96,128]{2,1,0:T(8,128)S(1)} %slice.85), channel_id=1, source_target_pairs={{0,16},{1,17},{2,18},{3,19},{4,12},{5,13},{6,14},{7,15},{8,24},{9,... | collective-permute-start | bytes 589832 | tf_op jit(solution)/shard_map/ppermute | solution.py:295
  38.9 4.8 %collective-permute-start.8 = (f32[4,96,128]{2,1,0:T(8,128)S(1)}, f32[4,96,128]{2,1,0:T(8,128)S(1)}, u32[]{:S(2)}, u32[]{:S(2)}) collective-permute-start(f32[4,96,128]{2,1,0:T(8,128)S(1)} %slice.95), channel_id=1, source_target_pairs={{0,16},{1,17},{2,18},{3,19},{4,12},{5,13},{6,14},{7,15},{8,24},{9,... | collective-permute-start | bytes 589832 | tf_op jit(solution)/shard_map/ppermute | solution.py:295
  40.6 5.7 %collective-permute-start.4 = (f32[2,96,128]{2,1,0:T(8,128)S(1)}, f32[2,96,128]{2,1,0:T(8,128)S(1)}, u32[]{:S(2)}, u32[]{:S(2)}) collective-permute-start(f32[2,96,128]{2,1,0:T(8,128)S(1)} %get-tuple-element.13), channel_id=1, source_target_pairs={{0,2},{1,3},{2,0},{3,1},{4,6},{5,7},{6,4},{7,5},{8,10},{9,11},{10,... | collective-permute-start | bytes 294920 | tf_op jit(solution)/shard_map/ppermute | solution.py:295
  43.7 6.6 %collective-permute-start.9 = (f32[2,96,128]{2,1,0:T(8,128)S(1)}, f32[2,96,128]{2,1,0:T(8,128)S(1)}, u32[]{:S(2)}, u32[]{:S(2)}) collective-permute-start(f32[2,96,128]{2,1,0:T(8,128)S(1)} %get-tuple-element.11), channel_id=1, source_target_pairs={{0,2},{1,3},{2,0},{3,1},{4,6},{5,7},{6,4},{7,5},{8,10},{9,11},{10,... | collective-permute-start | bytes 294920 | tf_op jit(solution)/shard_map/ppermute | solution.py:295

commit v5 on v4

--- a/solution.py
+++ b/solution.py
@@ -12,7 +12,7 @@
 TILES_DEV = 2
 GROUPS = ((0, 4), (2, 6), (1, 7), (3, 5))
 CHUNKS = ((0, 1), (2, 3))
-ORDERS = (("axyb", "yaxb"), ("xayb", "yaxb"))
+ORDERS = (("axyb", "yabx"), ("xayb", "yxab"))
 CALLS = ((0,), (1,))
 DEPTH = 2
 VMEM_SUMS = 16 << 20

time: 51.3 us -> 50.6 us (0.986)
  starting transfers between devices: 16.6 us -> 14.9 us
  waiting for transfers between devices: 22.7 us -> 23.7 us
    ppermute x10, starting transfers between devices: 16.6 us -> 14.9 us  [halve(): return (value[:half], lax.ppermute(value[half:], ('shot', 'freq'), pairs))]
    ppermute x10, waiting for transfers between devices: 22.7 us -> 23.7 us  [halve(): return (value[:half], lax.ppermute(value[half:], ('shot', 'freq'), pairs))]
  transfers between devices with their start and end apart: 10 -> 10, of which waited for: 6 -> 7; matrix products, arithmetic and copies ran while one was open for 2% -> 2% of each run, Pallas kernels for 6% -> 6%
where the time goes in v5:
time: 50.6 us; the launch traced here: 50.4 us
  waiting for transfers between devices  23.7 us (47%)
  starting transfers between devices  14.9 us (29%)
  Pallas kernels  9.69 us (19%)
  local copies, waits for them, and re-layouts  1.19 us (2%)
  other arithmetic  0.76 us (2%)
    ppermute x10, waiting for transfers between devices, halve(): return (value[:half], lax.ppermute(value[half:], ('shot', 'freq'), pairs))  23.7 us
    ppermute x10, starting transfers between devices, halve(): return (value[:half], lax.ppermute(value[half:], ('shot', 'freq'), pairs))  14.9 us
    pallas_call x2, Pallas kernels, bin_blocks(): pl.pallas_call(body, in_specs=[pl.BlockSpec(memory_space=pltpu.HBM), pl.B...  8.99 us
  transfers between devices with their start and end apart: 10, of which 7 were waited for; matrix products, arithmetic and copies ran while one was open for 2% of the time, Pallas kernels for 6%

profile of v5, /device:TPU:1, one launch (start us, length us, event | category | flops | bytes accessed | tf_op | source)
XLA Modules:
  0.0 50.4 jit_solution(4621342017887880484)
XLA Ops:
  0.0 5.9 %bin_blocks.2 = (f32[64,96,128]{2,1,0:T(8,128)S(1)}, f32[4,512,1024]{2,1,0:T(8,128)S(1)}, f32[4,4,128,128]{3,2,1,0:T(8,128)S(1)}) custom-call(s32[4,16]{1,0:T(4,128)} %refs_0_.3, f32[4,512,1024]{2,1,0:T(8,128)} %refs_1_.1, f32[4,16,128,128]{3,2,1,0:T(8,128)} %refs_2_.1, f32[2,4,48,256]{3,2,1,0:T(8,128)} %constant.4.clone.refs_3_), custom_call_target="tpu_custom_call" | custom-call | tf_op jit(solution)/shard_map/bin_blocks/pallas_call | solution.py:236
  5.9 0.0 copy-start
  5.9 0.1 slice.61
  6.0 0.1 collective-permute-start
  6.2 0.8 %copy-done = f32[2,4,48,256]{3,2,1,0:T(8,128)S(1)} copy-done((f32[2,4,48,256]{3,2,1,0:T(8,128)S(1)}, f32[2,4,48,256]{3,2,1,0:T(8,128)}, u32[]{:S(2)}) %copy-start) | copy-done | bytes 393240
  6.9 3.1 %bin_blocks.3 = f32[64,96,128]{2,1,0:T(8,128)S(1)} custom-call(s32[4,16]{1,0:T(4,128)} %refs_0_.3, f32[4,512,1024]{2,1,0:T(8,128)S(1)} %get-tuple-element.9.refs_1_, f32[4,4,128,128]{3,2,1,0:T(8,128)S(1)} %get-tuple-element.10.refs_2_, f32[2,4,48,256]{3,2,1,0:T(8,128)S(1)} %copy-done), custom_call_target="tpu_custom_call" | custom-call | tf_op jit(solution)/shard_map/bin_blocks/pallas_call | solution.py:236
  10.0 0.1 slice.89
  10.1 0.1 collective-permute-start.5
  10.2 0.0 collective-permute-done
  10.2 0.2 slice_add_fusion.1
  10.4 0.1 slice.81
  10.5 2.8 %collective-permute-start.1 = (f32[16,96,128]{2,1,0:T(8,128)S(1)}, f32[16,96,128]{2,1,0:T(8,128)S(1)}, u32[]{:S(2)}, u32[]{:S(2)}) collective-permute-start(f32[16,96,128]{2,1,0:T(8,128)S(1)} %slice.81), channel_id=1, source_target_pairs={{0,1},{1,0},{2,3},{3,2},{4,20},{5,21},{6,22},{7,23},{8,9},{9,8},{1... | collective-permute-start | bytes 2359304 | tf_op jit(solution)/shard_map/ppermute | solution.py:295
  13.2 0.3 collective-permute-done.5
  13.6 0.2 slice_add_fusion
  13.8 0.1 slice.91
  13.9 2.4 %collective-permute-start.6 = (f32[16,96,128]{2,1,0:T(8,128)S(1)}, f32[16,96,128]{2,1,0:T(8,128)S(1)}, u32[]{:S(2)}, u32[]{:S(2)}) collective-permute-start(f32[16,96,128]{2,1,0:T(8,128)S(1)} %slice.91), channel_id=1, source_target_pairs={{0,8},{1,9},{2,10},{3,11},{4,20},{5,21},{6,22},{7,23},{8,0},{9,1},... | collective-permute-start | bytes 2359304 | tf_op jit(solution)/shard_map/ppermute | solution.py:295
  16.3 6.6 %collective-permute-done.1 = f32[16,96,128]{2,1,0:T(8,128)S(1)} collective-permute-done((f32[16,96,128]{2,1,0:T(8,128)S(1)}, f32[16,96,128]{2,1,0:T(8,128)S(1)}, u32[]{:S(2)}, u32[]{:S(2)}) %collective-permute-start.1) | collective-permute-done | bytes 786464 | tf_op jit(solution)/shard_map/ppermute | solution.py:295
  22.9 0.1 slice_add_fusion.3
  23.0 1.6 %collective-permute-start.2 = (f32[8,96,128]{2,1,0:T(8,128)S(1)}, f32[8,96,128]{2,1,0:T(8,128)S(1)}, u32[]{:S(2)}, u32[]{:S(2)}) collective-permute-start(f32[8,96,128]{2,1,0:T(8,128)S(1)} %slice.83), channel_id=1, source_target_pairs={{0,8},{1,9},{2,10},{3,11},{4,5},{5,4},{6,7},{7,6},{8,0},{9,1},{10,... | collective-permute-start | bytes 1179656 | tf_op jit(solution)/shard_map/ppermute | solution.py:295
  24.6 6.7 %collective-permute-done.6 = f32[16,96,128]{2,1,0:T(8,128)S(1)} collective-permute-done((f32[16,96,128]{2,1,0:T(8,128)S(1)}, f32[16,96,128]{2,1,0:T(8,128)S(1)}, u32[]{:S(2)}, u32[]{:S(2)}) %collective-permute-start.6) | collective-permute-done | bytes 786464 | tf_op jit(solution)/shard_map/ppermute | solution.py:295
  31.3 0.1 slice_add_fusion.2
  31.5 1.5 %collective-permute-start.7 = (f32[8,96,128]{2,1,0:T(8,128)S(1)}, f32[8,96,128]{2,1,0:T(8,128)S(1)}, u32[]{:S(2)}, u32[]{:S(2)}) collective-permute-start(f32[8,96,128]{2,1,0:T(8,128)S(1)} %slice.93), channel_id=1, source_target_pairs={{0,1},{1,0},{2,3},{3,2},{4,12},{5,13},{6,14},{7,15},{8,9},{9,8},{1... | collective-permute-start | bytes 1179656 | tf_op jit(solution)/shard_map/ppermute | solution.py:295
  33.0 0.0 collective-permute-done.2
  33.0 2.4 %collective-permute-start.3 = (f32[4,96,128]{2,1,0:T(8,128)S(1)}, f32[4,96,128]{2,1,0:T(8,128)S(1)}, u32[]{:S(2)}, u32[]{:S(2)}) collective-permute-start(f32[4,96,128]{2,1,0:T(8,128)S(1)} %slice.85), channel_id=1, source_target_pairs={{0,16},{1,17},{2,18},{3,19},{4,6},{5,7},{6,4},{7,5},{8,24},{9,25},... | collective-permute-start | bytes 589832 | tf_op jit(solution)/shard_map/ppermute | solution.py:295
  35.4 3.0 %collective-permute-done.7 = f32[8,96,128]{2,1,0:T(8,128)S(1)} collective-permute-done((f32[8,96,128]{2,1,0:T(8,128)S(1)}, f32[8,96,128]{2,1,0:T(8,128)S(1)}, u32[]{:S(2)}, u32[]{:S(2)}) %collective-permute-start.7) | collective-permute-done | bytes 393248 | tf_op jit(solution)/shard_map/ppermute | solution.py:295
  38.5 0.1 slice_add_fusion.4
  38.5 1.3 %collective-permute-start.8 = (f32[4,96,128]{2,1,0:T(8,128)S(1)}, f32[4,96,128]{2,1,0:T(8,128)S(1)}, u32[]{:S(2)}, u32[]{:S(2)}) collective-permute-start(f32[4,96,128]{2,1,0:T(8,128)S(1)} %slice.95), channel_id=1, source_target_pairs={{0,16},{1,17},{2,18},{3,19},{4,5},{5,4},{6,7},{7,6},{8,24},{9,25},... | collective-permute-start | bytes 589832 | tf_op jit(solution)/shard_map/ppermute | solution.py:295
  39.8 0.8 %collective-permute-done.3 = f32[4,96,128]{2,1,0:T(8,128)S(1)} collective-permute-done((f32[4,96,128]{2,1,0:T(8,128)S(1)}, f32[4,96,128]{2,1,0:T(8,128)S(1)}, u32[]{:S(2)}, u32[]{:S(2)}) %collective-permute-start.3) | collective-permute-done | bytes 196640 | tf_op jit(solution)/shard_map/ppermute | solution.py:295
  40.7 0.5 collective-permute-start.4
  41.2 3.0 %collective-permute-done.8 = f32[4,96,128]{2,1,0:T(8,128)S(1)} collective-permute-done((f32[4,96,128]{2,1,0:T(8,128)S(1)}, f32[4,96,128]{2,1,0:T(8,128)S(1)}, u32[]{:S(2)}, u32[]{:S(2)}) %collective-permute-start.8) | collective-permute-done | bytes 196640 | tf_op jit(solution)/shard_map/ppermute | solution.py:295
  44.2 2.3 %collective-permute-start.9 = (f32[2,96,128]{2,1,0:T(8,128)S(1)}, f32[2,96,128]{2,1,0:T(8,128)S(1)}, u32[]{:S(2)}, u32[]{:S(2)}) collective-permute-start(f32[2,96,128]{2,1,0:T(8,128)S(1)} %get-tuple-element.11), channel_id=1, source_target_pairs={{0,2},{1,3},{2,0},{3,1},{4,6},{5,7},{6,4},{7,5},{8,10},{9,11},{10,... | collective-permute-start | bytes 294920 | tf_op jit(solution)/shard_map/ppermute | solution.py:295
  46.5 0.0 collective-permute-done.4.refs_1_
  46.5 3.2 %collective-permute-done.9.refs_3_ = f32[2,96,128]{2,1,0:T(8,128)S(1)} collective-permute-done((f32[2,96,128]{2,1,0:T(8,128)S(1)}, f32[2,96,128]{2,1,0:T(8,128)S(1)}, u32[]{:S(2)}, u32[]{:S(2)}) %collective-permute-start.9) | collective-permute-done | bytes 98336 | tf_op jit(solution)/shard_map/ppermute | solution.py:295
  49.7 0.7 %assemble.1 = f32[2,2,96,128]{3,2,1,0:T(8,128)} custom-call(f32[2,96,128]{2,1,0:T(8,128)S(1)} %get-tuple-element.14.refs_0_, f32[2,96,128]{2,1,0:T(8,128)S(1)} %collective-permute-done.4.refs_1_, f32[2,96,128]{2,1,0:T(8,128)S(1)} %get-tuple-element.12.refs_2_, f32[2,96,128]{2,1,0:T(8,128)S(1)} %collective-permute-done.9.refs_3_), custom_call_target="tpu_custom_call" | custom-call | tf_op jit(solution)/shard_map/assemble/pallas_call | solution.py:272
  (9 shorter events, 0.2 us)
Async XLA Ops:
  5.9 1.0 %copy-start = (f32[2,4,48,256]{3,2,1,0:T(8,128)S(1)}, f32[2,4,48,256]{3,2,1,0:T(8,128)}, u32[]{:S(2)}) copy-start(f32[2,4,48,256]{3,2,1,0:T(8,128)} %constant.5.clone.refs_3_) | copy-start | bytes 1179652
  6.0 4.2 %collective-permute-start = (f32[32,96,128]{2,1,0:T(8,128)S(1)}, f32[32,96,128]{2,1,0:T(8,128)S(1)}, u32[]{:S(2)}, u32[]{:S(2)}) collective-permute-start(f32[32,96,128]{2,1,0:T(8,128)S(1)} %slice.61), channel_id=1, source_target_pairs={{0,4},{1,5},{2,6},{3,7},{4,0},{5,1},{6,2},{7,3},{8,12},{9,13},{10,... | collective-permute-start | bytes 4718600 | tf_op jit(solution)/shard_map/ppermute | solution.py:295
  10.1 3.5 %collective-permute-start.5 = (f32[32,96,128]{2,1,0:T(8,128)S(1)}, f32[32,96,128]{2,1,0:T(8,128)S(1)}, u32[]{:S(2)}, u32[]{:S(2)}) collective-permute-start(f32[32,96,128]{2,1,0:T(8,128)S(1)} %slice.89), channel_id=1, source_target_pairs={{0,4},{1,5},{2,6},{3,7},{4,0},{5,1},{6,2},{7,3},{8,12},{9,13},{10,... | collective-permute-start | bytes 4718600 | tf_op jit(solution)/shard_map/ppermute | solution.py:295
  10.5 12.4 %collective-permute-start.1 = (f32[16,96,128]{2,1,0:T(8,128)S(1)}, f32[16,96,128]{2,1,0:T(8,128)S(1)}, u32[]{:S(2)}, u32[]{:S(2)}) collective-permute-start(f32[16,96,128]{2,1,0:T(8,128)S(1)} %slice.81), channel_id=1, source_target_pairs={{0,1},{1,0},{2,3},{3,2},{4,20},{5,21},{6,22},{7,23},{8,9},{9,8},{1... | collective-permute-start | bytes 2359304 | tf_op jit(solution)/shard_map/ppermute | solution.py:295
  13.9 17.4 %collective-permute-start.6 = (f32[16,96,128]{2,1,0:T(8,128)S(1)}, f32[16,96,128]{2,1,0:T(8,128)S(1)}, u32[]{:S(2)}, u32[]{:S(2)}) collective-permute-start(f32[16,96,128]{2,1,0:T(8,128)S(1)} %slice.91), channel_id=1, source_target_pairs={{0,8},{1,9},{2,10},{3,11},{4,20},{5,21},{6,22},{7,23},{8,0},{9,1},... | collective-permute-start | bytes 2359304 | tf_op jit(solution)/shard_map/ppermute | solution.py:295
  23.0 9.9 %collective-permute-start.2 = (f32[8,96,128]{2,1,0:T(8,128)S(1)}, f32[8,96,128]{2,1,0:T(8,128)S(1)}, u32[]{:S(2)}, u32[]{:S(2)}) collective-permute-start(f32[8,96,128]{2,1,0:T(8,128)S(1)} %slice.83), channel_id=1, source_target_pairs={{0,8},{1,9},{2,10},{3,11},{4,5},{5,4},{6,7},{7,6},{8,0},{9,1},{10,... | collective-permute-start | bytes 1179656 | tf_op jit(solution)/shard_map/ppermute | solution.py:295
  31.5 7.0 %collective-permute-start.7 = (f32[8,96,128]{2,1,0:T(8,128)S(1)}, f32[8,96,128]{2,1,0:T(8,128)S(1)}, u32[]{:S(2)}, u32[]{:S(2)}) collective-permute-start(f32[8,96,128]{2,1,0:T(8,128)S(1)} %slice.93), channel_id=1, source_target_pairs={{0,1},{1,0},{2,3},{3,2},{4,12},{5,13},{6,14},{7,15},{8,9},{9,8},{1... | collective-permute-start | bytes 1179656 | tf_op jit(solution)/shard_map/ppermute | solution.py:295
  33.0 7.6 %collective-permute-start.3 = (f32[4,96,128]{2,1,0:T(8,128)S(1)}, f32[4,96,128]{2,1,0:T(8,128)S(1)}, u32[]{:S(2)}, u32[]{:S(2)}) collective-permute-start(f32[4,96,128]{2,1,0:T(8,128)S(1)} %slice.85), channel_id=1, source_target_pairs={{0,16},{1,17},{2,18},{3,19},{4,6},{5,7},{6,4},{7,5},{8,24},{9,25},... | collective-permute-start | bytes 589832 | tf_op jit(solution)/shard_map/ppermute | solution.py:295
  38.5 5.6 %collective-permute-start.8 = (f32[4,96,128]{2,1,0:T(8,128)S(1)}, f32[4,96,128]{2,1,0:T(8,128)S(1)}, u32[]{:S(2)}, u32[]{:S(2)}) collective-permute-start(f32[4,96,128]{2,1,0:T(8,128)S(1)} %slice.95), channel_id=1, source_target_pairs={{0,16},{1,17},{2,18},{3,19},{4,5},{5,4},{6,7},{7,6},{8,24},{9,25},... | collective-permute-start | bytes 589832 | tf_op jit(solution)/shard_map/ppermute | solution.py:295
  40.7 5.8 %collective-permute-start.4 = (f32[2,96,128]{2,1,0:T(8,128)S(1)}, f32[2,96,128]{2,1,0:T(8,128)S(1)}, u32[]{:S(2)}, u32[]{:S(2)}) collective-permute-start(f32[2,96,128]{2,1,0:T(8,128)S(1)} %get-tuple-element.13), channel_id=1, source_target_pairs={{0,2},{1,3},{2,0},{3,1},{4,12},{5,13},{6,14},{7,15},{8,10},{9,11},... | collective-permute-start | bytes 294920 | tf_op jit(solution)/shard_map/ppermute | solution.py:295
  44.2 5.5 %collective-permute-start.9 = (f32[2,96,128]{2,1,0:T(8,128)S(1)}, f32[2,96,128]{2,1,0:T(8,128)S(1)}, u32[]{:S(2)}, u32[]{:S(2)}) collective-permute-start(f32[2,96,128]{2,1,0:T(8,128)S(1)} %get-tuple-element.11), channel_id=1, source_target_pairs={{0,2},{1,3},{2,0},{3,1},{4,6},{5,7},{6,4},{7,5},{8,10},{9,11},{10,... | collective-permute-start | bytes 294920 | tf_op jit(solution)/shard_map/ppermute | solution.py:295

commit v6 on v5

--- a/solution.py
+++ b/solution.py
@@ -98,13 +98,15 @@
 
 
 def bin_kernel(chunks, steps, freq_count, load, tiles_hbm, x_ref, w_ref, t_ref, *refs):
+    if load:
+        next_hbm, refs = refs[0], refs[1:]
     outs, refs = refs[: len(chunks)], refs[len(chunks) :]
     if load:
-        x_hbm, w_hbm, xbuf, wbuf = x_ref, w_ref, refs[0], refs[1]
-        refs = refs[2:]
+        x_hbm, w_hbm, xbuf, wbuf, nextbuf = x_ref, w_ref, *refs[:3]
+        refs = refs[3:]
     else:
         xbuf, wbuf = x_ref, w_ref
-    tiles, tbuf, table, spectra, tilesem, xsem, wsem, tsem = refs
+    tiles, tbuf, table, spectra, tilesem, xsem, wsem, tsem, nextsem = refs
     shots_here, blocks_here, block_len, tile_len = wbuf.shape
     me_shot, me_freq = lax.axis_index("shot"), lax.axis_index("freq")
     rows = t_ref.shape[2]
@@ -185,6 +187,9 @@
                 x_copy(i).wait()
                 if i + DEPTH < shots_here:
                     x_copy(i + DEPTH).start()
+                if i == shots_here - 1:
+                    next_copy = pltpu.make_async_copy(next_hbm, nextbuf, nextsem)
+                    next_copy.start()
                 if i + 1 < shots_here:
                     w_copy(i + 1).start()
             folded = fold(xbuf[i], groups)
@@ -193,14 +198,16 @@
                 transform(i, k, folded[k])
             if i and k < blocks_here:
                 spread(i - 1, k)
-
-
-def bin_blocks(tile_ids, traces, interp_weights, chunks, steps, shot_count, freq_count, load, keep):
+    if load:
+        next_copy.wait()
+
+
+def bin_blocks(tile_ids, traces, interp_weights, tables, chunks, steps, shot_count, freq_count, following):
+    load = following is not None
     shots_here, recs_here, time_len = traces.shape
     block_len, tile_len = interp_weights.shape[2:]
     blocks_here = recs_here // block_len
     groups = [g for chunk in chunks for g in chunk]
-    tables = jnp.asarray(dft_tables(groups, freq_count, time_len))
     rows = freq_count * tables.shape[2]
     slot_count = shot_count * freq_count * TILES_DEV
     kept = [
@@ -219,11 +226,10 @@
         pltpu.SemaphoreType.DMA((shots_here,)),
         pltpu.SemaphoreType.DMA((shots_here,)),
         pltpu.SemaphoreType.DMA((freq_count,)),
+        pltpu.SemaphoreType.DMA,
     ]
-    if load and keep:
-        out_shape += [pltpu.VMEM(k.shape, k.dtype) for k in kept]
-    elif load:
-        scratch = [pltpu.VMEM(k.shape, k.dtype) for k in kept] + scratch
+    if load:
+        out_shape += [pltpu.VMEM(k.shape, k.dtype) for k in [*kept, following]]
     place = pltpu.HBM if load else pltpu.VMEM
 
     def body(*refs):
@@ -233,6 +239,7 @@
     traces = pltpu.with_memory_space_constraint(traces, place)
     interp_weights = pltpu.with_memory_space_constraint(interp_weights, place)
     tables = pltpu.with_memory_space_constraint(tables, place)
+    more = [pltpu.with_memory_space_constraint(following, pltpu.HBM)] if load else []
     return pl.pallas_call(
         body,
         in_specs=[
@@ -240,13 +247,14 @@
             pl.BlockSpec(memory_space=place),
             pl.BlockSpec(memory_space=place),
             pl.BlockSpec(memory_space=place),
-        ],
+        ]
+        + [pl.BlockSpec(memory_space=pltpu.HBM)] * load,
         out_specs=[pl.BlockSpec(memory_space=pltpu.VMEM)] * len(out_shape),
         out_shape=out_shape,
         scratch_shapes=scratch,
         compiler_params=pltpu.CompilerParams(vmem_limit_bytes=VMEM_LIMIT),
         name="bin_blocks",
-    )(tile_ids, traces, interp_weights, tables)
+    )(tile_ids, traces, interp_weights, tables, *more)
 
 
 def assemble_kernel(*refs):
@@ -295,23 +303,26 @@
         return value[:half], lax.ppermute(value[half:], ("shot", "freq"), pairs)
 
     sums = [None] * len(CHUNKS)
+    first, following = (
+        jnp.asarray(dft_tables([g for c in call for g in CHUNKS[c]], freq_count, traces.shape[2])) for call in CALLS
+    )
     for n, call in enumerate(CALLS):
         chunks = tuple(CHUNKS[c] for c in call)
         made = bin_blocks(
             tile_ids,
             traces,
             interp_weights,
+            following if n else first,
             chunks,
             [steps[c] for c in call],
             shot_count,
             freq_count,
-            n == 0,
-            n == 0 and len(CALLS) > 1,
+            None if n else following,
         )
         for c, value in zip(call, made):
             sums[c] = value
         if len(made) > len(call):
-            traces, interp_weights = made[len(call) :]
+            traces, interp_weights, following = made[len(call) :]
     last = []
     for orders, value in zip(steps, sums):
         for ways in [(("shot", 0), ("shot", 0)), *zip(*orders)]:

time: 50.6 us -> 49.9 us (0.986)
  local copies, waits for them, and re-layouts: 1.19 us -> 0.43 us
    unnamed x2 -> x0, local copies, waits for them, and re-layouts: 0.76 us -> none
where the time goes in v6:
time: 49.9 us; the launch traced here: 49.7 us
  waiting for transfers between devices  23.3 us (47%)
  starting transfers between devices  15.3 us (31%)
  Pallas kernels  9.71 us (19%)
  other arithmetic  0.76 us (2%)
    ppermute x10, waiting for transfers between devices, halve(): return (value[:half], lax.ppermute(value[half:], ('shot', 'freq'), pairs))  23.3 us
    ppermute x10, starting transfers between devices, halve(): return (value[:half], lax.ppermute(value[half:], ('shot', 'freq'), pairs))  15.3 us
    pallas_call x2, Pallas kernels, bin_blocks(): pl.pallas_call(body, in_specs=[pl.BlockSpec(memory_space=pltpu.HBM), pl.B...  9.01 us
  transfers between devices with their start and end apart: 10, of which 7 were waited for; matrix products, arithmetic and copies ran while one was open for 2% of the time, Pallas kernels for 6%

profile of v6, /device:TPU:1, one launch (start us, length us, event | category | flops | bytes accessed | tf_op | source)
XLA Modules:
  0.0 49.7 jit_solution(16923268326093768798)
XLA Ops:
  0.0 5.9 %bin_blocks.2 = (f32[64,96,128]{2,1,0:T(8,128)S(1)}, f32[4,512,1024]{2,1,0:T(8,128)S(1)}, f32[4,4,128,128]{3,2,1,0:T(8,128)S(1)}, f32[2,4,48,256]{3,2,1,0:T(8,128)S(1)}) custom-call(s32[4,16]{1,0:T(4,128)} %refs_0_.3, f32[4,512,1024]{2,1,0:T(8,128)} %refs_1_.1, f32[4,16,128,128]{3,2,1,0:T(8,128)} %refs_2_.1, f32[2,4,48,256]{3,2,1,0:T(8,128)} %constant.4.clone.refs_3_, ...), custom_call_target="tpu_custom_call" | custom-call | tf_op jit(solution)/shard_map/bin_blocks/pallas_call | solution.py:243
  5.9 0.1 slice.61
  6.0 0.1 collective-permute-start
  6.2 3.1 %bin_blocks.3 = f32[64,96,128]{2,1,0:T(8,128)S(1)} custom-call(s32[4,16]{1,0:T(4,128)} %refs_0_.3, f32[4,512,1024]{2,1,0:T(8,128)S(1)} %get-tuple-element.10.refs_1_, f32[4,4,128,128]{3,2,1,0:T(8,128)S(1)} %get-tuple-element.11.refs_2_, f32[2,4,48,256]{3,2,1,0:T(8,128)S(1)} %get-tuple-element.12.refs_3_), custom_call_target="tpu_custom_call" | custom-call | tf_op jit(solution)/shard_map/bin_blocks/pallas_call | solution.py:243
  9.3 0.1 slice.89
  9.4 0.5 %collective-permute-start.5 = (f32[32,96,128]{2,1,0:T(8,128)S(1)}, f32[32,96,128]{2,1,0:T(8,128)S(1)}, u32[]{:S(2)}, u32[]{:S(2)}) collective-permute-start(f32[32,96,128]{2,1,0:T(8,128)S(1)} %slice.89), channel_id=1, source_target_pairs={{0,4},{1,5},{2,6},{3,7},{4,0},{5,1},{6,2},{7,3},{8,12},{9,13},{10,... | collective-permute-start | bytes 4718600 | tf_op jit(solution)/shard_map/ppermute | solution.py:303
  9.9 0.0 collective-permute-done
  9.9 0.2 slice_add_fusion.1
  10.1 0.1 slice.81
  10.1 2.3 %collective-permute-start.1 = (f32[16,96,128]{2,1,0:T(8,128)S(1)}, f32[16,96,128]{2,1,0:T(8,128)S(1)}, u32[]{:S(2)}, u32[]{:S(2)}) collective-permute-start(f32[16,96,128]{2,1,0:T(8,128)S(1)} %slice.81), channel_id=1, source_target_pairs={{0,1},{1,0},{2,3},{3,2},{4,20},{5,21},{6,22},{7,23},{8,9},{9,8},{1... | collective-permute-start | bytes 2359304 | tf_op jit(solution)/shard_map/ppermute | solution.py:303
  12.5 0.4 collective-permute-done.5
  12.9 0.2 slice_add_fusion
  13.2 0.1 slice.91
  13.2 2.7 %collective-permute-start.6 = (f32[16,96,128]{2,1,0:T(8,128)S(1)}, f32[16,96,128]{2,1,0:T(8,128)S(1)}, u32[]{:S(2)}, u32[]{:S(2)}) collective-permute-start(f32[16,96,128]{2,1,0:T(8,128)S(1)} %slice.91), channel_id=1, source_target_pairs={{0,8},{1,9},{2,10},{3,11},{4,20},{5,21},{6,22},{7,23},{8,0},{9,1},... | collective-permute-start | bytes 2359304 | tf_op jit(solution)/shard_map/ppermute | solution.py:303
  15.9 6.2 %collective-permute-done.1 = f32[16,96,128]{2,1,0:T(8,128)S(1)} collective-permute-done((f32[16,96,128]{2,1,0:T(8,128)S(1)}, f32[16,96,128]{2,1,0:T(8,128)S(1)}, u32[]{:S(2)}, u32[]{:S(2)}) %collective-permute-start.1) | collective-permute-done | bytes 786464 | tf_op jit(solution)/shard_map/ppermute | solution.py:303
  22.2 0.1 slice_add_fusion.3
  22.3 1.6 %collective-permute-start.2 = (f32[8,96,128]{2,1,0:T(8,128)S(1)}, f32[8,96,128]{2,1,0:T(8,128)S(1)}, u32[]{:S(2)}, u32[]{:S(2)}) collective-permute-start(f32[8,96,128]{2,1,0:T(8,128)S(1)} %slice.83), channel_id=1, source_target_pairs={{0,8},{1,9},{2,10},{3,11},{4,5},{5,4},{6,7},{7,6},{8,0},{9,1},{10,... | collective-permute-start | bytes 1179656 | tf_op jit(solution)/shard_map/ppermute | solution.py:303
  23.9 6.7 %collective-permute-done.6 = f32[16,96,128]{2,1,0:T(8,128)S(1)} collective-permute-done((f32[16,96,128]{2,1,0:T(8,128)S(1)}, f32[16,96,128]{2,1,0:T(8,128)S(1)}, u32[]{:S(2)}, u32[]{:S(2)}) %collective-permute-start.6) | collective-permute-done | bytes 786464 | tf_op jit(solution)/shard_map/ppermute | solution.py:303
  30.6 0.1 slice_add_fusion.2
  30.7 1.5 %collective-permute-start.7 = (f32[8,96,128]{2,1,0:T(8,128)S(1)}, f32[8,96,128]{2,1,0:T(8,128)S(1)}, u32[]{:S(2)}, u32[]{:S(2)}) collective-permute-start(f32[8,96,128]{2,1,0:T(8,128)S(1)} %slice.93), channel_id=1, source_target_pairs={{0,1},{1,0},{2,3},{3,2},{4,12},{5,13},{6,14},{7,15},{8,9},{9,8},{1... | collective-permute-start | bytes 1179656 | tf_op jit(solution)/shard_map/ppermute | solution.py:303
  32.2 0.0 collective-permute-done.2
  32.3 2.4 %collective-permute-start.3 = (f32[4,96,128]{2,1,0:T(8,128)S(1)}, f32[4,96,128]{2,1,0:T(8,128)S(1)}, u32[]{:S(2)}, u32[]{:S(2)}) collective-permute-start(f32[4,96,128]{2,1,0:T(8,128)S(1)} %slice.85), channel_id=1, source_target_pairs={{0,16},{1,17},{2,18},{3,19},{4,6},{5,7},{6,4},{7,5},{8,24},{9,25},... | collective-permute-start | bytes 589832 | tf_op jit(solution)/shard_map/ppermute | solution.py:303
  34.7 3.0 %collective-permute-done.7 = f32[8,96,128]{2,1,0:T(8,128)S(1)} collective-permute-done((f32[8,96,128]{2,1,0:T(8,128)S(1)}, f32[8,96,128]{2,1,0:T(8,128)S(1)}, u32[]{:S(2)}, u32[]{:S(2)}) %collective-permute-start.7) | collective-permute-done | bytes 393248 | tf_op jit(solution)/shard_map/ppermute | solution.py:303
  37.7 0.1 slice_add_fusion.4
  37.8 1.3 %collective-permute-start.8 = (f32[4,96,128]{2,1,0:T(8,128)S(1)}, f32[4,96,128]{2,1,0:T(8,128)S(1)}, u32[]{:S(2)}, u32[]{:S(2)}) collective-permute-start(f32[4,96,128]{2,1,0:T(8,128)S(1)} %slice.95), channel_id=1, source_target_pairs={{0,16},{1,17},{2,18},{3,19},{4,5},{5,4},{6,7},{7,6},{8,24},{9,25},... | collective-permute-start | bytes 589832 | tf_op jit(solution)/shard_map/ppermute | solution.py:303
  39.1 0.8 %collective-permute-done.3 = f32[4,96,128]{2,1,0:T(8,128)S(1)} collective-permute-done((f32[4,96,128]{2,1,0:T(8,128)S(1)}, f32[4,96,128]{2,1,0:T(8,128)S(1)}, u32[]{:S(2)}, u32[]{:S(2)}) %collective-permute-start.3) | collective-permute-done | bytes 196640 | tf_op jit(solution)/shard_map/ppermute | solution.py:303
  39.9 0.5 collective-permute-start.4
  40.4 3.0 %collective-permute-done.8 = f32[4,96,128]{2,1,0:T(8,128)S(1)} collective-permute-done((f32[4,96,128]{2,1,0:T(8,128)S(1)}, f32[4,96,128]{2,1,0:T(8,128)S(1)}, u32[]{:S(2)}, u32[]{:S(2)}) %collective-permute-start.8) | collective-permute-done | bytes 196640 | tf_op jit(solution)/shard_map/ppermute | solution.py:303
  43.5 2.5 %collective-permute-start.9 = (f32[2,96,128]{2,1,0:T(8,128)S(1)}, f32[2,96,128]{2,1,0:T(8,128)S(1)}, u32[]{:S(2)}, u32[]{:S(2)}) collective-permute-start(f32[2,96,128]{2,1,0:T(8,128)S(1)} %get-tuple-element.13), channel_id=1, source_target_pairs={{0,2},{1,3},{2,0},{3,1},{4,6},{5,7},{6,4},{7,5},{8,10},{9,11},{10,... | collective-permute-start | bytes 294920 | tf_op jit(solution)/shard_map/ppermute | solution.py:303
  45.9 0.0 collective-permute-done.4.refs_1_
  45.9 3.1 %collective-permute-done.9.refs_3_ = f32[2,96,128]{2,1,0:T(8,128)S(1)} collective-permute-done((f32[2,96,128]{2,1,0:T(8,128)S(1)}, f32[2,96,128]{2,1,0:T(8,128)S(1)}, u32[]{:S(2)}, u32[]{:S(2)}) %collective-permute-start.9) | collective-permute-done | bytes 98336 | tf_op jit(solution)/shard_map/ppermute | solution.py:303
  49.0 0.7 %assemble.1 = f32[2,2,96,128]{3,2,1,0:T(8,128)} custom-call(f32[2,96,128]{2,1,0:T(8,128)S(1)} %get-tuple-element.16.refs_0_, f32[2,96,128]{2,1,0:T(8,128)S(1)} %collective-permute-done.4.refs_1_, f32[2,96,128]{2,1,0:T(8,128)S(1)} %get-tuple-element.14.refs_2_, f32[2,96,128]{2,1,0:T(8,128)S(1)} %collective-permute-done.9.refs_3_), custom_call_target="tpu_custom_call" | custom-call | tf_op jit(solution)/shard_map/assemble/pallas_call | solution.py:280
  (9 shorter events, 0.2 us)
Async XLA Ops:
  6.0 3.8 %collective-permute-start = (f32[32,96,128]{2,1,0:T(8,128)S(1)}, f32[32,96,128]{2,1,0:T(8,128)S(1)}, u32[]{:S(2)}, u32[]{:S(2)}) collective-permute-start(f32[32,96,128]{2,1,0:T(8,128)S(1)} %slice.61), channel_id=1, source_target_pairs={{0,4},{1,5},{2,6},{3,7},{4,0},{5,1},{6,2},{7,3},{8,12},{9,13},{10,... | collective-permute-start | bytes 4718600 | tf_op jit(solution)/shard_map/ppermute | solution.py:303
  9.4 3.5 %collective-permute-start.5 = (f32[32,96,128]{2,1,0:T(8,128)S(1)}, f32[32,96,128]{2,1,0:T(8,128)S(1)}, u32[]{:S(2)}, u32[]{:S(2)}) collective-permute-start(f32[32,96,128]{2,1,0:T(8,128)S(1)} %slice.89), channel_id=1, source_target_pairs={{0,4},{1,5},{2,6},{3,7},{4,0},{5,1},{6,2},{7,3},{8,12},{9,13},{10,... | collective-permute-start | bytes 4718600 | tf_op jit(solution)/shard_map/ppermute | solution.py:303
  10.1 12.0 %collective-permute-start.1 = (f32[16,96,128]{2,1,0:T(8,128)S(1)}, f32[16,96,128]{2,1,0:T(8,128)S(1)}, u32[]{:S(2)}, u32[]{:S(2)}) collective-permute-start(f32[16,96,128]{2,1,0:T(8,128)S(1)} %slice.81), channel_id=1, source_target_pairs={{0,1},{1,0},{2,3},{3,2},{4,20},{5,21},{6,22},{7,23},{8,9},{9,8},{1... | collective-permute-start | bytes 2359304 | tf_op jit(solution)/shard_map/ppermute | solution.py:303
  13.2 17.4 %collective-permute-start.6 = (f32[16,96,128]{2,1,0:T(8,128)S(1)}, f32[16,96,128]{2,1,0:T(8,128)S(1)}, u32[]{:S(2)}, u32[]{:S(2)}) collective-permute-start(f32[16,96,128]{2,1,0:T(8,128)S(1)} %slice.91), channel_id=1, source_target_pairs={{0,8},{1,9},{2,10},{3,11},{4,20},{5,21},{6,22},{7,23},{8,0},{9,1},... | collective-permute-start | bytes 2359304 | tf_op jit(solution)/shard_map/ppermute | solution.py:303
  22.3 9.9 %collective-permute-start.2 = (f32[8,96,128]{2,1,0:T(8,128)S(1)}, f32[8,96,128]{2,1,0:T(8,128)S(1)}, u32[]{:S(2)}, u32[]{:S(2)}) collective-permute-start(f32[8,96,128]{2,1,0:T(8,128)S(1)} %slice.83), channel_id=1, source_target_pairs={{0,8},{1,9},{2,10},{3,11},{4,5},{5,4},{6,7},{7,6},{8,0},{9,1},{10,... | collective-permute-start | bytes 1179656 | tf_op jit(solution)/shard_map/ppermute | solution.py:303
  30.7 7.0 %collective-permute-start.7 = (f32[8,96,128]{2,1,0:T(8,128)S(1)}, f32[8,96,128]{2,1,0:T(8,128)S(1)}, u32[]{:S(2)}, u32[]{:S(2)}) collective-permute-start(f32[8,96,128]{2,1,0:T(8,128)S(1)} %slice.93), channel_id=1, source_target_pairs={{0,1},{1,0},{2,3},{3,2},{4,12},{5,13},{6,14},{7,15},{8,9},{9,8},{1... | collective-permute-start | bytes 1179656 | tf_op jit(solution)/shard_map/ppermute | solution.py:303
  32.3 7.6 %collective-permute-start.3 = (f32[4,96,128]{2,1,0:T(8,128)S(1)}, f32[4,96,128]{2,1,0:T(8,128)S(1)}, u32[]{:S(2)}, u32[]{:S(2)}) collective-permute-start(f32[4,96,128]{2,1,0:T(8,128)S(1)} %slice.85), channel_id=1, source_target_pairs={{0,16},{1,17},{2,18},{3,19},{4,6},{5,7},{6,4},{7,5},{8,24},{9,25},... | collective-permute-start | bytes 589832 | tf_op jit(solution)/shard_map/ppermute | solution.py:303
  37.8 5.6 %collective-permute-start.8 = (f32[4,96,128]{2,1,0:T(8,128)S(1)}, f32[4,96,128]{2,1,0:T(8,128)S(1)}, u32[]{:S(2)}, u32[]{:S(2)}) collective-permute-start(f32[4,96,128]{2,1,0:T(8,128)S(1)} %slice.95), channel_id=1, source_target_pairs={{0,16},{1,17},{2,18},{3,19},{4,5},{5,4},{6,7},{7,6},{8,24},{9,25},... | collective-permute-start | bytes 589832 | tf_op jit(solution)/shard_map/ppermute | solution.py:303
  39.9 6.0 %collective-permute-start.4 = (f32[2,96,128]{2,1,0:T(8,128)S(1)}, f32[2,96,128]{2,1,0:T(8,128)S(1)}, u32[]{:S(2)}, u32[]{:S(2)}) collective-permute-start(f32[2,96,128]{2,1,0:T(8,128)S(1)} %get-tuple-element.15), channel_id=1, source_target_pairs={{0,2},{1,3},{2,0},{3,1},{4,12},{5,13},{6,14},{7,15},{8,10},{9,11},... | collective-permute-start | bytes 294920 | tf_op jit(solution)/shard_map/ppermute | solution.py:303
  43.5 5.5 %collective-permute-start.9 = (f32[2,96,128]{2,1,0:T(8,128)S(1)}, f32[2,96,128]{2,1,0:T(8,128)S(1)}, u32[]{:S(2)}, u32[]{:S(2)}) collective-permute-start(f32[2,96,128]{2,1,0:T(8,128)S(1)} %get-tuple-element.13), channel_id=1, source_target_pairs={{0,2},{1,3},{2,0},{3,1},{4,6},{5,7},{6,4},{7,5},{8,10},{9,11},{10,... | collective-permute-start | bytes 294920 | tf_op jit(solution)/shard_map/ppermute | solution.py:303

commit v7 on v6

--- a/solution.py
+++ b/solution.py
@@ -106,10 +106,10 @@
         refs = refs[3:]
     else:
         xbuf, wbuf = x_ref, w_ref
-    tiles, tbuf, table, spectra, tilesem, xsem, wsem, tsem, nextsem = refs
+    tiles, tbuf, table, spectra, nexttab, tilesem, xsem, wsem, tsem, nextsem = refs
     shots_here, blocks_here, block_len, tile_len = wbuf.shape
     me_shot, me_freq = lax.axis_index("shot"), lax.axis_index("freq")
-    rows = t_ref.shape[2]
+    rows = t_ref.shape[2] if load else t_ref.shape[1] // (2 * freq_count)
     groups = [g for chunk in chunks for g in chunk]
     place, stride, start = {}, {}, 0
     for chunk in chunks:
@@ -126,8 +126,13 @@
     def t_copy(i):
         return pltpu.make_async_copy(t_ref.at[:, jnp.bitwise_xor(me_freq, i)], tbuf.at[:, i], tsem.at[i])
 
-    def near_table(n, i):
-        return tbuf[n, i] if load else t_ref[n, jnp.bitwise_xor(me_freq, i)]
+    def next_copy(i):
+        return pltpu.make_async_copy(next_hbm.at[:, jnp.bitwise_xor(me_freq, i)], nexttab.at[:, i], nextsem.at[i])
+
+    def prepare(source, target):
+        for n in range(source.shape[0]):
+            high, low = split(jnp.concatenate([source[n, i] for i in range(freq_count)], axis=0))
+            target[n] = jnp.concatenate([high, low], axis=0)
 
     tile_copy = pltpu.make_async_copy(tiles_hbm, tiles, tilesem)
     tile_copy.start()
@@ -143,9 +148,10 @@
     if load:
         for i in range(freq_count):
             t_copy(i).wait()
-    for n in range(len(groups)):
-        high, low = split(jnp.concatenate([near_table(n, i) for i in range(freq_count)], axis=0))
-        table[n] = jnp.concatenate([high, low], axis=0)
+    if load:
+        prepare(tbuf, table)
+    else:
+        table = t_ref
 
     def transform(i, n, part):
         high, low = split(part)
@@ -187,9 +193,13 @@
                 x_copy(i).wait()
                 if i + DEPTH < shots_here:
                     x_copy(i + DEPTH).start()
-                if i == shots_here - 1:
-                    next_copy = pltpu.make_async_copy(next_hbm, nextbuf, nextsem)
-                    next_copy.start()
+                if i == 0:
+                    for j in range(freq_count):
+                        next_copy(j).start()
+                if i == shots_here // 2:
+                    for j in range(freq_count):
+                        next_copy(j).wait()
+                    prepare(nexttab, nextbuf)
                 if i + 1 < shots_here:
                     w_copy(i + 1).start()
             folded = fold(xbuf[i], groups)
@@ -198,9 +208,6 @@
                 transform(i, k, folded[k])
             if i and k < blocks_here:
                 spread(i - 1, k)
-    if load:
-        next_copy.wait()
-
 
 def bin_blocks(tile_ids, traces, interp_weights, tables, chunks, steps, shot_count, freq_count, following):
     load = following is not None
@@ -208,28 +215,31 @@
     block_len, tile_len = interp_weights.shape[2:]
     blocks_here = recs_here // block_len
     groups = [g for chunk in chunks for g in chunk]
-    rows = freq_count * tables.shape[2]
+    rows = freq_count * tables.shape[2] if load else tables.shape[1] // 2
     slot_count = shot_count * freq_count * TILES_DEV
     kept = [
         jax.ShapeDtypeStruct(traces.shape, jnp.float32),
         jax.ShapeDtypeStruct((shots_here, blocks_here, block_len, tile_len), jnp.float32),
     ]
-    total = slot_count * len(GROUPS) * tables.shape[2] * tile_len * 4
+    total = slot_count * len(GROUPS) * rows // freq_count * tile_len * 4
     sums = pltpu.VMEM if total <= VMEM_SUMS else jax.ShapeDtypeStruct
-    out_shape = [sums((slot_count, tables.shape[2] * len(chunk), tile_len), jnp.float32) for chunk in chunks]
+    out_shape = [sums((slot_count, rows // freq_count * len(chunk), tile_len), jnp.float32) for chunk in chunks]
     scratch = [
         pltpu.SMEM(tile_ids.shape, jnp.int32),
         pltpu.VMEM(tables.shape, jnp.float32),
-        pltpu.VMEM((len(groups), 2 * rows, tables.shape[3]), jnp.bfloat16),
+        pltpu.VMEM((len(groups), 2 * rows, tables.shape[-1]), jnp.bfloat16),
         pltpu.VMEM((2, len(groups) * rows, recs_here), jnp.float32),
+        pltpu.VMEM(tables.shape if following is None else following.shape, jnp.float32),
         pltpu.SemaphoreType.DMA,
         pltpu.SemaphoreType.DMA((shots_here,)),
         pltpu.SemaphoreType.DMA((shots_here,)),
         pltpu.SemaphoreType.DMA((freq_count,)),
-        pltpu.SemaphoreType.DMA,
+        pltpu.SemaphoreType.DMA((freq_count,)),
     ]
     if load:
-        out_shape += [pltpu.VMEM(k.shape, k.dtype) for k in [*kept, following]]
+        count, _, part, depth = following.shape
+        kept.append(jax.ShapeDtypeStruct((count, 2 * freq_count * part, depth), jnp.bfloat16))
+        out_shape += [pltpu.VMEM(k.shape, k.dtype) for k in kept]
     place = pltpu.HBM if load else pltpu.VMEM
 
     def body(*refs):

time: 49.9 us -> 50.4 us (1.010)
  Pallas kernels: 9.71 us -> 10.3 us
    pallas_call x2, Pallas kernels: 9.01 us -> 9.57 us  [bin_blocks(): pl.pallas_call(body, in_specs=[pl.BlockSpec(memory_space=pltpu.HBM), pl.B...]
where the time goes in v7:
time: 50.4 us; the launch traced here: 50.3 us
  waiting for transfers between devices  23.3 us (46%)
  starting transfers between devices  15.3 us (30%)
  Pallas kernels  10.3 us (20%)
  other arithmetic  0.76 us (2%)
    ppermute x10, waiting for transfers between devices, halve(): return (value[:half], lax.ppermute(value[half:], ('shot', 'freq'), pairs))  23.3 us
    ppermute x10, starting transfers between devices, halve(): return (value[:half], lax.ppermute(value[half:], ('shot', 'freq'), pairs))  15.3 us
    pallas_call x2, Pallas kernels, bin_blocks(): pl.pallas_call(body, in_specs=[pl.BlockSpec(memory_space=pltpu.HBM), pl.B...  9.57 us
  transfers between devices with their start and end apart: 10, of which 7 were waited for; matrix products, arithmetic and copies ran while one was open for 2% of the time, Pallas kernels for 6%

profile of v7, /device:TPU:1, one launch (start us, length us, event | category | flops | bytes accessed | tf_op | source)
XLA Modules:
  0.0 50.3 jit_solution(1510595725451205005)
XLA Ops:
  0.0 6.5 %bin_blocks.2 = (f32[64,96,128]{2,1,0:T(8,128)S(1)}, f32[4,512,1024]{2,1,0:T(8,128)S(1)}, f32[4,4,128,128]{3,2,1,0:T(8,128)S(1)}, bf16[2,384,256]{2,1,0:T(8,128)(2,1)S(1)}) custom-call(s32[4,16]{1,0:T(4,128)} %refs_0_.3, f32[4,512,1024]{2,1,0:T(8,128)} %refs_1_.1, f32[4,16,128,128]{3,2,1,0:T(8,128)} %refs_2_.1, f32[2,4,48,256]{3,2,1,0:T(8,128)} %constant.4.clone.refs_3_, ...), custom_call_target="tpu_custom_call" | custom-call | tf_op jit(solution)/shard_map/bin_blocks/pallas_call | solution.py:253
  6.5 0.1 slice.61
  6.6 0.1 collective-permute-start
  6.7 3.1 %bin_blocks.3 = f32[64,96,128]{2,1,0:T(8,128)S(1)} custom-call(s32[4,16]{1,0:T(4,128)} %refs_0_.3, f32[4,512,1024]{2,1,0:T(8,128)S(1)} %get-tuple-element.10.refs_1_, f32[4,4,128,128]{3,2,1,0:T(8,128)S(1)} %get-tuple-element.11.refs_2_, bf16[2,384,256]{2,1,0:T(8,128)(2,1)S(1)} %get-tuple-element.12.refs_3_), custom_call_target="tpu_custom_call" | custom-call | tf_op jit(solution)/shard_map/bin_blocks/pallas_call | solution.py:253
  9.8 0.1 slice.89
  9.9 0.5 %collective-permute-start.5 = (f32[32,96,128]{2,1,0:T(8,128)S(1)}, f32[32,96,128]{2,1,0:T(8,128)S(1)}, u32[]{:S(2)}, u32[]{:S(2)}) collective-permute-start(f32[32,96,128]{2,1,0:T(8,128)S(1)} %slice.89), channel_id=1, source_target_pairs={{0,4},{1,5},{2,6},{3,7},{4,0},{5,1},{6,2},{7,3},{8,12},{9,13},{10,... | collective-permute-start | bytes 4718600 | tf_op jit(solution)/shard_map/ppermute | solution.py:313
  10.5 0.0 collective-permute-done
  10.5 0.2 slice_add_fusion.1
  10.7 0.1 slice.81
  10.7 2.3 %collective-permute-start.1 = (f32[16,96,128]{2,1,0:T(8,128)S(1)}, f32[16,96,128]{2,1,0:T(8,128)S(1)}, u32[]{:S(2)}, u32[]{:S(2)}) collective-permute-start(f32[16,96,128]{2,1,0:T(8,128)S(1)} %slice.81), channel_id=1, source_target_pairs={{0,1},{1,0},{2,3},{3,2},{4,20},{5,21},{6,22},{7,23},{8,9},{9,8},{1... | collective-permute-start | bytes 2359304 | tf_op jit(solution)/shard_map/ppermute | solution.py:313
  13.0 0.5 collective-permute-done.5
  13.5 0.2 slice_add_fusion
  13.7 0.1 slice.91
  13.8 2.7 %collective-permute-start.6 = (f32[16,96,128]{2,1,0:T(8,128)S(1)}, f32[16,96,128]{2,1,0:T(8,128)S(1)}, u32[]{:S(2)}, u32[]{:S(2)}) collective-permute-start(f32[16,96,128]{2,1,0:T(8,128)S(1)} %slice.91), channel_id=1, source_target_pairs={{0,8},{1,9},{2,10},{3,11},{4,20},{5,21},{6,22},{7,23},{8,0},{9,1},... | collective-permute-start | bytes 2359304 | tf_op jit(solution)/shard_map/ppermute | solution.py:313
  16.5 6.2 %collective-permute-done.1 = f32[16,96,128]{2,1,0:T(8,128)S(1)} collective-permute-done((f32[16,96,128]{2,1,0:T(8,128)S(1)}, f32[16,96,128]{2,1,0:T(8,128)S(1)}, u32[]{:S(2)}, u32[]{:S(2)}) %collective-permute-start.1) | collective-permute-done | bytes 786464 | tf_op jit(solution)/shard_map/ppermute | solution.py:313
  22.7 0.1 slice_add_fusion.3
  22.8 1.6 %collective-permute-start.2 = (f32[8,96,128]{2,1,0:T(8,128)S(1)}, f32[8,96,128]{2,1,0:T(8,128)S(1)}, u32[]{:S(2)}, u32[]{:S(2)}) collective-permute-start(f32[8,96,128]{2,1,0:T(8,128)S(1)} %slice.83), channel_id=1, source_target_pairs={{0,8},{1,9},{2,10},{3,11},{4,5},{5,4},{6,7},{7,6},{8,0},{9,1},{10,... | collective-permute-start | bytes 1179656 | tf_op jit(solution)/shard_map/ppermute | solution.py:313
  24.4 6.7 %collective-permute-done.6 = f32[16,96,128]{2,1,0:T(8,128)S(1)} collective-permute-done((f32[16,96,128]{2,1,0:T(8,128)S(1)}, f32[16,96,128]{2,1,0:T(8,128)S(1)}, u32[]{:S(2)}, u32[]{:S(2)}) %collective-permute-start.6) | collective-permute-done | bytes 786464 | tf_op jit(solution)/shard_map/ppermute | solution.py:313
  31.1 0.1 slice_add_fusion.2
  31.3 1.5 %collective-permute-start.7 = (f32[8,96,128]{2,1,0:T(8,128)S(1)}, f32[8,96,128]{2,1,0:T(8,128)S(1)}, u32[]{:S(2)}, u32[]{:S(2)}) collective-permute-start(f32[8,96,128]{2,1,0:T(8,128)S(1)} %slice.93), channel_id=1, source_target_pairs={{0,1},{1,0},{2,3},{3,2},{4,12},{5,13},{6,14},{7,15},{8,9},{9,8},{1... | collective-permute-start | bytes 1179656 | tf_op jit(solution)/shard_map/ppermute | solution.py:313
  32.8 0.0 collective-permute-done.2
  32.9 2.4 %collective-permute-start.3 = (f32[4,96,128]{2,1,0:T(8,128)S(1)}, f32[4,96,128]{2,1,0:T(8,128)S(1)}, u32[]{:S(2)}, u32[]{:S(2)}) collective-permute-start(f32[4,96,128]{2,1,0:T(8,128)S(1)} %slice.85), channel_id=1, source_target_pairs={{0,16},{1,17},{2,18},{3,19},{4,6},{5,7},{6,4},{7,5},{8,24},{9,25},... | collective-permute-start | bytes 589832 | tf_op jit(solution)/shard_map/ppermute | solution.py:313
  35.2 3.0 %collective-permute-done.7 = f32[8,96,128]{2,1,0:T(8,128)S(1)} collective-permute-done((f32[8,96,128]{2,1,0:T(8,128)S(1)}, f32[8,96,128]{2,1,0:T(8,128)S(1)}, u32[]{:S(2)}, u32[]{:S(2)}) %collective-permute-start.7) | collective-permute-done | bytes 393248 | tf_op jit(solution)/shard_map/ppermute | solution.py:313
  38.3 0.1 slice_add_fusion.4
  38.3 1.3 %collective-permute-start.8 = (f32[4,96,128]{2,1,0:T(8,128)S(1)}, f32[4,96,128]{2,1,0:T(8,128)S(1)}, u32[]{:S(2)}, u32[]{:S(2)}) collective-permute-start(f32[4,96,128]{2,1,0:T(8,128)S(1)} %slice.95), channel_id=1, source_target_pairs={{0,16},{1,17},{2,18},{3,19},{4,5},{5,4},{6,7},{7,6},{8,24},{9,25},... | collective-permute-start | bytes 589832 | tf_op jit(solution)/shard_map/ppermute | solution.py:313
  39.6 0.8 %collective-permute-done.3 = f32[4,96,128]{2,1,0:T(8,128)S(1)} collective-permute-done((f32[4,96,128]{2,1,0:T(8,128)S(1)}, f32[4,96,128]{2,1,0:T(8,128)S(1)}, u32[]{:S(2)}, u32[]{:S(2)}) %collective-permute-start.3) | collective-permute-done | bytes 196640 | tf_op jit(solution)/shard_map/ppermute | solution.py:313
  40.5 0.5 collective-permute-start.4
  41.0 3.0 %collective-permute-done.8 = f32[4,96,128]{2,1,0:T(8,128)S(1)} collective-permute-done((f32[4,96,128]{2,1,0:T(8,128)S(1)}, f32[4,96,128]{2,1,0:T(8,128)S(1)}, u32[]{:S(2)}, u32[]{:S(2)}) %collective-permute-start.8) | collective-permute-done | bytes 196640 | tf_op jit(solution)/shard_map/ppermute | solution.py:313
  44.0 2.5 %collective-permute-start.9 = (f32[2,96,128]{2,1,0:T(8,128)S(1)}, f32[2,96,128]{2,1,0:T(8,128)S(1)}, u32[]{:S(2)}, u32[]{:S(2)}) collective-permute-start(f32[2,96,128]{2,1,0:T(8,128)S(1)} %get-tuple-element.13), channel_id=1, source_target_pairs={{0,2},{1,3},{2,0},{3,1},{4,6},{5,7},{6,4},{7,5},{8,10},{9,11},{10,... | collective-permute-start | bytes 294920 | tf_op jit(solution)/shard_map/ppermute | solution.py:313
  46.5 0.0 collective-permute-done.4.refs_1_
  46.5 3.1 %collective-permute-done.9.refs_3_ = f32[2,96,128]{2,1,0:T(8,128)S(1)} collective-permute-done((f32[2,96,128]{2,1,0:T(8,128)S(1)}, f32[2,96,128]{2,1,0:T(8,128)S(1)}, u32[]{:S(2)}, u32[]{:S(2)}) %collective-permute-start.9) | collective-permute-done | bytes 98336 | tf_op jit(solution)/shard_map/ppermute | solution.py:313
  49.6 0.7 %assemble.1 = f32[2,2,96,128]{3,2,1,0:T(8,128)} custom-call(f32[2,96,128]{2,1,0:T(8,128)S(1)} %get-tuple-element.16.refs_0_, f32[2,96,128]{2,1,0:T(8,128)S(1)} %collective-permute-done.4.refs_1_, f32[2,96,128]{2,1,0:T(8,128)S(1)} %get-tuple-element.14.refs_2_, f32[2,96,128]{2,1,0:T(8,128)S(1)} %collective-permute-done.9.refs_3_), custom_call_target="tpu_custom_call" | custom-call | tf_op jit(solution)/shard_map/assemble/pallas_call | solution.py:290
  (9 shorter events, 0.2 us)
Async XLA Ops:
  6.6 3.8 %collective-permute-start = (f32[32,96,128]{2,1,0:T(8,128)S(1)}, f32[32,96,128]{2,1,0:T(8,128)S(1)}, u32[]{:S(2)}, u32[]{:S(2)}) collective-permute-start(f32[32,96,128]{2,1,0:T(8,128)S(1)} %slice.61), channel_id=1, source_target_pairs={{0,4},{1,5},{2,6},{3,7},{4,0},{5,1},{6,2},{7,3},{8,12},{9,13},{10,... | collective-permute-start | bytes 4718600 | tf_op jit(solution)/shard_map/ppermute | solution.py:313
  9.9 3.6 %collective-permute-start.5 = (f32[32,96,128]{2,1,0:T(8,128)S(1)}, f32[32,96,128]{2,1,0:T(8,128)S(1)}, u32[]{:S(2)}, u32[]{:S(2)}) collective-permute-start(f32[32,96,128]{2,1,0:T(8,128)S(1)} %slice.89), channel_id=1, source_target_pairs={{0,4},{1,5},{2,6},{3,7},{4,0},{5,1},{6,2},{7,3},{8,12},{9,13},{10,... | collective-permute-start | bytes 4718600 | tf_op jit(solution)/shard_map/ppermute | solution.py:313
  10.7 12.0 %collective-permute-start.1 = (f32[16,96,128]{2,1,0:T(8,128)S(1)}, f32[16,96,128]{2,1,0:T(8,128)S(1)}, u32[]{:S(2)}, u32[]{:S(2)}) collective-permute-start(f32[16,96,128]{2,1,0:T(8,128)S(1)} %slice.81), channel_id=1, source_target_pairs={{0,1},{1,0},{2,3},{3,2},{4,20},{5,21},{6,22},{7,23},{8,9},{9,8},{1... | collective-permute-start | bytes 2359304 | tf_op jit(solution)/shard_map/ppermute | solution.py:313
  13.8 17.3 %collective-permute-start.6 = (f32[16,96,128]{2,1,0:T(8,128)S(1)}, f32[16,96,128]{2,1,0:T(8,128)S(1)}, u32[]{:S(2)}, u32[]{:S(2)}) collective-permute-start(f32[16,96,128]{2,1,0:T(8,128)S(1)} %slice.91), channel_id=1, source_target_pairs={{0,8},{1,9},{2,10},{3,11},{4,20},{5,21},{6,22},{7,23},{8,0},{9,1},... | collective-permute-start | bytes 2359304 | tf_op jit(solution)/shard_map/ppermute | solution.py:313
  22.8 9.9 %collective-permute-start.2 = (f32[8,96,128]{2,1,0:T(8,128)S(1)}, f32[8,96,128]{2,1,0:T(8,128)S(1)}, u32[]{:S(2)}, u32[]{:S(2)}) collective-permute-start(f32[8,96,128]{2,1,0:T(8,128)S(1)} %slice.83), channel_id=1, source_target_pairs={{0,8},{1,9},{2,10},{3,11},{4,5},{5,4},{6,7},{7,6},{8,0},{9,1},{10,... | collective-permute-start | bytes 1179656 | tf_op jit(solution)/shard_map/ppermute | solution.py:313
  31.3 7.0 %collective-permute-start.7 = (f32[8,96,128]{2,1,0:T(8,128)S(1)}, f32[8,96,128]{2,1,0:T(8,128)S(1)}, u32[]{:S(2)}, u32[]{:S(2)}) collective-permute-start(f32[8,96,128]{2,1,0:T(8,128)S(1)} %slice.93), channel_id=1, source_target_pairs={{0,1},{1,0},{2,3},{3,2},{4,12},{5,13},{6,14},{7,15},{8,9},{9,8},{1... | collective-permute-start | bytes 1179656 | tf_op jit(solution)/shard_map/ppermute | solution.py:313
  32.9 7.6 %collective-permute-start.3 = (f32[4,96,128]{2,1,0:T(8,128)S(1)}, f32[4,96,128]{2,1,0:T(8,128)S(1)}, u32[]{:S(2)}, u32[]{:S(2)}) collective-permute-start(f32[4,96,128]{2,1,0:T(8,128)S(1)} %slice.85), channel_id=1, source_target_pairs={{0,16},{1,17},{2,18},{3,19},{4,6},{5,7},{6,4},{7,5},{8,24},{9,25},... | collective-permute-start | bytes 589832 | tf_op jit(solution)/shard_map/ppermute | solution.py:313
  38.3 5.6 %collective-permute-start.8 = (f32[4,96,128]{2,1,0:T(8,128)S(1)}, f32[4,96,128]{2,1,0:T(8,128)S(1)}, u32[]{:S(2)}, u32[]{:S(2)}) collective-permute-start(f32[4,96,128]{2,1,0:T(8,128)S(1)} %slice.95), channel_id=1, source_target_pairs={{0,16},{1,17},{2,18},{3,19},{4,5},{5,4},{6,7},{7,6},{8,24},{9,25},... | collective-permute-start | bytes 589832 | tf_op jit(solution)/shard_map/ppermute | solution.py:313
  40.5 6.0 %collective-permute-start.4 = (f32[2,96,128]{2,1,0:T(8,128)S(1)}, f32[2,96,128]{2,1,0:T(8,128)S(1)}, u32[]{:S(2)}, u32[]{:S(2)}) collective-permute-start(f32[2,96,128]{2,1,0:T(8,128)S(1)} %get-tuple-element.15), channel_id=1, source_target_pairs={{0,2},{1,3},{2,0},{3,1},{4,12},{5,13},{6,14},{7,15},{8,10},{9,11},... | collective-permute-start | bytes 294920 | tf_op jit(solution)/shard_map/ppermute | solution.py:313
  44.0 5.5 %collective-permute-start.9 = (f32[2,96,128]{2,1,0:T(8,128)S(1)}, f32[2,96,128]{2,1,0:T(8,128)S(1)}, u32[]{:S(2)}, u32[]{:S(2)}) collective-permute-start(f32[2,96,128]{2,1,0:T(8,128)S(1)} %get-tuple-element.13), channel_id=1, source_target_pairs={{0,2},{1,3},{2,0},{3,1},{4,6},{5,7},{6,4},{7,5},{8,10},{9,11},{10,... | collective-permute-start | bytes 294920 | tf_op jit(solution)/shard_map/ppermute | solution.py:313

commit v8 on v6

--- a/solution.py
+++ b/solution.py
@@ -12,7 +12,7 @@
 TILES_DEV = 2
 GROUPS = ((0, 4), (2, 6), (1, 7), (3, 5))
 CHUNKS = ((0, 1), (2, 3))
-ORDERS = (("axyb", "yabx"), ("xayb", "yxab"))
+ORDERS = (("ayxb", "xaby"), ("yaxb", "xyab"))
 CALLS = ((0,), (1,))
 DEPTH = 2
 VMEM_SUMS = 16 << 20

time: 49.9 us -> 49.9 us (level)
  no operation moved by 1% of the time
where the time goes in v8:
time: 49.9 us; the launch traced here: 49.7 us
  waiting for transfers between devices  23.3 us (47%)
  starting transfers between devices  15.4 us (31%)
  Pallas kernels  9.71 us (19%)
  other arithmetic  0.76 us (2%)
    ppermute x10, waiting for transfers between devices, halve(): return (value[:half], lax.ppermute(value[half:], ('shot', 'freq'), pairs))  23.3 us
    ppermute x10, starting transfers between devices, halve(): return (value[:half], lax.ppermute(value[half:], ('shot', 'freq'), pairs))  15.4 us
    pallas_call x2, Pallas kernels, bin_blocks(): pl.pallas_call(body, in_specs=[pl.BlockSpec(memory_space=pltpu.HBM), pl.B...  9.01 us
  transfers between devices with their start and end apart: 10, of which 7 were waited for; matrix products, arithmetic and copies ran while one was open for 2% of the time, Pallas kernels for 6%

profile of v8, /device:TPU:1, one launch (start us, length us, event | category | flops | bytes accessed | tf_op | source)
XLA Modules:
  0.0 49.7 jit_solution(3449877236851724997)
XLA Ops:
  0.0 5.9 %bin_blocks.2 = (f32[64,96,128]{2,1,0:T(8,128)S(1)}, f32[4,512,1024]{2,1,0:T(8,128)S(1)}, f32[4,4,128,128]{3,2,1,0:T(8,128)S(1)}, f32[2,4,48,256]{3,2,1,0:T(8,128)S(1)}) custom-call(s32[4,16]{1,0:T(4,128)} %refs_0_.3, f32[4,512,1024]{2,1,0:T(8,128)} %refs_1_.1, f32[4,16,128,128]{3,2,1,0:T(8,128)} %refs_2_.1, f32[2,4,48,256]{3,2,1,0:T(8,128)} %constant.4.clone.refs_3_, ...), custom_call_target="tpu_custom_call" | custom-call | tf_op jit(solution)/shard_map/bin_blocks/pallas_call | solution.py:243
  5.9 0.1 slice.61
  6.0 0.1 collective-permute-start
  6.2 3.1 %bin_blocks.3 = f32[64,96,128]{2,1,0:T(8,128)S(1)} custom-call(s32[4,16]{1,0:T(4,128)} %refs_0_.3, f32[4,512,1024]{2,1,0:T(8,128)S(1)} %get-tuple-element.10.refs_1_, f32[4,4,128,128]{3,2,1,0:T(8,128)S(1)} %get-tuple-element.11.refs_2_, f32[2,4,48,256]{3,2,1,0:T(8,128)S(1)} %get-tuple-element.12.refs_3_), custom_call_target="tpu_custom_call" | custom-call | tf_op jit(solution)/shard_map/bin_blocks/pallas_call | solution.py:243
  9.3 0.1 slice.89
  9.4 0.5 %collective-permute-start.5 = (f32[32,96,128]{2,1,0:T(8,128)S(1)}, f32[32,96,128]{2,1,0:T(8,128)S(1)}, u32[]{:S(2)}, u32[]{:S(2)}) collective-permute-start(f32[32,96,128]{2,1,0:T(8,128)S(1)} %slice.89), channel_id=1, source_target_pairs={{0,4},{1,5},{2,6},{3,7},{4,0},{5,1},{6,2},{7,3},{8,12},{9,13},{10,... | collective-permute-start | bytes 4718600 | tf_op jit(solution)/shard_map/ppermute | solution.py:303
  9.9 0.0 collective-permute-done
  9.9 0.2 slice_add_fusion.1
  10.1 0.1 slice.81
  10.1 2.3 %collective-permute-start.1 = (f32[16,96,128]{2,1,0:T(8,128)S(1)}, f32[16,96,128]{2,1,0:T(8,128)S(1)}, u32[]{:S(2)}, u32[]{:S(2)}) collective-permute-start(f32[16,96,128]{2,1,0:T(8,128)S(1)} %slice.81), channel_id=1, source_target_pairs={{0,1},{1,0},{2,3},{3,2},{4,12},{5,13},{6,14},{7,15},{8,9},{9,8},{1... | collective-permute-start | bytes 2359304 | tf_op jit(solution)/shard_map/ppermute | solution.py:303
  12.4 0.5 collective-permute-done.5
  12.9 0.2 slice_add_fusion
  13.2 0.1 slice.91
  13.2 2.7 %collective-permute-start.6 = (f32[16,96,128]{2,1,0:T(8,128)S(1)}, f32[16,96,128]{2,1,0:T(8,128)S(1)}, u32[]{:S(2)}, u32[]{:S(2)}) collective-permute-start(f32[16,96,128]{2,1,0:T(8,128)S(1)} %slice.91), channel_id=1, source_target_pairs={{0,16},{1,17},{2,18},{3,19},{4,12},{5,13},{6,14},{7,15},{8,24},{9,... | collective-permute-start | bytes 2359304 | tf_op jit(solution)/shard_map/ppermute | solution.py:303
  15.9 6.2 %collective-permute-done.1 = f32[16,96,128]{2,1,0:T(8,128)S(1)} collective-permute-done((f32[16,96,128]{2,1,0:T(8,128)S(1)}, f32[16,96,128]{2,1,0:T(8,128)S(1)}, u32[]{:S(2)}, u32[]{:S(2)}) %collective-permute-start.1) | collective-permute-done | bytes 786464 | tf_op jit(solution)/shard_map/ppermute | solution.py:303
  22.1 0.1 slice_add_fusion.3
  22.3 1.6 %collective-permute-start.2 = (f32[8,96,128]{2,1,0:T(8,128)S(1)}, f32[8,96,128]{2,1,0:T(8,128)S(1)}, u32[]{:S(2)}, u32[]{:S(2)}) collective-permute-start(f32[8,96,128]{2,1,0:T(8,128)S(1)} %slice.83), channel_id=1, source_target_pairs={{0,16},{1,17},{2,18},{3,19},{4,5},{5,4},{6,7},{7,6},{8,24},{9,25},... | collective-permute-start | bytes 1179656 | tf_op jit(solution)/shard_map/ppermute | solution.py:303
  23.9 6.7 %collective-permute-done.6 = f32[16,96,128]{2,1,0:T(8,128)S(1)} collective-permute-done((f32[16,96,128]{2,1,0:T(8,128)S(1)}, f32[16,96,128]{2,1,0:T(8,128)S(1)}, u32[]{:S(2)}, u32[]{:S(2)}) %collective-permute-start.6) | collective-permute-done | bytes 786464 | tf_op jit(solution)/shard_map/ppermute | solution.py:303
  30.5 0.1 slice_add_fusion.2
  30.7 1.6 %collective-permute-start.7 = (f32[8,96,128]{2,1,0:T(8,128)S(1)}, f32[8,96,128]{2,1,0:T(8,128)S(1)}, u32[]{:S(2)}, u32[]{:S(2)}) collective-permute-start(f32[8,96,128]{2,1,0:T(8,128)S(1)} %slice.93), channel_id=1, source_target_pairs={{0,1},{1,0},{2,3},{3,2},{4,20},{5,21},{6,22},{7,23},{8,9},{9,8},{1... | collective-permute-start | bytes 1179656 | tf_op jit(solution)/shard_map/ppermute | solution.py:303
  32.2 0.0 collective-permute-done.2
  32.3 2.4 %collective-permute-start.3 = (f32[4,96,128]{2,1,0:T(8,128)S(1)}, f32[4,96,128]{2,1,0:T(8,128)S(1)}, u32[]{:S(2)}, u32[]{:S(2)}) collective-permute-start(f32[4,96,128]{2,1,0:T(8,128)S(1)} %slice.85), channel_id=1, source_target_pairs={{0,8},{1,9},{2,10},{3,11},{4,6},{5,7},{6,4},{7,5},{8,0},{9,1},{10,... | collective-permute-start | bytes 589832 | tf_op jit(solution)/shard_map/ppermute | solution.py:303
  34.7 3.0 %collective-permute-done.7 = f32[8,96,128]{2,1,0:T(8,128)S(1)} collective-permute-done((f32[8,96,128]{2,1,0:T(8,128)S(1)}, f32[8,96,128]{2,1,0:T(8,128)S(1)}, u32[]{:S(2)}, u32[]{:S(2)}) %collective-permute-start.7) | collective-permute-done | bytes 393248 | tf_op jit(solution)/shard_map/ppermute | solution.py:303
  37.7 0.1 slice_add_fusion.4
  37.8 1.3 %collective-permute-start.8 = (f32[4,96,128]{2,1,0:T(8,128)S(1)}, f32[4,96,128]{2,1,0:T(8,128)S(1)}, u32[]{:S(2)}, u32[]{:S(2)}) collective-permute-start(f32[4,96,128]{2,1,0:T(8,128)S(1)} %slice.95), channel_id=1, source_target_pairs={{0,8},{1,9},{2,10},{3,11},{4,5},{5,4},{6,7},{7,6},{8,0},{9,1},{10,... | collective-permute-start | bytes 589832 | tf_op jit(solution)/shard_map/ppermute | solution.py:303
  39.1 0.8 %collective-permute-done.3 = f32[4,96,128]{2,1,0:T(8,128)S(1)} collective-permute-done((f32[4,96,128]{2,1,0:T(8,128)S(1)}, f32[4,96,128]{2,1,0:T(8,128)S(1)}, u32[]{:S(2)}, u32[]{:S(2)}) %collective-permute-start.3) | collective-permute-done | bytes 196640 | tf_op jit(solution)/shard_map/ppermute | solution.py:303
  39.9 0.5 collective-permute-start.4
  40.4 3.0 %collective-permute-done.8 = f32[4,96,128]{2,1,0:T(8,128)S(1)} collective-permute-done((f32[4,96,128]{2,1,0:T(8,128)S(1)}, f32[4,96,128]{2,1,0:T(8,128)S(1)}, u32[]{:S(2)}, u32[]{:S(2)}) %collective-permute-start.8) | collective-permute-done | bytes 196640 | tf_op jit(solution)/shard_map/ppermute | solution.py:303
  43.5 2.5 %collective-permute-start.9 = (f32[2,96,128]{2,1,0:T(8,128)S(1)}, f32[2,96,128]{2,1,0:T(8,128)S(1)}, u32[]{:S(2)}, u32[]{:S(2)}) collective-permute-start(f32[2,96,128]{2,1,0:T(8,128)S(1)} %get-tuple-element.13), channel_id=1, source_target_pairs={{0,2},{1,3},{2,0},{3,1},{4,6},{5,7},{6,4},{7,5},{8,10},{9,11},{10,... | collective-permute-start | bytes 294920 | tf_op jit(solution)/shard_map/ppermute | solution.py:303
  45.9 0.0 collective-permute-done.4.refs_1_
  45.9 3.1 %collective-permute-done.9.refs_3_ = f32[2,96,128]{2,1,0:T(8,128)S(1)} collective-permute-done((f32[2,96,128]{2,1,0:T(8,128)S(1)}, f32[2,96,128]{2,1,0:T(8,128)S(1)}, u32[]{:S(2)}, u32[]{:S(2)}) %collective-permute-start.9) | collective-permute-done | bytes 98336 | tf_op jit(solution)/shard_map/ppermute | solution.py:303
  49.0 0.7 %assemble.1 = f32[2,2,96,128]{3,2,1,0:T(8,128)} custom-call(f32[2,96,128]{2,1,0:T(8,128)S(1)} %get-tuple-element.16.refs_0_, f32[2,96,128]{2,1,0:T(8,128)S(1)} %collective-permute-done.4.refs_1_, f32[2,96,128]{2,1,0:T(8,128)S(1)} %get-tuple-element.14.refs_2_, f32[2,96,128]{2,1,0:T(8,128)S(1)} %collective-permute-done.9.refs_3_), custom_call_target="tpu_custom_call" | custom-call | tf_op jit(solution)/shard_map/assemble/pallas_call | solution.py:280
  (9 shorter events, 0.2 us)
Async XLA Ops:
  6.0 3.8 %collective-permute-start = (f32[32,96,128]{2,1,0:T(8,128)S(1)}, f32[32,96,128]{2,1,0:T(8,128)S(1)}, u32[]{:S(2)}, u32[]{:S(2)}) collective-permute-start(f32[32,96,128]{2,1,0:T(8,128)S(1)} %slice.61), channel_id=1, source_target_pairs={{0,4},{1,5},{2,6},{3,7},{4,0},{5,1},{6,2},{7,3},{8,12},{9,13},{10,... | collective-permute-start | bytes 4718600 | tf_op jit(solution)/shard_map/ppermute | solution.py:303
  9.4 3.5 %collective-permute-start.5 = (f32[32,96,128]{2,1,0:T(8,128)S(1)}, f32[32,96,128]{2,1,0:T(8,128)S(1)}, u32[]{:S(2)}, u32[]{:S(2)}) collective-permute-start(f32[32,96,128]{2,1,0:T(8,128)S(1)} %slice.89), channel_id=1, source_target_pairs={{0,4},{1,5},{2,6},{3,7},{4,0},{5,1},{6,2},{7,3},{8,12},{9,13},{10,... | collective-permute-start | bytes 4718600 | tf_op jit(solution)/shard_map/ppermute | solution.py:303
  10.1 12.0 %collective-permute-start.1 = (f32[16,96,128]{2,1,0:T(8,128)S(1)}, f32[16,96,128]{2,1,0:T(8,128)S(1)}, u32[]{:S(2)}, u32[]{:S(2)}) collective-permute-start(f32[16,96,128]{2,1,0:T(8,128)S(1)} %slice.81), channel_id=1, source_target_pairs={{0,1},{1,0},{2,3},{3,2},{4,12},{5,13},{6,14},{7,15},{8,9},{9,8},{1... | collective-permute-start | bytes 2359304 | tf_op jit(solution)/shard_map/ppermute | solution.py:303
  13.2 17.3 %collective-permute-start.6 = (f32[16,96,128]{2,1,0:T(8,128)S(1)}, f32[16,96,128]{2,1,0:T(8,128)S(1)}, u32[]{:S(2)}, u32[]{:S(2)}) collective-permute-start(f32[16,96,128]{2,1,0:T(8,128)S(1)} %slice.91), channel_id=1, source_target_pairs={{0,16},{1,17},{2,18},{3,19},{4,12},{5,13},{6,14},{7,15},{8,24},{9,... | collective-permute-start | bytes 2359304 | tf_op jit(solution)/shard_map/ppermute | solution.py:303
  22.3 10.0 %collective-permute-start.2 = (f32[8,96,128]{2,1,0:T(8,128)S(1)}, f32[8,96,128]{2,1,0:T(8,128)S(1)}, u32[]{:S(2)}, u32[]{:S(2)}) collective-permute-start(f32[8,96,128]{2,1,0:T(8,128)S(1)} %slice.83), channel_id=1, source_target_pairs={{0,16},{1,17},{2,18},{3,19},{4,5},{5,4},{6,7},{7,6},{8,24},{9,25},... | collective-permute-start | bytes 1179656 | tf_op jit(solution)/shard_map/ppermute | solution.py:303
  30.7 7.0 %collective-permute-start.7 = (f32[8,96,128]{2,1,0:T(8,128)S(1)}, f32[8,96,128]{2,1,0:T(8,128)S(1)}, u32[]{:S(2)}, u32[]{:S(2)}) collective-permute-start(f32[8,96,128]{2,1,0:T(8,128)S(1)} %slice.93), channel_id=1, source_target_pairs={{0,1},{1,0},{2,3},{3,2},{4,20},{5,21},{6,22},{7,23},{8,9},{9,8},{1... | collective-permute-start | bytes 1179656 | tf_op jit(solution)/shard_map/ppermute | solution.py:303
  32.3 7.6 %collective-permute-start.3 = (f32[4,96,128]{2,1,0:T(8,128)S(1)}, f32[4,96,128]{2,1,0:T(8,128)S(1)}, u32[]{:S(2)}, u32[]{:S(2)}) collective-permute-start(f32[4,96,128]{2,1,0:T(8,128)S(1)} %slice.85), channel_id=1, source_target_pairs={{0,8},{1,9},{2,10},{3,11},{4,6},{5,7},{6,4},{7,5},{8,0},{9,1},{10,... | collective-permute-start | bytes 589832 | tf_op jit(solution)/shard_map/ppermute | solution.py:303
  37.8 5.6 %collective-permute-start.8 = (f32[4,96,128]{2,1,0:T(8,128)S(1)}, f32[4,96,128]{2,1,0:T(8,128)S(1)}, u32[]{:S(2)}, u32[]{:S(2)}) collective-permute-start(f32[4,96,128]{2,1,0:T(8,128)S(1)} %slice.95), channel_id=1, source_target_pairs={{0,8},{1,9},{2,10},{3,11},{4,5},{5,4},{6,7},{7,6},{8,0},{9,1},{10,... | collective-permute-start | bytes 589832 | tf_op jit(solution)/shard_map/ppermute | solution.py:303
  39.9 6.0 %collective-permute-start.4 = (f32[2,96,128]{2,1,0:T(8,128)S(1)}, f32[2,96,128]{2,1,0:T(8,128)S(1)}, u32[]{:S(2)}, u32[]{:S(2)}) collective-permute-start(f32[2,96,128]{2,1,0:T(8,128)S(1)} %get-tuple-element.15), channel_id=1, source_target_pairs={{0,2},{1,3},{2,0},{3,1},{4,20},{5,21},{6,22},{7,23},{8,10},{9,11},... | collective-permute-start | bytes 294920 | tf_op jit(solution)/shard_map/ppermute | solution.py:303
  43.5 5.5 %collective-permute-start.9 = (f32[2,96,128]{2,1,0:T(8,128)S(1)}, f32[2,96,128]{2,1,0:T(8,128)S(1)}, u32[]{:S(2)}, u32[]{:S(2)}) collective-permute-start(f32[2,96,128]{2,1,0:T(8,128)S(1)} %get-tuple-element.13), channel_id=1, source_target_pairs={{0,2},{1,3},{2,0},{3,1},{4,6},{5,7},{6,4},{7,5},{8,10},{9,11},{10,... | collective-permute-start | bytes 294920 | tf_op jit(solution)/shard_map/ppermute | solution.py:303
